TPU v7x, 256 devices: a whole 4x4x8 slice. The times are simulated.
256 devices in a mesh: gx: 4 (over x), gy: 8 (over y, core), gz: 8 (over z).
Axes of the slice: x: 4, y: 4, z: 8, core: 2. Of those that a mesh axis runs over, the one named last changes fastest.
Arguments:
- source: float32 [64, 128, 1024], P('gx', 'gy', 'gz'), may hold values from -8 to 8
- conductivity: float32 [64, 128, 1024], P('gx', 'gy', 'gz'), may hold values from 0.25 to 3
Outputs:
- solution: float32 [64, 128, 1024], P('gx', 'gy', 'gz')
- residual: float32 [64, 128, 1024], P('gx', 'gy', 'gz')
All inputs are finite; a program needn't handle non-finite values.
Results may differ from a plain program's by a relative error of at most 0.0003.
Values sent between devices are 32-bit elements; how exact they have to be, the bound alone decides.
No kernel may reach another device: no remote copies, remote signals or barrier semaphores. Data moves between devices by JAX's collectives and lax.ppermute only.
A program may use at most 192 MiB of HBM per device.

v0:
```python
import functools

import jax
import jax.numpy as jnp
import numpy as np
from jax import lax
from jax.experimental import pallas as pl
from jax.experimental.pallas import tpu as pltpu
from jax.sharding import PartitionSpec as P

F32 = jnp.float32
CSWEEPS = 32
BUDGET = 48 * 1024 * 1024


def chebyshev_terms(sweep_count, lower_bound, upper_bound):
    center = (upper_bound + lower_bound) / 2.0
    half_width = (upper_bound - lower_bound) / 2.0
    sigma_ratio = center / half_width
    rho_now = 1.0 / sigma_ratio
    terms = []
    for _ in range(sweep_count - 1):
        rho_next = 1.0 / (2.0 * sigma_ratio - rho_now)
        terms.append((rho_next * rho_now, 2.0 * rho_next / half_width))
        rho_now = rho_next
    return 1.0 / center, terms


FIRST, TERMS = chebyshev_terms(4, 0.6, 2.0)
CFIRST, CTERMS = chebyshev_terms(CSWEEPS, 0.05, 2.0)


def harmonic(a, b):
    return 2.0 * a * b / (a + b)


def roll(a, shift, axis):
    return pltpu.roll(a, shift % a.shape[axis], axis)


def iota(shape, dim):
    return lax.broadcasted_iota(jnp.int32, shape, dim)


def exact_dot(a, m):
    return jnp.dot(a, m, precision=lax.Precision.HIGHEST, preferred_element_type=F32)


def signed(index, size, cut):
    return jnp.where(index < cut, index, index - size)


def loop(lo, hi, unroll, body):
    count = hi - lo
    assert count % unroll == 0

    def step(t, carry):
        for u in range(unroll):
            body(lo + t * unroll + u)
        return carry

    lax.fori_loop(0, count // unroll, step, 0)


class Level:
    def __init__(self, cx, cy, cz, inv, rhs, wrap):
        self.cx, self.cy, self.cz, self.inv, self.rhs, self.wrap = cx, cy, cz, inv, rhs, wrap

    def around(self, i):
        if self.wrap:
            return (i + self.wrap - 1) & (self.wrap - 1), (i + 1) & (self.wrap - 1)
        return i - 1, i + 1

    def defect(self, v, i):
        below, above = self.around(i)
        here = v[i]
        cy, cz = self.cy[i], self.cz[i]
        total = self.cx[i] * v[below] + self.cx[above] * v[above]
        total = total + (cy * roll(here, 1, 0) + roll(cy * here, -1, 0))
        total = total + (cz * roll(here, 1, 1) + roll(cz * here, -1, 1))
        return here, self.rhs[i] - here + self.inv[i] * total


def sweep(level, src, dst, upd, lo, hi, unroll, momentum, push, store_update=True):
    def body(i):
        here, d = level.defect(src, i)
        e = push * d
        if momentum is not None:
            e = momentum * upd[i] + e
        if store_update:
            upd[i] = e
        dst[i] = here + e

    loop(lo, hi, unroll, body)


def z_pack(get, planes, rows, starts, width, per):
    lane = iota((rows, 128), 1)
    out = []
    for start in starts:
        tiles = []
        for g in range(0, planes, per):
            acc = jnp.zeros((rows, 128), F32)
            for p in range(g, min(g + per, planes)):
                plane, base = get(p)
                at = (p - g) * width
                moved = roll(plane, at - start - base, 1)
                acc = jnp.where((lane >= at) & (lane < at + width), moved, acc)
            tiles.append(acc)
        out.append(tiles)
    return out


def pack0(f_ref, b_ref, up_ref, down_ref):
    for ref, start_f, start_b in ((up_ref, 120, 119), (down_ref, 0, 0)):
        (tiles,) = z_pack(lambda p: (f_ref[p], 0), 32, 32, (start_f,), 8, 16)
        for g, t in enumerate(tiles):
            ref[g] = t
        (tiles,) = z_pack(lambda p: (b_ref[p + 1], 0), 32, 32, (start_b,), 9, 14)
        for g, t in enumerate(tiles):
            ref[2 + g] = t


def fine_down(
    f_ref, b_ref, ylo_ref, yhi_ref, zlo_ref, zhi_ref,
    u_ref, cx_ref, cy_ref, cz_ref, inv_ref, rhs_ref, diag_ref, xp_ref,
    bw, ew, va, vb, upd, cxw, dw, scr,
):
    px, py, pz = lax.axis_index("gx"), lax.axis_index("gy"), lax.axis_index("gz")
    lane1 = iota((32, 128), 1)
    lane = iota((32, 256), 1)
    row = iota((32, 256), 0)
    for i in range(34):
        q = min(max(i - 1, 0), 31)
        g, at = q // 14, (q % 14) * 9
        right = roll(zhi_ref[2 + g], -at, 1)
        left = roll(zlo_ref[2 + g], 119 - at, 1)
        bw[i, :, 0:128] = b_ref[i]
        bw[i, :, 128:256] = jnp.where(lane1 < 9, right, jnp.where(lane1 >= 119, left, 1.0))
    for i in range(32):
        g, at = i // 16, (i % 16) * 8
        right = roll(zhi_ref[g], -at, 1)
        left = roll(zlo_ref[g], 120 - at, 1)
        va[i, :, 0:128] = f_ref[i]
        va[i, :, 128:256] = jnp.where(lane1 < 8, right, jnp.where(lane1 >= 120, left, 0.0))
    y_at = (16 * py + signed(row, 32, 24)) & 127
    z_at = (128 * pz + signed(lane, 256, 192)) & 1023
    y_open = jnp.where(y_at == 0, 0.0, 1.0)
    z_open = jnp.where(z_at == 0, 0.0, 1.0)
    y_edge = jnp.where((y_at == 0) | (y_at == 127), 1.0, 0.0)
    z_edge = jnp.where((z_at == 0) | (z_at == 1023), 1.0, 0.0)

    def x_at(i):
        return (16 * px + (i + 56)) & 63

    def face_x(i):
        open_x = jnp.where(x_at(i) == 0, 0.0, 1.0).astype(F32)
        cxw[i] = open_x * harmonic(bw[i + 1], bw[i])

    loop(0, 33, 1, face_x)

    def coefficients(i):
        b = bw[i + 1]
        e_at = jnp.clip(i - 8, 0, 15)
        below = ylo_ref[pl.ds(e_at, 1), :]
        above = yhi_ref[pl.ds(e_at, 1), :]
        below = jnp.concatenate([below, below], axis=1)
        above = jnp.concatenate([above, above], axis=1)
        before = jnp.where(row == 24, jnp.broadcast_to(below, (32, 256)), roll(b, 1, 0))
        cy = y_open * harmonic(b, before)
        outer = harmonic(b[16:24], jnp.broadcast_to(above, (8, 256))) * y_open_next
        after = roll(cy, -1, 0)
        after = jnp.concatenate(
            [after[0:16], jnp.where(row[16:24] == 23, outer, after[16:24]), after[24:32]], axis=0
        )
        cz = z_open * harmonic(b, roll(b, 1, 1))
        own = harmonic(b, b)
        x_edge = jnp.where((x_at(i) == 0) | (x_at(i) == 63), 1.0, 0.0).astype(F32)
        e = own * (y_edge + z_edge + x_edge)
        d = cxw[i] + cxw[i + 1] + (cy + after) + (cz + roll(cz, -1, 1)) + e
        inv = 1.0 / d
        cx_ref[i] = cxw[i]
        cy_ref[i] = cy
        cz_ref[i] = cz
        inv_ref[i] = inv
        ew[i] = e
        dw[i] = d
        g = va[i] * inv
        rhs_ref[i] = g
        first = FIRST * g
        upd[i] = first
        va[i] = first

    y_next = (16 * py + 24) & 127
    y_open_next = jnp.where(y_next == 0, 0.0, 1.0).astype(F32)
    loop(0, 32, 2, coefficients)
    level = Level(cx_ref, cy_ref, cz_ref, inv_ref, rhs_ref, 0)
    sweep(level, va, vb, upd, 1, 31, 2, *TERMS[0])
    sweep(level, vb, va, upd, 2, 30, 2, *TERMS[1])
    sweep(level, va, u_ref, upd, 3, 29, 2, *TERMS[2], store_update=False)

    def save_diag(i):
        diag_ref[i] = dw[i + 8, 0:16, 0:128]

    loop(0, 16, 4, save_diag)

    def put(a, p, value):
        scr[a, 0, p * 32 : p * 32 + 32, :] = value[:, 0:128]
        scr[a, 1, p * 32 : p * 32 + 32, :] = value[:, 128:256]

    for p in range(8):
        i = 8 + 2 * p
        total = None
        for k in (i, i + 1):
            _, d = level.defect(u_ref, k)
            r = dw[k] * d
            total = r if total is None else total + r
        put(0, p, 0.125 * total)
        put(1, p, 0.25 * cx_ref[i])
        put(2, p, 0.25 * (cy_ref[i] + cy_ref[i + 1]))
        put(3, p, 0.25 * (cz_ref[i] + cz_ref[i + 1]))
        put(4, p, 0.25 * (ew[i] + ew[i + 1]))
    fine_lane = iota((256, 128), 0)
    coarse_lane = iota((256, 128), 1)
    both = jnp.where((fine_lane >> 1) == coarse_lane, 1.0, 0.0)
    even = jnp.where(fine_lane == 2 * coarse_lane, 1.0, 0.0)
    half = iota((8, 128), 1) < 64
    for a in range(5):
        def rows_of(offset):
            return jnp.concatenate(
                [scr[a, t, pl.ds(offset, 128, stride=2), :] for t in range(2)], axis=1
            )

        folded = rows_of(0)
        if a != 2:
            folded = folded + rows_of(1)
        res = exact_dot(folded, even if a == 3 else both)
        for j in range(4):
            for t in range(2):
                lo = res[j * 16 + t * 8 : j * 16 + t * 8 + 8]
                hi = res[(j + 4) * 16 + t * 8 : (j + 4) * 16 + t * 8 + 8]
                xp_ref[a, j, t * 8 : t * 8 + 8, :] = jnp.where(half, lo, roll(hi, 64, 1))


def pack1(w_ref, up_ref, down_ref):
    for a in range(5):
        def get(p):
            k, j = p // 8, p % 8
            return w_ref[a, 4 * k + j % 4], 64 * (j // 4)

        ups, downs = z_pack(get, 32, 32, (53, 0), 11, 11)
        for g in range(3):
            up_ref[a, g] = ups[g]
            down_ref[a, g] = downs[g]


def pair_matrices(cut, size_in=128):
    fine = iota((size_in, 128), 0)
    coarse = iota((size_in, 128), 1)
    at = signed(fine, size_in, cut)
    both = jnp.where(((at >> 1) & 127) == coarse, 1.0, 0.0)
    even = jnp.where((((at >> 1) & 127) == coarse) & ((at & 1) == 0), 1.0, 0.0)
    return both, even


def restrict(scr, both, even, count):
    out = []
    for a in range(5):
        folded = scr[a, pl.ds(0, count, stride=2), :]
        if a != 2:
            folded = folded + scr[a, pl.ds(1, count, stride=2), :]
        out.append(exact_dot(folded, even if a == 3 else both))
    return out


def mid_down(
    w_ref, zlo_ref, zhi_ref,
    u_ref, cx_ref, cy_ref, cz_ref, inv_ref, rhs_ref, own_ref, ym_ref, yp_ref,
    va, vb, upd, ew, dw, scr,
):
    lane = iota((32, 128), 1)
    targets = (va, cx_ref, cy_ref, cz_ref, ew)
    for a in range(5):
        fill = 1.0 if a == 4 else 0.0
        for p in range(32):
            k, j = p // 8, p % 8
            base = w_ref[a, 4 * k + j % 4]
            if j >= 4:
                base = roll(base, 64, 1)
            g, at = p // 11, (p % 11) * 11
            right = roll(zhi_ref[a, g], 64 - at, 1)
            left = roll(zlo_ref[a, g], 117 - at, 1)
            halo = jnp.where(lane < 75, right, jnp.where(lane >= 117, left, fill))
            targets[a][p] = jnp.where(lane < 64, base, halo)

    def coefficients(i):
        above = (i + 1) & 31
        cy, cz = cy_ref[i], cz_ref[i]
        d = cx_ref[i] + cx_ref[above] + (cy + roll(cy, -1, 0)) + (cz + roll(cz, -1, 1)) + ew[i]
        inv = 1.0 / d
        inv_ref[i] = inv
        dw[i] = d
        g = 4.0 * va[i] * inv
        rhs_ref[i] = g
        first = FIRST * g
        upd[i] = first
        va[i] = first

    loop(0, 32, 4, coefficients)
    level = Level(cx_ref, cy_ref, cz_ref, inv_ref, rhs_ref, 32)
    sweep(level, va, vb, upd, 0, 32, 4, *TERMS[0])
    sweep(level, vb, va, upd, 0, 32, 4, *TERMS[1])
    sweep(level, va, u_ref, upd, 0, 32, 4, *TERMS[2], store_update=False)
    for p in range(16):
        i = 2 * p
        _, d0 = level.defect(u_ref, i)
        _, d1 = level.defect(u_ref, i + 1)
        at = slice(32 * p, 32 * p + 32)
        scr[0, at, :] = 0.03125 * (dw[i] * d0 + dw[i + 1] * d1)
        scr[1, at, :] = 0.25 * cx_ref[i]
        scr[2, at, :] = 0.25 * (cy_ref[i] + cy_ref[i + 1])
        scr[3, at, :] = 0.25 * (cz_ref[i] + cz_ref[i + 1])
        scr[4, at, :] = 0.25 * (ew[i] + ew[i + 1])
    both, even = pair_matrices(96)
    f, cx, cy, cz, e = [r.reshape(16, 16, 128) for r in restrict(scr, both, even, 256)]
    cx_next = jnp.concatenate([cx[1:], cx[:1]], axis=0)
    planes = []
    for p in range(16):
        d = cx[p] + cx_next[p] + (cy[p] + roll(cy[p], -1, 0)) + (cz[p] + roll(cz[p], -1, 1)) + e[p]
        planes.append((f[p], cx[p], cy[p], cz[p], d))
    lane8 = iota((16, 128), 1)
    for a in range(5):
        for j in range(4):
            packed = planes[j][a]
            for k in range(1, 4):
                packed = jnp.where(lane8 >= 32 * k, roll(planes[4 * k + j][a], 32 * k, 1), packed)
            own_ref[a, j] = packed
            ym_ref[a, j] = roll(packed, 1, 0)[0:8]
            yp_ref[a, j] = roll(packed, 3, 0)[0:8]


def pack2(w_ref, up_ref, down_ref):
    for a in range(5):
        def get(p):
            return w_ref[a, p % 4], 32 * (p // 4)

        ups, downs = z_pack(get, 16, 32, (21, 0), 11, 11)
        for g in range(2):
            up_ref[a, g] = ups[g]
            down_ref[a, g] = downs[g]


def low_down(
    w_ref, zlo_ref, zhi_ref,
    u_ref, cx_ref, cy_ref, cz_ref, inv_ref, rhs_ref, own_ref,
    va, vb, upd, dw, scr,
):
    lane = iota((32, 128), 1)
    targets = (va, cx_ref, cy_ref, cz_ref, dw)
    for a in range(5):
        fill = 1.0 if a == 4 else 0.0
        for p in range(16):
            base = roll(w_ref[a, p % 4], -32 * (p // 4), 1)
            g, at = p // 11, (p % 11) * 11
            right = roll(zhi_ref[a, g], 32 - at, 1)
            left = roll(zlo_ref[a, g], 117 - at, 1)
            halo = jnp.where(lane < 43, right, jnp.where(lane >= 117, left, fill))
            targets[a][p] = jnp.where(lane < 32, base, halo)

    def coefficients(i):
        inv = 1.0 / dw[i]
        inv_ref[i] = inv
        g = 16.0 * va[i] * inv
        rhs_ref[i] = g
        first = FIRST * g
        upd[i] = first
        va[i] = first

    loop(0, 16, 4, coefficients)
    level = Level(cx_ref, cy_ref, cz_ref, inv_ref, rhs_ref, 16)
    sweep(level, va, vb, upd, 0, 16, 4, *TERMS[0])
    sweep(level, vb, va, upd, 0, 16, 4, *TERMS[1])
    sweep(level, va, u_ref, upd, 0, 16, 4, *TERMS[2], store_update=False)

    def edge(i):
        above = (i + 1) & 15
        cy, cz = cy_ref[i], cz_ref[i]
        inner = cx_ref[i] + cx_ref[above] + (cy + roll(cy, -1, 0)) + (cz + roll(cz, -1, 1))
        return dw[i] - inner

    for p in range(8):
        i = 2 * p
        _, d0 = level.defect(u_ref, i)
        _, d1 = level.defect(u_ref, i + 1)
        at = slice(32 * p, 32 * p + 32)
        scr[0, at, :] = 0.0078125 * (dw[i] * d0 + dw[i + 1] * d1)
        scr[1, at, :] = 0.25 * cx_ref[i]
        scr[2, at, :] = 0.25 * (cy_ref[i] + cy_ref[i + 1])
        scr[3, at, :] = 0.25 * (cz_ref[i] + cz_ref[i + 1])
        scr[4, at, :] = 0.25 * (edge(i) + edge(i + 1))
    both, even = pair_matrices(96)
    f, cx, cy, cz, e = [r.reshape(8, 16, 128) for r in restrict(scr, both, even, 128)]
    planes = []
    for p in range(8):
        inner = cx[p] + cx[(p + 1) % 8] + (cy[p] + roll(cy[p], -1, 0))
        d = inner + (cz[p] + roll(cz[p], -1, 1)) + e[p]
        planes.append((f[p], cx[p], cy[p], cz[p], d))
    lane16 = iota((16, 128), 1)
    for a in range(5):
        packed = planes[0][a]
        for p in range(1, 8):
            packed = jnp.where(lane16 >= 16 * p, roll(planes[p][a], 16 * p, 1), packed)
        own_ref[a] = roll(packed, 3, 0)[0:8]


def spread(dup, w, rows, matrix):
    count = w.shape[0]
    dup[pl.ds(0, count, stride=2), :] = w
    dup[pl.ds(1, count, stride=2), :] = w
    return exact_dot(dup[0 : 2 * count, :], matrix)


def spread_matrix(cut, size):
    coarse = iota((128, size), 0)
    at = signed(iota((128, size), 1), size, cut)
    return jnp.where(((at >> 1) & 127) == coarse, 1.0, 0.0)


def post(level, va, vb, upd, ranges, unroll):
    lo, hi = ranges[0]
    sweep(level, va, vb, upd, lo, hi, unroll, None, FIRST)
    src, dst = vb, va
    for n in range(3):
        lo, hi = ranges[n + 1]
        sweep(level, src, dst, upd, lo, hi, unroll, *TERMS[n], store_update=n < 2)
        src, dst = dst, src


def up(
    g_ref,
    u2, cx2, cy2, cz2, inv2, rhs2,
    u1, cx1, cy1, cz1, inv1, rhs1,
    u0, cx0, cy0, cz0, inv0, rhs0, diag0,
    sol_ref, res_ref,
    l3, inv3, rhs3, u3, va3, vb3, upd3, scr3,
    va2, vb2, upd2, dup2, va1, vb1, upd1, dup1, va0, vb0, upd0, dup0,
):
    me = lax.axis_index("gz")
    lane = iota((16, 128), 1)
    for a in range(5):
        tiles = [roll(g_ref[(me + k) & 7, a], -3, 0) for k in range(8)]
        for p in range(8):
            plane = roll(tiles[0], -16 * p, 1)
            for k in range(1, 8):
                plane = jnp.where(lane >= 16 * k, roll(tiles[k], 16 * (k - p), 1), plane)
            l3[a, p] = plane
    f3, cx3, cy3, cz3, d3 = [l3.at[a] for a in range(5)]
    level = Level(cx3, cy3, cz3, inv3, rhs3, 8)

    def start3(i):
        inv = 1.0 / d3[i]
        inv3[i] = inv
        g = 64.0 * f3[i] * inv
        rhs3[i] = g
        first = FIRST * g
        upd3[i] = first
        va3[i] = first

    loop(0, 8, 8, start3)
    sweep(level, va3, vb3, upd3, 0, 8, 8, *TERMS[0])
    sweep(level, vb3, va3, upd3, 0, 8, 8, *TERMS[1])
    sweep(level, va3, u3, upd3, 0, 8, 8, *TERMS[2], store_update=False)
    for p in range(4):
        i = 2 * p
        _, r0 = level.defect(u3, i)
        _, r1 = level.defect(u3, i + 1)
        at = slice(16 * p, 16 * p + 16)
        scr3[0, at, :] = (0.125 / 64.0) * (d3[i] * r0 + d3[i + 1] * r1)
        scr3[1, at, :] = 0.25 * cx3[i]
        scr3[2, at, :] = 0.25 * (cy3[i] + cy3[i + 1])
        scr3[3, at, :] = 0.25 * (cz3[i] + cz3[i + 1])
        total = None
        for k in (i, i + 1):
            cy, cz = cy3[k], cz3[k]
            inner = cx3[k] + cx3[(k + 1) % 8] + (cy + roll(cy, -1, 0))
            inner = inner + (cz + roll(cz, -1, 1))
            total = d3[k] - inner if total is None else total + (d3[k] - inner)
        scr3[4, at, :] = 0.25 * total
    fine = iota((128, 128), 0)
    coarse = iota((128, 128), 1) & 63
    both = jnp.where((fine >> 1) == coarse, 1.0, 0.0)
    even = jnp.where(fine == 2 * coarse, 1.0, 0.0)
    f, cx, cy, cz, e = restrict(scr3, both, even, 32)

    def cut(a, p):
        return a[8 * p : 8 * p + 8]

    fs, cxs, cys, czs = [[cut(a, p) for p in range(4)] for a in (f, cx, cy, cz)]
    invs, gs, vs, es = [], [], [], []
    for p in range(4):
        d = cxs[p] + cxs[(p + 1) % 4] + (cys[p] + roll(cys[p], -1, 0))
        d = d + (czs[p] + roll(czs[p], -1, 1)) + cut(e, p)
        invs.append(1.0 / d)
        gs.append(256.0 * fs[p] * invs[p])
        es.append(CFIRST * gs[p])
        vs.append(es[p])
    xlo = [invs[p] * cxs[p] for p in range(4)]
    xhi = [invs[p] * cxs[(p + 1) % 4] for p in range(4)]
    ylo = [invs[p] * cys[p] for p in range(4)]
    yhi = [invs[p] * roll(cys[p], -1, 0) for p in range(4)]
    zlo = [invs[p] * czs[p] for p in range(4)]
    zhi = [invs[p] * roll(czs[p], -1, 1) for p in range(4)]
    for momentum, push in CTERMS:
        momentum, push = float(np.float32(momentum)), float(np.float32(push))
        new_v, new_e = [], []
        for p in range(4):
            v = vs[p]
            total = xlo[p] * vs[(p + 3) % 4] + xhi[p] * vs[(p + 1) % 4]
            total = total + (ylo[p] * roll(v, 1, 0) + yhi[p] * roll(v, -1, 0))
            total = total + (zlo[p] * roll(v, 1, 1) + zhi[p] * roll(v, -1, 1))
            ne = momentum * es[p] + push * ((gs[p] - v) + total)
            new_e.append(ne)
            new_v.append(v + ne)
        vs, es = new_v, new_e
    w4 = jnp.concatenate(vs, axis=0)
    fine = iota((128, 128), 1)
    coarse = iota((128, 128), 0)
    m = jnp.where((fine >> 1) == coarse, 1.0, 0.0)
    wide = spread(dup2, w4, 8, m)
    for i in range(8):
        p = i // 2
        va3[i] = u3[i] + wide[16 * p : 16 * p + 16]
    post(level, va3, vb3, upd3, [(0, 8)] * 4, 8)
    w3 = va3[...].reshape(128, 128)
    wide = spread(dup2, w3, 16, spread_matrix(96, 128))
    for i in range(16):
        p = i // 2
        va2[i] = u2[i] + wide[32 * p : 32 * p + 32]
    level = Level(cx2, cy2, cz2, inv2, rhs2, 16)
    post(level, va2, vb2, upd2, [(0, 16)] * 4, 4)
    w2 = jnp.concatenate([va2[:, 0:8, :], va2[:, 24:32, :]], axis=1).reshape(256, 128)
    wide = spread(dup1, w2, 16, spread_matrix(96, 128))
    for i in range(32):
        p = i // 2
        va1[i] = u1[i] + wide[32 * p : 32 * p + 32]
    level = Level(cx1, cy1, cz1, inv1, rhs1, 32)
    post(level, va1, vb1, upd1, [(0, 32)] * 4, 4)
    rows = [
        jnp.concatenate([va1[i % 32, 0:8, :], mix_rows(va1, i % 32)], axis=0) for i in range(-4, 12)
    ]
    w1 = jnp.concatenate(rows, axis=0)
    wide = spread(dup0, w1, 16, spread_matrix(192, 256))
    for i in range(3, 29):
        p = i // 2
        va0[i] = u0[i] + wide[32 * p : 32 * p + 32]
    level = Level(cx0, cy0, cz0, inv0, rhs0, 0)
    post(level, va0, vb0, upd0, [(4, 28), (5, 27), (6, 26), (7, 25)], 2)

    def finish(i):
        here, d = level.defect(va0, i)
        sol_ref[i - 8] = here[0:16, 0:128]
        res_ref[i - 8] = diag0[i - 8] * d[0:16, 0:128]

    loop(8, 24, 2, finish)


def mix_rows(ref, i):
    low = iota((8, 128), 0) < 4
    return jnp.where(low, ref[i, 8:16, :], ref[i, 24:32, :])


def call(body, args, outs, scratch=()):
    return pl.pallas_call(
        body,
        out_shape=[jax.ShapeDtypeStruct(s, F32) for s in outs],
        scratch_shapes=[pltpu.VMEM(s, F32) for s in scratch],
        compiler_params=pltpu.CompilerParams(vmem_limit_bytes=BUDGET),
        name=body.__name__,
    )(*args)


def move(values, axis, shift):
    size = lax.axis_size(axis)
    return lax.ppermute(values, axis, [((i + shift) % size, i) for i in range(size)])


def local(source, conductivity):
    f, b = source, conductivity
    from_lo = move(jnp.concatenate([f[8:16], b[7:16]]), "gx", -1)
    from_hi = move(jnp.concatenate([f[0:8], b[0:9]]), "gx", 1)
    fx = jnp.concatenate([from_lo[:8], f, from_hi[:8]])
    bx = jnp.concatenate([from_lo[8:], b, from_hi[8:]])

    def y_slab(at, edge):
        return jnp.concatenate(
            [fx[:, at : at + 8], bx[1:33, at : at + 8], bx[9:25, edge].reshape(2, 8, 128)]
        )

    from_lo = move(y_slab(8, 7), "gy", -1)
    from_hi = move(y_slab(0, 8), "gy", 1)
    fw = jnp.concatenate([fx, from_hi[:32], from_lo[:32]], axis=1)
    inner = jnp.concatenate([bx[1:33], from_hi[32:64], from_lo[32:64]], axis=1)
    first = jnp.concatenate([bx[:1], bx[:1]], axis=1)
    last = jnp.concatenate([bx[33:], bx[33:]], axis=1)
    bw = jnp.concatenate([first, inner, last])
    ylo, yhi = from_lo[64:].reshape(16, 128), from_hi[64:].reshape(16, 128)
    up0, down0 = call(pack0, (fw, bw), [(5, 32, 128)] * 2)
    zlo, zhi = move(up0, "gz", -1), move(down0, "gz", 1)
    big = (32, 32, 256)
    u0, cx0, cy0, cz0, inv0, rhs0, diag0, xp = call(
        fine_down,
        (fw, bw, ylo, yhi, zlo, zhi),
        [big] * 6 + [(16, 16, 128), (5, 4, 16, 128)],
        [(34, 32, 256), big, big, big, big, (33, 32, 256), big, (5, 2, 256, 128)],
    )
    x_all = jnp.concatenate([xp] + [move(xp, "gx", k) for k in (1, 2, 3)], axis=1)
    own, halo = x_all[:, :, 0:8], x_all[:, :, 8:16]

    def with_rows(at):
        part = halo[:, :, at : at + 4]
        return jnp.concatenate(
            [own, jnp.concatenate([part[:, :8], part[:, 8:]], axis=2)], axis=1
        )

    from_hi = move(with_rows(0), "gy", 1)
    from_lo = move(with_rows(4), "gy", -1)

    def unfold(got):
        part = got[:, 16:]
        return jnp.concatenate([part[:, :, 0:4], part[:, :, 4:8]], axis=1)

    w1 = jnp.concatenate(
        [own, from_hi[:, :16], unfold(from_hi), unfold(from_lo), from_lo[:, :16]], axis=2
    )
    up1, down1 = call(pack1, (w1,), [(5, 3, 32, 128)] * 2)
    zlo, zhi = move(up1, "gz", -1), move(down1, "gz", 1)
    mid = (32, 32, 128)
    u1, cx1, cy1, cz1, inv1, rhs1, own2, ym, yp = call(
        mid_down,
        (w1, zlo, zhi),
        [mid] * 6 + [(5, 4, 16, 128), (5, 4, 8, 128), (5, 4, 8, 128)],
        [mid] * 5 + [(5, 512, 128)],
    )
    from_hi, from_lo = move(ym, "gy", 2), move(yp, "gy", -2)
    w2 = jnp.concatenate(
        [own2[:, :, 0:7], from_hi, own2[:, :, 7:13], from_lo, own2[:, :, 13:16]], axis=2
    )
    up2, down2 = call(pack2, (w2,), [(5, 2, 32, 128)] * 2)
    zlo, zhi = move(up2, "gz", -1), move(down2, "gz", 1)
    low = (16, 32, 128)
    u2, cx2, cy2, cz2, inv2, rhs2, own3 = call(
        low_down,
        (w2, zlo, zhi),
        [low] * 6 + [(5, 8, 128)],
        [low] * 4 + [(5, 256, 128)],
    )
    both = jnp.concatenate([own3, move(own3, "gy", 4)], axis=1)
    everyone = jnp.broadcast_to(both[None], (8, 5, 16, 128))
    gathered = lax.all_to_all(everyone, "gz", 0, 0)
    tiny = (8, 16, 128)
    return tuple(
        call(
            up,
            (
                gathered,
                u2, cx2, cy2, cz2, inv2, rhs2,
                u1, cx1, cy1, cz1, inv1, rhs1,
                u0, cx0, cy0, cz0, inv0, rhs0, diag0,
            ),
            [(16, 16, 128)] * 2,
            [(5,) + tiny] + [tiny] * 6 + [(5, 64, 128)]
            + [low] * 3 + [(256, 128)] + [mid] * 3 + [(512, 128)] + [big] * 3 + [(512, 128)],
        )
    )


def solution(mesh):
    spec = P("gx", "gy", "gz")
    return jax.shard_map(
        local, mesh=mesh, in_specs=(spec, spec), out_specs=(spec, spec), check_vma=False
    )
```

profile of v0, /device:TPU:32, one launch (start us, length us, event | category | flops | bytes accessed | tf_op | source)
XLA Modules:
  0.0 148.7 jit_solution(18005998776427805805)
XLA Ops:
  0.6 0.0 copy-start.13
  0.7 0.9 fusion.9
  1.6 1.0 fusion.10
  2.6 2.8 %collective-permute-start.1 = (f32[17,16,128]{2,1,0:T(8,128)S(1)}, f32[17,16,128]{2,1,0:T(8,128)S(1)}, u32[]{:S(2)}, u32[]{:S(2)}) collective-permute-start(f32[17,16,128]{2,1,0:T(8,128)S(1)} %pad_maximum_fusion.13), channel_id=1, source_target_pairs={{64,0},{128,64},{192,128},{0,192},{65,1},{129,65},{193,129},{1,193... | collective-permute-start | bytes 417800 | tf_op jit(solution)/shard_map/ppermute | solution.py:584
  5.4 0.1 collective-permute-start
  5.5 0.9 fusion.8
  6.4 1.9 %collective-permute-done.1 = f32[17,16,128]{2,1,0:T(8,128)S(1)} collective-permute-done((f32[17,16,128]{2,1,0:T(8,128)S(1)}, f32[17,16,128]{2,1,0:T(8,128)S(1)}, u32[]{:S(2)}, u32[]{:S(2)}) %collective-permute-start.1) | collective-permute-done | bytes 139296 | tf_op jit(solution)/shard_map/ppermute | solution.py:584
  8.4 3.5 %collective-permute-done = f32[17,16,128]{2,1,0:T(8,128)S(1)} collective-permute-done((f32[17,16,128]{2,1,0:T(8,128)S(1)}, f32[17,16,128]{2,1,0:T(8,128)S(1)}, u32[]{:S(2)}, u32[]{:S(2)}) %collective-permute-start) | collective-permute-done | bytes 139296 | tf_op jit(solution)/shard_map/ppermute | solution.py:584
  12.0 0.1 fusion.4
  12.1 0.0 collective-permute-start.3
  12.1 2.9 %collective-permute-start.2 = (f32[66,8,128]{2,1,0:T(8,128)S(1)}, f32[66,8,128]{2,1,0:T(8,128)S(1)}, u32[]{:S(2)}, u32[]{:S(2)}) collective-permute-start(f32[66,8,128]{2,1,0:T(8,128)S(1)} %pad_maximum_fusion.7), channel_id=1, source_target_pairs={{8,0},{16,8},{24,16},{32,24},{40,32},{48,40},{56,48},{0,56},{9,1},... | collective-permute-start | bytes 811016 | tf_op jit(solution)/shard_map/ppermute | solution.py:584
  15.1 0.0 slice-start.1
  15.1 0.0 slice-start.2
  15.1 4.1 %collective-permute-done.3 = f32[66,8,128]{2,1,0:T(8,128)S(1)} collective-permute-done((f32[66,8,128]{2,1,0:T(8,128)S(1)}, f32[66,8,128]{2,1,0:T(8,128)S(1)}, u32[]{:S(2)}, u32[]{:S(2)}) %collective-permute-start.3) | collective-permute-done | bytes 270368 | tf_op jit(solution)/shard_map/ppermute | solution.py:584
  19.2 0.0 collective-permute-done.2
  19.4 0.6 pack0.1
  19.9 2.0 %collective-permute-start.4 = (f32[5,32,128]{2,1,0:T(8,128)S(1)}, f32[5,32,128]{2,1,0:T(8,128)S(1)}, u32[]{:S(2)}, u32[]{:S(2)}) collective-permute-start(f32[5,32,128]{2,1,0:T(8,128)S(1)} %get-tuple-element.32), channel_id=1, source_target_pairs={{7,0},{0,1},{1,2},{2,3},{3,4},{4,5},{5,6},{6,7},{15,8},{8,9},{9,10... | collective-permute-start | bytes 245768 | tf_op jit(solution)/shard_map/ppermute | solution.py:584
  21.9 0.1 collective-permute-start.5
  22.1 2.8 %collective-permute-done.4.zlo_ref = f32[5,32,128]{2,1,0:T(8,128)S(1)} collective-permute-done((f32[5,32,128]{2,1,0:T(8,128)S(1)}, f32[5,32,128]{2,1,0:T(8,128)S(1)}, u32[]{:S(2)}, u32[]{:S(2)}) %collective-permute-start.4) | collective-permute-done | bytes 81952 | tf_op jit(solution)/shard_map/ppermute | solution.py:584
  24.8 1.8 %collective-permute-done.5.zhi_ref = f32[5,32,128]{2,1,0:T(8,128)S(1)} collective-permute-done((f32[5,32,128]{2,1,0:T(8,128)S(1)}, f32[5,32,128]{2,1,0:T(8,128)S(1)}, u32[]{:S(2)}, u32[]{:S(2)}) %collective-permute-start.5) | collective-permute-done | bytes 81952 | tf_op jit(solution)/shard_map/ppermute | solution.py:584
  26.7 10.4 %fine_down.1 = (f32[32,32,256]{2,1,0:T(8,128)S(1)}, f32[32,32,256]{2,1,0:T(8,128)S(1)}, f32[32,32,256]{2,1,0:T(8,128)S(1)}, f32[32,32,256]{2,1,0:T(8,128)S(1)}, ...) custom-call(f32[32,32,128]{2,1,0:T(8,128)S(1)} %pad_maximum_fusion.2, ...), custom_call_target="tpu_custom_call" | custom-call | tf_op jit(solution)/shard_map/fine_down/pallas_call | solution.py:573
  37.0 1.0 copy-done.2
  38.0 0.2 collective-permute-start.6
  38.3 1.8 %collective-permute-start.8 = (f32[5,4,16,128]{3,2,1,0:T(8,128)S(1)}, f32[5,4,16,128]{3,2,1,0:T(8,128)S(1)}, u32[]{:S(2)}, u32[]{:S(2)}) collective-permute-start(f32[5,4,16,128]{3,2,1,0:T(8,128)S(1)} %get-tuple-element.34), channel_id=1, source_target_pairs={{192,0},{0,64},{64,128},{128,192},{193,1},{1,65},{65,129},{129,193... | collective-permute-start | bytes 491528 | tf_op jit(solution)/shard_map/ppermute | solution.py:584
  40.1 0.0 collective-permute-start.7
  40.1 5.1 %collective-permute-done.6 = f32[5,4,16,128]{3,2,1,0:T(8,128)S(1)} collective-permute-done((f32[5,4,16,128]{3,2,1,0:T(8,128)S(1)}, f32[5,4,16,128]{3,2,1,0:T(8,128)S(1)}, u32[]{:S(2)}, u32[]{:S(2)}) %collective-permute-start.6) | collective-permute-done | bytes 163872 | tf_op jit(solution)/shard_map/ppermute | solution.py:584
  45.2 1.8 %collective-permute-done.7 = f32[5,4,16,128]{3,2,1,0:T(8,128)S(1)} collective-permute-done((f32[5,4,16,128]{3,2,1,0:T(8,128)S(1)}, f32[5,4,16,128]{3,2,1,0:T(8,128)S(1)}, u32[]{:S(2)}, u32[]{:S(2)}) %collective-permute-start.7) | collective-permute-done | bytes 163872 | tf_op jit(solution)/shard_map/ppermute | solution.py:584
  47.0 1.4 collective-permute-done.8
  48.5 0.1 pad_maximum_fusion
  48.7 0.0 collective-permute-start.10
  48.7 2.9 %collective-permute-start.9 = (f32[5,24,8,128]{3,2,1,0:T(8,128)S(1)}, f32[5,24,8,128]{3,2,1,0:T(8,128)S(1)}, u32[]{:S(2)}, u32[]{:S(2)}) collective-permute-start(f32[5,24,8,128]{3,2,1,0:T(8,128)S(1)} %get-tuple-element.67), channel_id=1, source_target_pairs={{8,0},{16,8},{24,16},{32,24},{40,32},{48,40},{56,48},{0,56},{9,1},... | collective-permute-start | bytes 1474568 | tf_op jit(solution)/shard_map/ppermute | solution.py:584
  51.6 6.5 %collective-permute-done.10 = f32[5,24,8,128]{3,2,1,0:T(8,128)S(1)} collective-permute-done((f32[5,24,8,128]{3,2,1,0:T(8,128)S(1)}, f32[5,24,8,128]{3,2,1,0:T(8,128)S(1)}, u32[]{:S(2)}, u32[]{:S(2)}) %collective-permute-start.10) | collective-permute-done | bytes 491552 | tf_op jit(solution)/shard_map/ppermute | solution.py:584
  58.2 0.7 pad_maximum_fusion.11
  58.9 0.0 collective-permute-done.9
  58.9 0.7 pad_maximum_fusion.10
  59.7 2.9 %concatenate.91.w_ref = f32[5,16,32,128]{3,2,1,0:T(8,128)S(1)} concatenate(f32[5,16,8,128]{3,2,1,0:T(8,128)S(1)} %pad_maximum_fusion.3, f32[5,16,8,128]{3,2,1,0:T(8,128)S(1)} %slice.190, f32[5,16,4,128]{3,2,1,0:T(4,128)} %pad_maximum_fusion.10, f32[5,16,4,128]{3,2,1,0:T(4,128)} %pad_maximum_fusion.11, f32[5,16,8,128]{3,2,1,0:T(8,128)S(1)} %slice.197), dimensions={2} | concatenate | bytes 2621440 | tf_op jit(solution)/shard_map/concatenate | solution.py:632
  62.5 1.4 pack1.1
  63.9 3.3 %collective-permute-start.11 = (f32[5,3,32,128]{3,2,1,0:T(8,128)S(1)}, f32[5,3,32,128]{3,2,1,0:T(8,128)S(1)}, u32[]{:S(2)}, u32[]{:S(2)}) collective-permute-start(f32[5,3,32,128]{3,2,1,0:T(8,128)S(1)} %get-tuple-element.35), channel_id=1, source_target_pairs={{7,0},{0,1},{1,2},{2,3},{3,4},{4,5},{5,6},{6,7},{15,8},{8,9},{9,10... | collective-permute-start | bytes 737288 | tf_op jit(solution)/shard_map/ppermute | solution.py:584
  67.2 0.0 collective-permute-start.12
  67.2 4.8 %collective-permute-done.11.zlo_ref = f32[5,3,32,128]{3,2,1,0:T(8,128)S(1)} collective-permute-done((f32[5,3,32,128]{3,2,1,0:T(8,128)S(1)}, f32[5,3,32,128]{3,2,1,0:T(8,128)S(1)}, u32[]{:S(2)}, u32[]{:S(2)}) %collective-permute-start.11) | collective-permute-done | bytes 245792 | tf_op jit(solution)/shard_map/ppermute | solution.py:584
  72.0 3.5 %collective-permute-done.12.zhi_ref = f32[5,3,32,128]{3,2,1,0:T(8,128)S(1)} collective-permute-done((f32[5,3,32,128]{3,2,1,0:T(8,128)S(1)}, f32[5,3,32,128]{3,2,1,0:T(8,128)S(1)}, u32[]{:S(2)}, u32[]{:S(2)}) %collective-permute-start.12) | collective-permute-done | bytes 245792 | tf_op jit(solution)/shard_map/ppermute | solution.py:584
  75.5 6.5 %mid_down.1 = (f32[32,32,128]{2,1,0:T(8,128)S(1)}, f32[32,32,128]{2,1,0:T(8,128)S(1)}, f32[32,32,128]{2,1,0:T(8,128)S(1)}, f32[32,32,128]{2,1,0:T(8,128)S(1)}, f...) custom-call(f32[5,16,32,128]{3,2,1,0:T(8,128)S(1)} %concatenate.91.w, ...), custom_call_target="tpu_custom_call" | custom-call | tf_op jit(solution)/shard_map/mid_down/pallas_call | solution.py:573
  81.9 0.8 copy-done.3
  82.7 0.8 copy-done.5
  83.6 0.8 copy-done.7
  84.3 0.8 copy-done.9
  85.1 2.9 %collective-permute-start.13 = (f32[5,4,8,128]{3,2,1,0:T(8,128)S(1)}, f32[5,4,8,128]{3,2,1,0:T(8,128)S(1)}, u32[]{:S(2)}, u32[]{:S(2)}) collective-permute-start(f32[5,4,8,128]{3,2,1,0:T(8,128)S(1)} %get-tuple-element.38), channel_id=1, source_target_pairs={{16,0},{24,8},{32,16},{40,24},{48,32},{56,40},{0,48},{8,56},{17,1}... | collective-permute-start | bytes 245768 | tf_op jit(solution)/shard_map/ppermute | solution.py:584
  88.1 0.0 collective-permute-start.14
  88.1 2.0 %collective-permute-done.13 = f32[5,4,8,128]{3,2,1,0:T(8,128)S(1)} collective-permute-done((f32[5,4,8,128]{3,2,1,0:T(8,128)S(1)}, f32[5,4,8,128]{3,2,1,0:T(8,128)S(1)}, u32[]{:S(2)}, u32[]{:S(2)}) %collective-permute-start.13) | collective-permute-done | bytes 81952 | tf_op jit(solution)/shard_map/ppermute | solution.py:584
  90.1 3.6 %collective-permute-done.14 = f32[5,4,8,128]{3,2,1,0:T(8,128)S(1)} collective-permute-done((f32[5,4,8,128]{3,2,1,0:T(8,128)S(1)}, f32[5,4,8,128]{3,2,1,0:T(8,128)S(1)}, u32[]{:S(2)}, u32[]{:S(2)}) %collective-permute-start.14) | collective-permute-done | bytes 81952 | tf_op jit(solution)/shard_map/ppermute | solution.py:584
  93.7 0.5 concatenate.92.w_ref
  94.2 0.7 pack2.1
  94.9 1.8 %collective-permute-start.15 = (f32[5,2,32,128]{3,2,1,0:T(8,128)S(1)}, f32[5,2,32,128]{3,2,1,0:T(8,128)S(1)}, u32[]{:S(2)}, u32[]{:S(2)}) collective-permute-start(f32[5,2,32,128]{3,2,1,0:T(8,128)S(1)} %get-tuple-element.40), channel_id=1, source_target_pairs={{7,0},{0,1},{1,2},{2,3},{3,4},{4,5},{5,6},{6,7},{15,8},{8,9},{9,10... | collective-permute-start | bytes 491528 | tf_op jit(solution)/shard_map/ppermute | solution.py:584
  96.7 0.3 collective-permute-start.16
  97.0 3.3 %collective-permute-done.15.zlo_ref = f32[5,2,32,128]{3,2,1,0:T(8,128)S(1)} collective-permute-done((f32[5,2,32,128]{3,2,1,0:T(8,128)S(1)}, f32[5,2,32,128]{3,2,1,0:T(8,128)S(1)}, u32[]{:S(2)}, u32[]{:S(2)}) %collective-permute-start.15) | collective-permute-done | bytes 163872 | tf_op jit(solution)/shard_map/ppermute | solution.py:584
  100.3 1.7 %collective-permute-done.16.zhi_ref = f32[5,2,32,128]{3,2,1,0:T(8,128)S(1)} collective-permute-done((f32[5,2,32,128]{3,2,1,0:T(8,128)S(1)}, f32[5,2,32,128]{3,2,1,0:T(8,128)S(1)}, u32[]{:S(2)}, u32[]{:S(2)}) %collective-permute-start.16) | collective-permute-done | bytes 163872 | tf_op jit(solution)/shard_map/ppermute | solution.py:584
  102.1 3.4 %low_down.1 = (f32[16,32,128]{2,1,0:T(8,128)S(1)}, f32[16,32,128]{2,1,0:T(8,128)S(1)}, f32[16,32,128]{2,1,0:T(8,128)S(1)}, f32[16,32,128]{2,1,0:T(8,128)S(1)}, f...) custom-call(f32[5,4,32,128]{3,2,1,0:T(8,128)S(1)} %concatenate.92.w_ref, ...), custom_call_target="tpu_custom_call" | custom-call | tf_op jit(solution)/shard_map/low_down/pallas_call | solution.py:573
  105.5 0.1 collective-permute-start.17
  105.6 5.3 %collective-permute-done.17 = f32[5,8,128]{2,1,0:T(8,128)S(1)} collective-permute-done((f32[5,8,128]{2,1,0:T(8,128)S(1)}, f32[5,8,128]{2,1,0:T(8,128)S(1)}, u32[]{:S(2)}, u32[]{:S(2)}) %collective-permute-start.17) | collective-permute-done | bytes 20512 | tf_op jit(solution)/shard_map/ppermute | solution.py:584
  110.9 14.7 %all_to_all.5.g_ref = f32[8,5,16,128]{3,2,1,0:T(8,128)S(1)} all-to-all(f32[8,5,16,128]{3,2,1,0:T(8,128)S(1)} %broadcast_in_dim.2), channel_id=1, replica_groups=mesh['gx'=4,'gy'=8,'gz'=8] {'gz'}, dimensions={0} | all-to-all | bytes 655360 | tf_op jit(solution)/shard_map/all_to_all | solution.py:659
  125.5 1.0 copy-done.6
  126.6 1.0 copy-done.8
  127.6 1.0 copy-done.10
  128.7 20.0 %up.1 = (f32[16,16,128]{2,1,0:T(8,128)}, f32[16,16,128]{2,1,0:T(8,128)}) custom-call(f32[8,5,16,128]{3,2,1,0:T(8,128)S(1)} %all_to_all.5.g_ref, f32[16,32,128]{2,1,0:T(8,128)S(1)} %get-tuple-element.43.u2, f32[16,32,128]{2,1,0:T(8,128)S(1)} %get-tuple-element.44.cx2, f32[16,32,128]{2,1,0:T(8,128)S(1)} %get-tuple-element.45.cy2, ...), custom_call_target="tpu_custom_call" | custom-call | tf_op jit(solution)/shard_map/up/pallas_call | solution.py:573
  (59 shorter events, 0.6 us)
Async XLA Ops:
  0.6 11.3 %copy-start.12 = (f32[16,16,128]{2,1,0:T(8,128)S(1)}, f32[16,16,128]{2,1,0:T(8,128)}, u32[]{:S(2)}) copy-start(f32[16,16,128]{2,1,0:T(8,128)} %param.2) | copy-start | bytes 393220
  0.6 11.2 %copy-start.13 = (f32[16,16,128]{2,1,0:T(8,128)S(1)}, f32[16,16,128]{2,1,0:T(8,128)}, u32[]{:S(2)}) copy-start(f32[16,16,128]{2,1,0:T(8,128)} %param.3) | copy-start | bytes 393220
  2.6 5.8 %collective-permute-start.1 = (f32[17,16,128]{2,1,0:T(8,128)S(1)}, f32[17,16,128]{2,1,0:T(8,128)S(1)}, u32[]{:S(2)}, u32[]{:S(2)}) collective-permute-start(f32[17,16,128]{2,1,0:T(8,128)S(1)} %pad_maximum_fusion.13), channel_id=1, source_target_pairs={{64,0},{128,64},{192,128},{0,192},{65,1},{129,65},{193,129},{1,193... | collective-permute-start | bytes 417800 | tf_op jit(solution)/shard_map/ppermute | solution.py:584
  5.4 6.4 %collective-permute-start = (f32[17,16,128]{2,1,0:T(8,128)S(1)}, f32[17,16,128]{2,1,0:T(8,128)S(1)}, u32[]{:S(2)}, u32[]{:S(2)}) collective-permute-start(f32[17,16,128]{2,1,0:T(8,128)S(1)} %pad_maximum_fusion.12), channel_id=1, source_target_pairs={{192,0},{0,64},{64,128},{128,192},{193,1},{1,65},{65,129},{129,193... | collective-permute-start | bytes 417800 | tf_op jit(solution)/shard_map/ppermute | solution.py:584
  8.4 6.7 %copy-start.14 = (f32[17,16,128]{2,1,0:T(8,128)}, f32[17,16,128]{2,1,0:T(8,128)S(1)}, u32[]{:S(2)}) copy-start(f32[17,16,128]{2,1,0:T(8,128)S(1)} %collective-permute-done.1) | copy-start | bytes 417796
  11.9 3.2 %copy-start.15 = (f32[17,16,128]{2,1,0:T(8,128)}, f32[17,16,128]{2,1,0:T(8,128)S(1)}, u32[]{:S(2)}) copy-start(f32[17,16,128]{2,1,0:T(8,128)S(1)} %collective-permute-done) | copy-start | bytes 417796
  11.9 3.2 %copy-start.11 = (f32[34,16,128]{2,1,0:T(8,128)}, f32[34,16,128]{2,1,0:T(8,128)S(1)}, u32[]{:S(2)}) copy-start(f32[34,16,128]{2,1,0:T(8,128)S(1)} %pad_maximum_fusion.6) | copy-start | bytes 835588
  12.1 7.1 %collective-permute-start.3 = (f32[66,8,128]{2,1,0:T(8,128)S(1)}, f32[66,8,128]{2,1,0:T(8,128)S(1)}, u32[]{:S(2)}, u32[]{:S(2)}) collective-permute-start(f32[66,8,128]{2,1,0:T(8,128)S(1)} %pad_maximum_fusion.8), channel_id=1, source_target_pairs={{56,0},{0,8},{8,16},{16,24},{24,32},{32,40},{40,48},{48,56},{57,1}... | collective-permute-start | bytes 811016 | tf_op jit(solution)/shard_map/ppermute | solution.py:584
  12.1 7.1 %collective-permute-start.2 = (f32[66,8,128]{2,1,0:T(8,128)S(1)}, f32[66,8,128]{2,1,0:T(8,128)S(1)}, u32[]{:S(2)}, u32[]{:S(2)}) collective-permute-start(f32[66,8,128]{2,1,0:T(8,128)S(1)} %pad_maximum_fusion.7), channel_id=1, source_target_pairs={{8,0},{16,8},{24,16},{32,24},{40,32},{48,40},{56,48},{0,56},{9,1},... | collective-permute-start | bytes 811016 | tf_op jit(solution)/shard_map/ppermute | solution.py:584
  15.1 4.2 %slice-start = ((f32[34,16,128]{2,1,0:T(8,128)}), f32[32,16,128]{2,1,0:T(8,128)S(1)}, s32[]{:S(2)}) async-start(f32[34,16,128]{2,1,0:T(8,128)} %copy-done.11), calls=%async_computation.1 | async-start | bytes 524288 | tf_op jit(solution)/shard_map/slice | solution.py:602
  15.1 4.2 %slice-start.1 = ((f32[17,16,128]{2,1,0:T(8,128)}), f32[1,16,128]{2,1,0:T(8,128)S(1)}, s32[]{:S(2)}) async-start(f32[17,16,128]{2,1,0:T(8,128)} %copy-done.14), calls=%async_computation.2 | async-start | bytes 16384 | tf_op jit(solution)/shard_map/slice | solution.py:604
  15.1 4.2 %slice-start.2 = ((f32[17,16,128]{2,1,0:T(8,128)}), f32[1,16,128]{2,1,0:T(8,128)S(1)}, s32[]{:S(2)}) async-start(f32[17,16,128]{2,1,0:T(8,128)} %copy-done.15), calls=%async_computation.3 | async-start | bytes 16384 | tf_op jit(solution)/shard_map/slice | solution.py:603
  19.9 4.9 %collective-permute-start.4 = (f32[5,32,128]{2,1,0:T(8,128)S(1)}, f32[5,32,128]{2,1,0:T(8,128)S(1)}, u32[]{:S(2)}, u32[]{:S(2)}) collective-permute-start(f32[5,32,128]{2,1,0:T(8,128)S(1)} %get-tuple-element.32), channel_id=1, source_target_pairs={{7,0},{0,1},{1,2},{2,3},{3,4},{4,5},{5,6},{6,7},{15,8},{8,9},{9,10... | collective-permute-start | bytes 245768 | tf_op jit(solution)/shard_map/ppermute | solution.py:584
  21.9 4.7 %collective-permute-start.5 = (f32[5,32,128]{2,1,0:T(8,128)S(1)}, f32[5,32,128]{2,1,0:T(8,128)S(1)}, u32[]{:S(2)}, u32[]{:S(2)}) collective-permute-start(f32[5,32,128]{2,1,0:T(8,128)S(1)} %get-tuple-element.33), channel_id=1, source_target_pairs={{1,0},{2,1},{3,2},{4,3},{5,4},{6,5},{7,6},{0,7},{9,8},{10,9},{11,1... | collective-permute-start | bytes 245768 | tf_op jit(solution)/shard_map/ppermute | solution.py:584
  37.0 1.0 copy-start.2
  38.0 10.5 %copy-start = (f32[32,32,256]{2,1,0:T(8,128)}, f32[32,32,256]{2,1,0:T(8,128)S(1)}, u32[]{:S(2)}) copy-start(f32[32,32,256]{2,1,0:T(8,128)S(1)} %get-tuple-element.56.cx0) | copy-start | bytes 3145732
  38.0 10.5 %copy-start.1 = (f32[32,32,256]{2,1,0:T(8,128)}, f32[32,32,256]{2,1,0:T(8,128)S(1)}, u32[]{:S(2)}) copy-start(f32[32,32,256]{2,1,0:T(8,128)S(1)} %get-tuple-element.57.cy0) | copy-start | bytes 3145732
  38.0 7.1 %collective-permute-start.6 = (f32[5,4,16,128]{3,2,1,0:T(8,128)S(1)}, f32[5,4,16,128]{3,2,1,0:T(8,128)S(1)}, u32[]{:S(2)}, u32[]{:S(2)}) collective-permute-start(f32[5,4,16,128]{3,2,1,0:T(8,128)S(1)} %get-tuple-element.34), channel_id=1, source_target_pairs={{64,0},{128,64},{192,128},{0,192},{65,1},{129,65},{193,129},{1,193... | collective-permute-start | bytes 491528 | tf_op jit(solution)/shard_map/ppermute | solution.py:584
  38.3 10.2 %collective-permute-start.8 = (f32[5,4,16,128]{3,2,1,0:T(8,128)S(1)}, f32[5,4,16,128]{3,2,1,0:T(8,128)S(1)}, u32[]{:S(2)}, u32[]{:S(2)}) collective-permute-start(f32[5,4,16,128]{3,2,1,0:T(8,128)S(1)} %get-tuple-element.34), channel_id=1, source_target_pairs={{192,0},{0,64},{64,128},{128,192},{193,1},{1,65},{65,129},{129,193... | collective-permute-start | bytes 491528 | tf_op jit(solution)/shard_map/ppermute | solution.py:584
  40.1 6.9 %collective-permute-start.7 = (f32[5,4,16,128]{3,2,1,0:T(8,128)S(1)}, f32[5,4,16,128]{3,2,1,0:T(8,128)S(1)}, u32[]{:S(2)}, u32[]{:S(2)}) collective-permute-start(f32[5,4,16,128]{3,2,1,0:T(8,128)S(1)} %get-tuple-element.34), channel_id=1, source_target_pairs={{128,0},{192,64},{0,128},{64,192},{129,1},{193,65},{1,129},{65,193... | collective-permute-start | bytes 491528 | tf_op jit(solution)/shard_map/ppermute | solution.py:584
  48.7 9.5 %collective-permute-start.10 = (f32[5,24,8,128]{3,2,1,0:T(8,128)S(1)}, f32[5,24,8,128]{3,2,1,0:T(8,128)S(1)}, u32[]{:S(2)}, u32[]{:S(2)}) collective-permute-start(f32[5,24,8,128]{3,2,1,0:T(8,128)S(1)} %get-tuple-element.66), channel_id=1, source_target_pairs={{56,0},{0,8},{8,16},{16,24},{24,32},{32,40},{40,48},{48,56},{57,1}... | collective-permute-start | bytes 1474568 | tf_op jit(solution)/shard_map/ppermute | solution.py:584
  48.7 10.2 %collective-permute-start.9 = (f32[5,24,8,128]{3,2,1,0:T(8,128)S(1)}, f32[5,24,8,128]{3,2,1,0:T(8,128)S(1)}, u32[]{:S(2)}, u32[]{:S(2)}) collective-permute-start(f32[5,24,8,128]{3,2,1,0:T(8,128)S(1)} %get-tuple-element.67), channel_id=1, source_target_pairs={{8,0},{16,8},{24,16},{32,24},{40,32},{48,40},{56,48},{0,56},{9,1},... | collective-permute-start | bytes 1474568 | tf_op jit(solution)/shard_map/ppermute | solution.py:584
  63.9 8.1 %collective-permute-start.11 = (f32[5,3,32,128]{3,2,1,0:T(8,128)S(1)}, f32[5,3,32,128]{3,2,1,0:T(8,128)S(1)}, u32[]{:S(2)}, u32[]{:S(2)}) collective-permute-start(f32[5,3,32,128]{3,2,1,0:T(8,128)S(1)} %get-tuple-element.35), channel_id=1, source_target_pairs={{7,0},{0,1},{1,2},{2,3},{3,4},{4,5},{5,6},{6,7},{15,8},{8,9},{9,10... | collective-permute-start | bytes 737288 | tf_op jit(solution)/shard_map/ppermute | solution.py:584
  67.2 8.2 %collective-permute-start.12 = (f32[5,3,32,128]{3,2,1,0:T(8,128)S(1)}, f32[5,3,32,128]{3,2,1,0:T(8,128)S(1)}, u32[]{:S(2)}, u32[]{:S(2)}) collective-permute-start(f32[5,3,32,128]{3,2,1,0:T(8,128)S(1)} %get-tuple-element.36), channel_id=1, source_target_pairs={{1,0},{2,1},{3,2},{4,3},{5,4},{6,5},{7,6},{0,7},{9,8},{10,9},{11,1... | collective-permute-start | bytes 737288 | tf_op jit(solution)/shard_map/ppermute | solution.py:584
  81.9 0.8 copy-start.3
  82.7 0.8 copy-start.5
  83.6 0.8 copy-start.7
  84.3 0.8 copy-start.9
  85.1 5.0 %collective-permute-start.13 = (f32[5,4,8,128]{3,2,1,0:T(8,128)S(1)}, f32[5,4,8,128]{3,2,1,0:T(8,128)S(1)}, u32[]{:S(2)}, u32[]{:S(2)}) collective-permute-start(f32[5,4,8,128]{3,2,1,0:T(8,128)S(1)} %get-tuple-element.38), channel_id=1, source_target_pairs={{16,0},{24,8},{32,16},{40,24},{48,32},{56,40},{0,48},{8,56},{17,1}... | collective-permute-start | bytes 245768 | tf_op jit(solution)/shard_map/ppermute | solution.py:584
  88.1 5.7 %collective-permute-start.14 = (f32[5,4,8,128]{3,2,1,0:T(8,128)S(1)}, f32[5,4,8,128]{3,2,1,0:T(8,128)S(1)}, u32[]{:S(2)}, u32[]{:S(2)}) collective-permute-start(f32[5,4,8,128]{3,2,1,0:T(8,128)S(1)} %get-tuple-element.39), channel_id=1, source_target_pairs={{48,0},{56,8},{0,16},{8,24},{16,32},{24,40},{32,48},{40,56},{49,1}... | collective-permute-start | bytes 245768 | tf_op jit(solution)/shard_map/ppermute | solution.py:584
  88.1 37.4 %copy-start.4 = (f32[32,32,128]{2,1,0:T(8,128)S(1)}, f32[32,32,128]{2,1,0:T(8,128)}, u32[]{:S(2)}) copy-start(f32[32,32,128]{2,1,0:T(8,128)} %copy-done.3) | copy-start | bytes 1572868
  94.9 5.4 %collective-permute-start.15 = (f32[5,2,32,128]{3,2,1,0:T(8,128)S(1)}, f32[5,2,32,128]{3,2,1,0:T(8,128)S(1)}, u32[]{:S(2)}, u32[]{:S(2)}) collective-permute-start(f32[5,2,32,128]{3,2,1,0:T(8,128)S(1)} %get-tuple-element.40), channel_id=1, source_target_pairs={{7,0},{0,1},{1,2},{2,3},{3,4},{4,5},{5,6},{6,7},{15,8},{8,9},{9,10... | collective-permute-start | bytes 491528 | tf_op jit(solution)/shard_map/ppermute | solution.py:584
  96.7 5.3 %collective-permute-start.16 = (f32[5,2,32,128]{3,2,1,0:T(8,128)S(1)}, f32[5,2,32,128]{3,2,1,0:T(8,128)S(1)}, u32[]{:S(2)}, u32[]{:S(2)}) collective-permute-start(f32[5,2,32,128]{3,2,1,0:T(8,128)S(1)} %get-tuple-element.41), channel_id=1, source_target_pairs={{1,0},{2,1},{3,2},{4,3},{5,4},{6,5},{7,6},{0,7},{9,8},{10,9},{11,1... | collective-permute-start | bytes 491528 | tf_op jit(solution)/shard_map/ppermute | solution.py:584
  105.5 5.4 %collective-permute-start.17 = (f32[5,8,128]{2,1,0:T(8,128)S(1)}, f32[5,8,128]{2,1,0:T(8,128)S(1)}, u32[]{:S(2)}, u32[]{:S(2)}) collective-permute-start(f32[5,8,128]{2,1,0:T(8,128)S(1)} %get-tuple-element.42), channel_id=1, source_target_pairs={{32,0},{40,8},{48,16},{56,24},{0,32},{8,40},{16,48},{24,56},{33,1}... | collective-permute-start | bytes 61448 | tf_op jit(solution)/shard_map/ppermute | solution.py:584
  125.5 1.0 copy-start.6
  126.6 1.0 copy-start.8
  127.6 1.0 copy-start.10
where the time goes:
time: 150 us; the launch traced here: 149 us
  waiting for transfers between devices  53 us (35%)
  Pallas kernels  43 us (29%)
  starting transfers between devices  21.4 us (14%)
  blocking collectives  14.7 us (10%)
  local copies, waits for them, and re-layouts  13.9 us (9%)
  other arithmetic  1.72 us (1%)
    ppermute x18, waiting for transfers between devices, move(): lax.ppermute(values, axis, [((i + shift) % size, i) for i in range(size)])  53 us
    pallas_call x7, Pallas kernels, call(): pl.pallas_call(body, out_shape=[jax.ShapeDtypeStruct(s, F32) for s in out...  43 us
    ppermute x18, starting transfers between devices, move(): lax.ppermute(values, axis, [((i + shift) % size, i) for i in range(size)])  21.4 us
    all_to_all x1, blocking collectives, local(): gathered = lax.all_to_all(everyone, 'gz', 0, 0)  14.7 us
    unnamed x34, local copies, waits for them, and re-layouts  7.37 us
  transfers between devices with their start and end apart: 18, of which 16 were waited for; matrix products, arithmetic and copies ran while one was open for 1% of the time, Pallas kernels for 0%

commit v1 on v0

--- a/solution.py
+++ b/solution.py
@@ -10,7 +10,8 @@
 
 F32 = jnp.float32
 CSWEEPS = 32
-BUDGET = 48 * 1024 * 1024
+MIB = 1024 * 1024
+WIDE = 4
 
 
 def chebyshev_terms(sweep_count, lower_bound, upper_bound):
@@ -52,7 +53,7 @@
 
 def loop(lo, hi, unroll, body):
     count = hi - lo
-    assert count % unroll == 0
+    unroll = max(u for u in range(1, unroll * WIDE + 1) if count % u == 0)
 
     def step(t, carry):
         for u in range(unroll):
@@ -60,6 +61,10 @@
         return carry
 
     lax.fori_loop(0, count // unroll, step, 0)
+
+
+def copies_of(sources, targets, sems):
+    return [pltpu.make_async_copy(a, b, s) for a, b, s in zip(sources, targets, sems)]
 
 
 class Level:
@@ -111,6 +116,20 @@
     return out
 
 
+def packx0(f_ref, b_ref, up_ref, down_ref, *sems):
+    pairs = (
+        (f_ref.at[8:16], up_ref.at[0:8]),
+        (b_ref.at[7:16], up_ref.at[8:17]),
+        (f_ref.at[0:8], down_ref.at[0:8]),
+        (b_ref.at[0:9], down_ref.at[8:17]),
+    )
+    moves = [pltpu.make_async_copy(a, b, s) for (a, b), s in zip(pairs, sems)]
+    for m in moves:
+        m.start()
+    for m in moves:
+        m.wait()
+
+
 def pack0(f_ref, b_ref, up_ref, down_ref):
     for ref, start_f, start_b in ((up_ref, 120, 119), (down_ref, 0, 0)):
         (tiles,) = z_pack(lambda p: (f_ref[p], 0), 32, 32, (start_f,), 8, 16)
@@ -123,9 +142,15 @@
 
 def fine_down(
     f_ref, b_ref, ylo_ref, yhi_ref, zlo_ref, zhi_ref,
-    u_ref, cx_ref, cy_ref, cz_ref, inv_ref, rhs_ref, diag_ref, xp_ref,
-    bw, ew, va, vb, upd, cxw, dw, scr,
+    u_far, cx_far, cy_far, cz_far, inv_far, rhs_far, diag_ref, xp_ref,
+    u_ref, cx_ref, cy_ref, cz_ref, inv_ref, rhs_ref,
+    bw, ew, va, vb, upd, cxw, dw, scr, *sems,
 ):
+    saves = copies_of(
+        (cx_ref, cy_ref, cz_ref, inv_ref, rhs_ref, u_ref),
+        (cx_far, cy_far, cz_far, inv_far, rhs_far, u_far),
+        sems,
+    )
     px, py, pz = lax.axis_index("gx"), lax.axis_index("gy"), lax.axis_index("gz")
     lane1 = iota((32, 128), 1)
     lane = iota((32, 256), 1)
@@ -194,10 +219,13 @@
     y_next = (16 * py + 24) & 127
     y_open_next = jnp.where(y_next == 0, 0.0, 1.0).astype(F32)
     loop(0, 32, 2, coefficients)
+    for m in saves[:5]:
+        m.start()
     level = Level(cx_ref, cy_ref, cz_ref, inv_ref, rhs_ref, 0)
     sweep(level, va, vb, upd, 1, 31, 2, *TERMS[0])
     sweep(level, vb, va, upd, 2, 30, 2, *TERMS[1])
     sweep(level, va, u_ref, upd, 3, 29, 2, *TERMS[2], store_update=False)
+    saves[5].start()
 
     def save_diag(i):
         diag_ref[i] = dw[i + 8, 0:16, 0:128]
@@ -240,10 +268,40 @@
                 lo = res[j * 16 + t * 8 : j * 16 + t * 8 + 8]
                 hi = res[(j + 4) * 16 + t * 8 : (j + 4) * 16 + t * 8 + 8]
                 xp_ref[a, j, t * 8 : t * 8 + 8, :] = jnp.where(half, lo, roll(hi, 64, 1))
-
-
-def pack1(w_ref, up_ref, down_ref):
-    for a in range(5):
+    for m in saves:
+        m.wait()
+
+
+def packy1(x0, x1, x2, x3, up_ref, down_ref):
+    low = iota((8, 128), 0) < 4
+    xs = (x0, x1, x2, x3)
+    for a in range(5):
+        for q in range(16):
+            own = xs[q // 4][a, q % 4, 0:8, :]
+            up_ref[a, q] = own
+            down_ref[a, q] = own
+        for q in range(8):
+            one = xs[q // 4][a, q % 4, 8:16, :]
+            two = xs[2 + q // 4][a, q % 4, 8:16, :]
+            up_ref[a, 16 + q] = jnp.where(low, roll(one, 4, 0), two)
+            down_ref[a, 16 + q] = jnp.where(low, one, roll(two, 4, 0))
+
+
+def pack1(x0, x1, x2, x3, lo_ref, hi_ref, up_ref, down_ref, w_ref):
+    low = iota((8, 128), 0) < 4
+    xs = (x0, x1, x2, x3)
+    for a in range(5):
+        for q in range(16):
+            right, left = hi_ref[a, 16 + q % 8], lo_ref[a, 16 + q % 8]
+            if q < 8:
+                edge = jnp.where(low, right, roll(left, 4, 0))
+            else:
+                edge = jnp.where(low, roll(right, 4, 0), left)
+            w_ref[a, q, 0:8, :] = xs[q // 4][a, q % 4, 0:8, :]
+            w_ref[a, q, 8:16, :] = hi_ref[a, q]
+            w_ref[a, q, 16:24, :] = edge
+            w_ref[a, q, 24:32, :] = lo_ref[a, q]
+
         def get(p):
             k, j = p // 8, p % 8
             return w_ref[a, 4 * k + j % 4], 64 * (j // 4)
@@ -275,9 +333,15 @@
 
 def mid_down(
     w_ref, zlo_ref, zhi_ref,
-    u_ref, cx_ref, cy_ref, cz_ref, inv_ref, rhs_ref, own_ref, ym_ref, yp_ref,
-    va, vb, upd, ew, dw, scr,
+    u_far, cx_far, cy_far, cz_far, inv_far, rhs_far, own_ref, ym_ref, yp_ref,
+    u_ref, cx_ref, cy_ref, cz_ref, inv_ref, rhs_ref,
+    va, vb, upd, ew, dw, scr, *sems,
 ):
+    saves = copies_of(
+        (cx_ref, cy_ref, cz_ref, inv_ref, rhs_ref, u_ref),
+        (cx_far, cy_far, cz_far, inv_far, rhs_far, u_far),
+        sems,
+    )
     lane = iota((32, 128), 1)
     targets = (va, cx_ref, cy_ref, cz_ref, ew)
     for a in range(5):
@@ -307,10 +371,13 @@
         va[i] = first
 
     loop(0, 32, 4, coefficients)
+    for m in saves[:5]:
+        m.start()
     level = Level(cx_ref, cy_ref, cz_ref, inv_ref, rhs_ref, 32)
     sweep(level, va, vb, upd, 0, 32, 4, *TERMS[0])
     sweep(level, vb, va, upd, 0, 32, 4, *TERMS[1])
     sweep(level, va, u_ref, upd, 0, 32, 4, *TERMS[2], store_update=False)
+    saves[5].start()
     for p in range(16):
         i = 2 * p
         _, d0 = level.defect(u_ref, i)
@@ -329,18 +396,29 @@
         d = cx[p] + cx_next[p] + (cy[p] + roll(cy[p], -1, 0)) + (cz[p] + roll(cz[p], -1, 1)) + e[p]
         planes.append((f[p], cx[p], cy[p], cz[p], d))
     lane8 = iota((16, 128), 1)
+    row8 = iota((8, 128), 0)
     for a in range(5):
         for j in range(4):
             packed = planes[j][a]
             for k in range(1, 4):
                 packed = jnp.where(lane8 >= 32 * k, roll(planes[4 * k + j][a], 32 * k, 1), packed)
             own_ref[a, j] = packed
-            ym_ref[a, j] = roll(packed, 1, 0)[0:8]
-            yp_ref[a, j] = roll(packed, 3, 0)[0:8]
-
-
-def pack2(w_ref, up_ref, down_ref):
-    for a in range(5):
+            ym_ref[a, j] = jnp.where(row8 == 7, packed[8:16], packed[0:8])
+            yp_ref[a, j] = jnp.where(row8 < 5, packed[0:8], packed[8:16])
+    for m in saves:
+        m.wait()
+
+
+def pack2(own_ref, hi_ref, far_ref, lo_ref, up_ref, down_ref, w_ref):
+    row = iota((8, 128), 0)
+    for a in range(5):
+        for j in range(4):
+            hi, far, lo = hi_ref[a, j], far_ref[a, j], lo_ref[a, j]
+            w_ref[a, j, 0:8, :] = jnp.where(row == 7, hi, own_ref[a, j, 0:8, :])
+            w_ref[a, j, 8:16, :] = jnp.where(row == 7, far, hi)
+            w_ref[a, j, 16:24, :] = jnp.where(row < 5, far, lo)
+            w_ref[a, j, 24:32, :] = jnp.where(row < 5, lo, own_ref[a, j, 8:16, :])
+
         def get(p):
             return w_ref[a, p % 4], 32 * (p // 4)
 
@@ -352,9 +430,15 @@
 
 def low_down(
     w_ref, zlo_ref, zhi_ref,
-    u_ref, cx_ref, cy_ref, cz_ref, inv_ref, rhs_ref, own_ref,
-    va, vb, upd, dw, scr,
+    u_far, cx_far, cy_far, cz_far, inv_far, rhs_far, own_ref,
+    u_ref, cx_ref, cy_ref, cz_ref, inv_ref, rhs_ref,
+    va, vb, upd, dw, scr, *sems,
 ):
+    saves = copies_of(
+        (cx_ref, cy_ref, cz_ref, inv_ref, rhs_ref, u_ref),
+        (cx_far, cy_far, cz_far, inv_far, rhs_far, u_far),
+        sems,
+    )
     lane = iota((32, 128), 1)
     targets = (va, cx_ref, cy_ref, cz_ref, dw)
     for a in range(5):
@@ -377,10 +461,13 @@
         va[i] = first
 
     loop(0, 16, 4, coefficients)
+    for m in saves[:5]:
+        m.start()
     level = Level(cx_ref, cy_ref, cz_ref, inv_ref, rhs_ref, 16)
     sweep(level, va, vb, upd, 0, 16, 4, *TERMS[0])
     sweep(level, vb, va, upd, 0, 16, 4, *TERMS[1])
     sweep(level, va, u_ref, upd, 0, 16, 4, *TERMS[2], store_update=False)
+    saves[5].start()
 
     def edge(i):
         above = (i + 1) & 15
@@ -410,7 +497,9 @@
         packed = planes[0][a]
         for p in range(1, 8):
             packed = jnp.where(lane16 >= 16 * p, roll(planes[p][a], 16 * p, 1), packed)
-        own_ref[a] = roll(packed, 3, 0)[0:8]
+        own_ref[a] = packed
+    for m in saves:
+        m.wait()
 
 
 def spread(dup, w, rows, matrix):
@@ -437,18 +526,23 @@
 
 
 def up(
-    g_ref,
-    u2, cx2, cy2, cz2, inv2, rhs2,
-    u1, cx1, cy1, cz1, inv1, rhs1,
-    u0, cx0, cy0, cz0, inv0, rhs0, diag0,
-    sol_ref, res_ref,
-    l3, inv3, rhs3, u3, va3, vb3, upd3, scr3,
-    va2, vb2, upd2, dup2, va1, vb1, upd1, dup1, va0, vb0, upd0, dup0,
+    g_ref, *refs,
 ):
+    fars, refs = refs[:19], refs[19:]
+    (sol_ref, res_ref), refs = refs[:2], refs[2:]
+    (l3, inv3, rhs3, u3, va3, vb3, upd3, scr3), refs = refs[:8], refs[8:]
+    (va2, vb2, upd2, dup2, va1, vb1, upd1, dup1, va0, vb0, upd0, dup0), refs = refs[:12], refs[12:]
+    nears, sems = refs[:19], refs[19:]
+    u2, cx2, cy2, cz2, inv2, rhs2 = nears[:6]
+    u1, cx1, cy1, cz1, inv1, rhs1 = nears[6:12]
+    u0, cx0, cy0, cz0, inv0, rhs0, diag0 = nears[12:]
+    loads = copies_of(fars, nears, sems)
+    for m in loads:
+        m.start()
     me = lax.axis_index("gz")
     lane = iota((16, 128), 1)
     for a in range(5):
-        tiles = [roll(g_ref[(me + k) & 7, a], -3, 0) for k in range(8)]
+        tiles = [g_ref[(me + k) & 7, a] for k in range(8)]
         for p in range(8):
             plane = roll(tiles[0], -16 * p, 1)
             for k in range(1, 8):
@@ -531,6 +625,8 @@
         p = i // 2
         va3[i] = u3[i] + wide[16 * p : 16 * p + 16]
     post(level, va3, vb3, upd3, [(0, 8)] * 4, 8)
+    for m in loads[:6]:
+        m.wait()
     w3 = va3[...].reshape(128, 128)
     wide = spread(dup2, w3, 16, spread_matrix(96, 128))
     for i in range(16):
@@ -538,6 +634,8 @@
         va2[i] = u2[i] + wide[32 * p : 32 * p + 32]
     level = Level(cx2, cy2, cz2, inv2, rhs2, 16)
     post(level, va2, vb2, upd2, [(0, 16)] * 4, 4)
+    for m in loads[6:12]:
+        m.wait()
     w2 = jnp.concatenate([va2[:, 0:8, :], va2[:, 24:32, :]], axis=1).reshape(256, 128)
     wide = spread(dup1, w2, 16, spread_matrix(96, 128))
     for i in range(32):
@@ -545,6 +643,8 @@
         va1[i] = u1[i] + wide[32 * p : 32 * p + 32]
     level = Level(cx1, cy1, cz1, inv1, rhs1, 32)
     post(level, va1, vb1, upd1, [(0, 32)] * 4, 4)
+    for m in loads[12:]:
+        m.wait()
     rows = [
         jnp.concatenate([va1[i % 32, 0:8, :], mix_rows(va1, i % 32)], axis=0) for i in range(-4, 12)
     ]
@@ -569,12 +669,16 @@
     return jnp.where(low, ref[i, 8:16, :], ref[i, 24:32, :])
 
 
-def call(body, args, outs, scratch=()):
+def call(body, args, outs, scratch=(), limit=16, far_in=(), far_out=(), copies=0):
+    near, far = pl.BlockSpec(memory_space=pltpu.VMEM), pl.BlockSpec(memory_space=pltpu.HBM)
     return pl.pallas_call(
         body,
         out_shape=[jax.ShapeDtypeStruct(s, F32) for s in outs],
-        scratch_shapes=[pltpu.VMEM(s, F32) for s in scratch],
-        compiler_params=pltpu.CompilerParams(vmem_limit_bytes=BUDGET),
+        in_specs=[far if i in far_in else near for i in range(len(args))],
+        out_specs=[far if i in far_out else near for i in range(len(outs))],
+        scratch_shapes=[pltpu.VMEM(s, F32) for s in scratch]
+        + [pltpu.SemaphoreType.DMA] * copies,
+        compiler_params=pltpu.CompilerParams(vmem_limit_bytes=limit * MIB),
         name=body.__name__,
     )(*args)
 
@@ -586,8 +690,10 @@
 
 def local(source, conductivity):
     f, b = source, conductivity
-    from_lo = move(jnp.concatenate([f[8:16], b[7:16]]), "gx", -1)
-    from_hi = move(jnp.concatenate([f[0:8], b[0:9]]), "gx", 1)
+    to_hi, to_lo = call(
+        packx0, (f, b), [(17, 16, 128)] * 2, far_in=(0, 1), copies=4
+    )
+    from_lo, from_hi = move(to_hi, "gx", -1), move(to_lo, "gx", 1)
     fx = jnp.concatenate([from_lo[:8], f, from_hi[:8]])
     bx = jnp.concatenate([from_lo[8:], b, from_hi[8:]])
 
@@ -611,51 +717,42 @@
         fine_down,
         (fw, bw, ylo, yhi, zlo, zhi),
         [big] * 6 + [(16, 16, 128), (5, 4, 16, 128)],
-        [(34, 32, 256), big, big, big, big, (33, 32, 256), big, (5, 2, 256, 128)],
-    )
-    x_all = jnp.concatenate([xp] + [move(xp, "gx", k) for k in (1, 2, 3)], axis=1)
-    own, halo = x_all[:, :, 0:8], x_all[:, :, 8:16]
-
-    def with_rows(at):
-        part = halo[:, :, at : at + 4]
-        return jnp.concatenate(
-            [own, jnp.concatenate([part[:, :8], part[:, 8:]], axis=2)], axis=1
-        )
-
-    from_hi = move(with_rows(0), "gy", 1)
-    from_lo = move(with_rows(4), "gy", -1)
-
-    def unfold(got):
-        part = got[:, 16:]
-        return jnp.concatenate([part[:, :, 0:4], part[:, :, 4:8]], axis=1)
-
-    w1 = jnp.concatenate(
-        [own, from_hi[:, :16], unfold(from_hi), unfold(from_lo), from_lo[:, :16]], axis=2
-    )
-    up1, down1 = call(pack1, (w1,), [(5, 3, 32, 128)] * 2)
+        [big] * 6 + [(34, 32, 256), big, big, big, big, (33, 32, 256), big, (5, 2, 256, 128)],
+        28,
+        far_out=range(6),
+        copies=6,
+    )
+    xs = [xp] + [move(xp, "gx", k) for k in (1, 2, 3)]
+    to_hi, to_lo = call(packy1, xs, [(5, 24, 8, 128)] * 2)
+    from_lo, from_hi = move(to_hi, "gy", -1), move(to_lo, "gy", 1)
+    up1, down1, w1 = call(
+        pack1, xs + [from_lo, from_hi], [(5, 3, 32, 128)] * 2 + [(5, 16, 32, 128)]
+    )
     zlo, zhi = move(up1, "gz", -1), move(down1, "gz", 1)
     mid = (32, 32, 128)
     u1, cx1, cy1, cz1, inv1, rhs1, own2, ym, yp = call(
         mid_down,
         (w1, zlo, zhi),
         [mid] * 6 + [(5, 4, 16, 128), (5, 4, 8, 128), (5, 4, 8, 128)],
-        [mid] * 5 + [(5, 512, 128)],
-    )
-    from_hi, from_lo = move(ym, "gy", 2), move(yp, "gy", -2)
-    w2 = jnp.concatenate(
-        [own2[:, :, 0:7], from_hi, own2[:, :, 7:13], from_lo, own2[:, :, 13:16]], axis=2
-    )
-    up2, down2 = call(pack2, (w2,), [(5, 2, 32, 128)] * 2)
+        [mid] * 11 + [(5, 512, 128)],
+        far_out=range(6),
+        copies=6,
+    )
+    from_hi, from_lo, far = move(ym, "gy", 2), move(yp, "gy", -2), move(ym, "gy", 4)
+    up2, down2, w2 = call(
+        pack2, (own2, from_hi, far, from_lo), [(5, 2, 32, 128)] * 2 + [(5, 4, 32, 128)]
+    )
     zlo, zhi = move(up2, "gz", -1), move(down2, "gz", 1)
     low = (16, 32, 128)
     u2, cx2, cy2, cz2, inv2, rhs2, own3 = call(
         low_down,
         (w2, zlo, zhi),
-        [low] * 6 + [(5, 8, 128)],
-        [low] * 4 + [(5, 256, 128)],
-    )
-    both = jnp.concatenate([own3, move(own3, "gy", 4)], axis=1)
-    everyone = jnp.broadcast_to(both[None], (8, 5, 16, 128))
+        [low] * 6 + [(5, 16, 128)],
+        [low] * 10 + [(5, 256, 128)],
+        far_out=range(6),
+        copies=6,
+    )
+    everyone = jnp.broadcast_to(own3[None], (8, 5, 16, 128))
     gathered = lax.all_to_all(everyone, "gz", 0, 0)
     tiny = (8, 16, 128)
     return tuple(
@@ -669,7 +766,11 @@
             ),
             [(16, 16, 128)] * 2,
             [(5,) + tiny] + [tiny] * 6 + [(5, 64, 128)]
-            + [low] * 3 + [(256, 128)] + [mid] * 3 + [(512, 128)] + [big] * 3 + [(512, 128)],
+            + [low] * 3 + [(256, 128)] + [mid] * 3 + [(512, 128)] + [big] * 3 + [(512, 128)]
+            + [low] * 6 + [mid] * 6 + [big] * 6 + [(16, 16, 128)],
+            28,
+            far_in=range(1, 20),
+            copies=19,
         )
     )
 

time: 150 us -> 121 us (0.81)
  local copies, waits for them, and re-layouts: 13.9 us -> 1.97 us
  Pallas kernels: 43 us -> 32.1 us
  waiting for transfers between devices: 53 us -> 42.1 us
  starting transfers between devices: 21.4 us -> 27.2 us
  other arithmetic: 1.72 us -> 0.16 us
    ppermute x18, waiting for transfers between devices: 53 us -> 42.1 us  [move(): lax.ppermute(values, axis, [((i + shift) % size, i) for i in range(size)])]
    pallas_call x7 -> x9, Pallas kernels: 43 us -> 32.1 us  [call(): pl.pallas_call(body, out_shape=[jax.ShapeDtypeStruct(s, F32) for s in out...]
    ppermute x18, starting transfers between devices: 21.4 us -> 27.2 us  [move(): lax.ppermute(values, axis, [((i + shift) % size, i) for i in range(size)])]
    unnamed x34 -> x10, local copies, waits for them, and re-layouts: 7.37 us -> 1.81 us
    concatenate x4 -> x0, local copies, waits for them, and re-layouts: 3.37 us -> none  [the longest x1 2.85 us: local(): jnp.concatenate([own, from_hi[:, :16], unfold(from_hi), unfold(from_lo),...]
    slice x11 -> x0, local copies, waits for them, and re-layouts: 2.09 us -> none  [the longest x2 1.91 us: local(): from_lo = move(jnp.concatenate([f[8:16], b[7:16]]), 'gx', -1)]
    concatenate x7 -> x0, other arithmetic: 1.56 us -> none  [the longest x2 1.41 us: unfold(): return jnp.concatenate([part[:, :, 0:4], part[:, :, 4:8]], axis=1)]
  transfers between devices with their start and end apart: 18 -> 18, of which waited for: 16 -> 14; matrix products, arithmetic and copies ran while one was open for 1% -> 0% of each run, Pallas kernels for 0% -> 0%
where the time goes in v1:
time: 121 us; the launch traced here: 120 us
  waiting for transfers between devices  42.1 us (35%)
  Pallas kernels  32.1 us (27%)
  starting transfers between devices  27.2 us (22%)
  blocking collectives  15.3 us (13%)
  local copies, waits for them, and re-layouts  1.97 us (2%)
    ppermute x18, waiting for transfers between devices, move(): lax.ppermute(values, axis, [((i + shift) % size, i) for i in range(size)])  42.1 us
    pallas_call x9, Pallas kernels, call(): pl.pallas_call(body, out_shape=[jax.ShapeDtypeStruct(s, F32) for s in out...  32.1 us
    ppermute x18, starting transfers between devices, move(): lax.ppermute(values, axis, [((i + shift) % size, i) for i in range(size)])  27.2 us
    all_to_all x1, blocking collectives, local(): gathered = lax.all_to_all(everyone, 'gz', 0, 0)  15.3 us
  transfers between devices with their start and end apart: 18, of which 14 were waited for; matrix products, arithmetic and copies ran while one was open for 0% of the time, Pallas kernels for 0%

profile of v1, /device:TPU:32, one launch (start us, length us, event | category | flops | bytes accessed | tf_op | source)
XLA Modules:
  0.0 119.9 jit_solution(7673501554596064458)
XLA Ops:
  0.6 0.0 copy-start
  0.6 0.9 copy-done
  1.5 0.0 copy-start.1
  1.5 0.9 copy-done.1
  2.4 0.4 packx0.1
  2.8 1.6 %collective-permute-start = (f32[17,16,128]{2,1,0:T(8,128)S(1)}, f32[17,16,128]{2,1,0:T(8,128)S(1)}, u32[]{:S(2)}, u32[]{:S(2)}) collective-permute-start(f32[17,16,128]{2,1,0:T(8,128)S(1)} %get-tuple-element.38), channel_id=1, source_target_pairs={{192,0},{0,64},{64,128},{128,192},{193,1},{1,65},{65,129},{129,193... | collective-permute-start | bytes 417800 | tf_op jit(solution)/shard_map/ppermute | solution.py:688
  4.4 1.7 %collective-permute-start.1 = (f32[17,16,128]{2,1,0:T(8,128)S(1)}, f32[17,16,128]{2,1,0:T(8,128)S(1)}, u32[]{:S(2)}, u32[]{:S(2)}) collective-permute-start(f32[17,16,128]{2,1,0:T(8,128)S(1)} %get-tuple-element.39), channel_id=1, source_target_pairs={{64,0},{128,64},{192,128},{0,192},{65,1},{129,65},{193,129},{1,193... | collective-permute-start | bytes 417800 | tf_op jit(solution)/shard_map/ppermute | solution.py:688
  6.1 3.4 %collective-permute-done = f32[17,16,128]{2,1,0:T(8,128)S(1)} collective-permute-done((f32[17,16,128]{2,1,0:T(8,128)S(1)}, f32[17,16,128]{2,1,0:T(8,128)S(1)}, u32[]{:S(2)}, u32[]{:S(2)}) %collective-permute-start) | collective-permute-done | bytes 139296 | tf_op jit(solution)/shard_map/ppermute | solution.py:688
  9.5 0.0 copy-start.3
  9.5 0.0 collective-permute-done.1
  9.5 0.0 copy-start.4
  9.6 0.0 copy-start.2
  9.7 0.0 collective-permute-start.3
  9.8 2.9 %collective-permute-start.2 = (f32[66,8,128]{2,1,0:T(8,128)S(1)}, f32[66,8,128]{2,1,0:T(8,128)S(1)}, u32[]{:S(2)}, u32[]{:S(2)}) collective-permute-start(f32[66,8,128]{2,1,0:T(8,128)S(1)} %pad_maximum_fusion.2), channel_id=1, source_target_pairs={{8,0},{16,8},{24,16},{32,24},{40,32},{48,40},{56,48},{0,56},{9,1},... | collective-permute-start | bytes 811016 | tf_op jit(solution)/shard_map/ppermute | solution.py:688
  12.7 0.0 copy-done.2
  12.7 0.0 copy-done.3
  12.7 0.0 slice-start
  12.7 0.0 copy-done.4
  12.7 0.0 slice-start.1
  12.8 0.0 slice-start.2
  12.8 4.1 %collective-permute-done.3 = f32[66,8,128]{2,1,0:T(8,128)S(1)} collective-permute-done((f32[66,8,128]{2,1,0:T(8,128)S(1)}, f32[66,8,128]{2,1,0:T(8,128)S(1)}, u32[]{:S(2)}, u32[]{:S(2)}) %collective-permute-start.3) | collective-permute-done | bytes 270368 | tf_op jit(solution)/shard_map/ppermute | solution.py:688
  16.9 0.0 collective-permute-done.2
  16.9 0.0 slice-done
  17.0 0.0 slice-done.1
  17.0 0.0 slice-done.2
  17.0 0.6 pack0.1
  17.6 2.0 %collective-permute-start.4 = (f32[5,32,128]{2,1,0:T(8,128)S(1)}, f32[5,32,128]{2,1,0:T(8,128)S(1)}, u32[]{:S(2)}, u32[]{:S(2)}) collective-permute-start(f32[5,32,128]{2,1,0:T(8,128)S(1)} %get-tuple-element.40), channel_id=1, source_target_pairs={{7,0},{0,1},{1,2},{2,3},{3,4},{4,5},{5,6},{6,7},{15,8},{8,9},{9,10... | collective-permute-start | bytes 245768 | tf_op jit(solution)/shard_map/ppermute | solution.py:688
  19.6 0.1 collective-permute-start.5
  19.7 2.8 %collective-permute-done.4.zlo_ref = f32[5,32,128]{2,1,0:T(8,128)S(1)} collective-permute-done((f32[5,32,128]{2,1,0:T(8,128)S(1)}, f32[5,32,128]{2,1,0:T(8,128)S(1)}, u32[]{:S(2)}, u32[]{:S(2)}) %collective-permute-start.4) | collective-permute-done | bytes 81952 | tf_op jit(solution)/shard_map/ppermute | solution.py:688
  22.5 1.8 %collective-permute-done.5.zhi_ref = f32[5,32,128]{2,1,0:T(8,128)S(1)} collective-permute-done((f32[5,32,128]{2,1,0:T(8,128)S(1)}, f32[5,32,128]{2,1,0:T(8,128)S(1)}, u32[]{:S(2)}, u32[]{:S(2)}) %collective-permute-start.5) | collective-permute-done | bytes 81952 | tf_op jit(solution)/shard_map/ppermute | solution.py:688
  24.3 7.5 %fine_down.1 = (f32[32,32,256]{2,1,0:T(8,128)S(1)}, f32[32,32,256]{2,1,0:T(8,128)S(1)}, f32[32,32,256]{2,1,0:T(8,128)S(1)}, f32[32,32,256]{2,1,0:T(8,128)S(1)}, ...) custom-call(f32[32,32,128]{2,1,0:T(8,128)S(1)} %pad_maximum_fusion.f, ...), custom_call_target="tpu_custom_call" | custom-call | tf_op jit(solution)/shard_map/fine_down/pallas_call | solution.py:674
  31.8 1.5 %collective-permute-start.8 = (f32[5,4,16,128]{3,2,1,0:T(8,128)S(1)}, f32[5,4,16,128]{3,2,1,0:T(8,128)S(1)}, u32[]{:S(2)}, u32[]{:S(2)}) collective-permute-start(f32[5,4,16,128]{3,2,1,0:T(8,128)S(1)} %get-tuple-element.42.x0), channel_id=1, source_target_pairs={{192,0},{0,64},{64,128},{128,192},{193,1},{1,65},{65,129},{129,193... | collective-permute-start | bytes 491528 | tf_op jit(solution)/shard_map/ppermute | solution.py:688
  33.3 2.9 %collective-permute-start.7 = (f32[5,4,16,128]{3,2,1,0:T(8,128)S(1)}, f32[5,4,16,128]{3,2,1,0:T(8,128)S(1)}, u32[]{:S(2)}, u32[]{:S(2)}) collective-permute-start(f32[5,4,16,128]{3,2,1,0:T(8,128)S(1)} %get-tuple-element.42.x0), channel_id=1, source_target_pairs={{128,0},{192,64},{0,128},{64,192},{129,1},{193,65},{1,129},{65,193... | collective-permute-start | bytes 491528 | tf_op jit(solution)/shard_map/ppermute | solution.py:688
  36.3 0.9 collective-permute-start.6
  37.2 1.8 %collective-permute-done.8.x3 = f32[5,4,16,128]{3,2,1,0:T(8,128)S(1)} collective-permute-done((f32[5,4,16,128]{3,2,1,0:T(8,128)S(1)}, f32[5,4,16,128]{3,2,1,0:T(8,128)S(1)}, u32[]{:S(2)}, u32[]{:S(2)}) %collective-permute-start.8) | collective-permute-done | bytes 163872 | tf_op jit(solution)/shard_map/ppermute | solution.py:688
  39.0 4.4 %collective-permute-done.7.x2 = f32[5,4,16,128]{3,2,1,0:T(8,128)S(1)} collective-permute-done((f32[5,4,16,128]{3,2,1,0:T(8,128)S(1)}, f32[5,4,16,128]{3,2,1,0:T(8,128)S(1)}, u32[]{:S(2)}, u32[]{:S(2)}) %collective-permute-start.7) | collective-permute-done | bytes 163872 | tf_op jit(solution)/shard_map/ppermute | solution.py:688
  43.4 0.0 collective-permute-done.6.x1
  43.4 0.1 packy1.1
  43.5 0.0 collective-permute-start.9
  43.5 2.9 %collective-permute-start.10 = (f32[5,24,8,128]{3,2,1,0:T(8,128)S(1)}, f32[5,24,8,128]{3,2,1,0:T(8,128)S(1)}, u32[]{:S(2)}, u32[]{:S(2)}) collective-permute-start(f32[5,24,8,128]{3,2,1,0:T(8,128)S(1)} %get-tuple-element.44), channel_id=1, source_target_pairs={{8,0},{16,8},{24,16},{32,24},{40,32},{48,40},{56,48},{0,56},{9,1},... | collective-permute-start | bytes 1474568 | tf_op jit(solution)/shard_map/ppermute | solution.py:688
  46.5 6.5 %collective-permute-done.9.lo_ref = f32[5,24,8,128]{3,2,1,0:T(8,128)S(1)} collective-permute-done((f32[5,24,8,128]{3,2,1,0:T(8,128)S(1)}, f32[5,24,8,128]{3,2,1,0:T(8,128)S(1)}, u32[]{:S(2)}, u32[]{:S(2)}) %collective-permute-start.9) | collective-permute-done | bytes 491552 | tf_op jit(solution)/shard_map/ppermute | solution.py:688
  53.0 0.0 collective-permute-done.10.hi_ref
  53.0 1.4 %pack1.1 = (f32[5,3,32,128]{3,2,1,0:T(8,128)S(1)}, f32[5,3,32,128]{3,2,1,0:T(8,128)S(1)}, f32[5,16,32,128]{3,2,1,0:T(8,128)S(1)}) custom-call(f32[5,4,16,128]{3,2,1,0:T(8,128)S(1)} %get-tuple-element.42.x0, f32[5,4,16,128]{3,2,1,0:T(8,128)S(1)} %collective-permute-done.6.x1, f32[5,4,16,128]{3,2,1,0:T(8,128)S(1)} %collective-permute-done.7.x2, ...), custom_call_target="tpu_custom_call" | custom-call | tf_op jit(solution)/shard_map/pack1/pallas_call | solution.py:674
  54.4 3.3 %collective-permute-start.11 = (f32[5,3,32,128]{3,2,1,0:T(8,128)S(1)}, f32[5,3,32,128]{3,2,1,0:T(8,128)S(1)}, u32[]{:S(2)}, u32[]{:S(2)}) collective-permute-start(f32[5,3,32,128]{3,2,1,0:T(8,128)S(1)} %get-tuple-element.46), channel_id=1, source_target_pairs={{7,0},{0,1},{1,2},{2,3},{3,4},{4,5},{5,6},{6,7},{15,8},{8,9},{9,10... | collective-permute-start | bytes 737288 | tf_op jit(solution)/shard_map/ppermute | solution.py:688
  57.7 0.0 collective-permute-start.12
  57.7 5.5 %collective-permute-done.11.zlo_ref = f32[5,3,32,128]{3,2,1,0:T(8,128)S(1)} collective-permute-done((f32[5,3,32,128]{3,2,1,0:T(8,128)S(1)}, f32[5,3,32,128]{3,2,1,0:T(8,128)S(1)}, u32[]{:S(2)}, u32[]{:S(2)}) %collective-permute-start.11) | collective-permute-done | bytes 245792 | tf_op jit(solution)/shard_map/ppermute | solution.py:688
  63.2 3.5 %collective-permute-done.12.zhi_ref = f32[5,3,32,128]{3,2,1,0:T(8,128)S(1)} collective-permute-done((f32[5,3,32,128]{3,2,1,0:T(8,128)S(1)}, f32[5,3,32,128]{3,2,1,0:T(8,128)S(1)}, u32[]{:S(2)}, u32[]{:S(2)}) %collective-permute-start.12) | collective-permute-done | bytes 245792 | tf_op jit(solution)/shard_map/ppermute | solution.py:688
  66.6 5.1 %mid_down.1 = (f32[32,32,128]{2,1,0:T(8,128)S(1)}, f32[32,32,128]{2,1,0:T(8,128)S(1)}, f32[32,32,128]{2,1,0:T(8,128)S(1)}, f32[32,32,128]{2,1,0:T(8,128)S(1)}, f...) custom-call(f32[5,16,32,128]{3,2,1,0:T(8,128)S(1)} %get-tuple-elemen, ...), custom_call_target="tpu_custom_call" | custom-call | tf_op jit(solution)/shard_map/mid_down/pallas_call | solution.py:674
  71.7 0.1 collective-permute-start.15
  71.8 3.2 %collective-permute-start.14 = (f32[5,4,8,128]{3,2,1,0:T(8,128)S(1)}, f32[5,4,8,128]{3,2,1,0:T(8,128)S(1)}, u32[]{:S(2)}, u32[]{:S(2)}) collective-permute-start(f32[5,4,8,128]{3,2,1,0:T(8,128)S(1)} %get-tuple-element.49), channel_id=1, source_target_pairs={{32,0},{40,8},{48,16},{56,24},{0,32},{8,40},{16,48},{24,56},{33,1}... | collective-permute-start | bytes 245768 | tf_op jit(solution)/shard_map/ppermute | solution.py:688
  75.0 1.7 %collective-permute-start.13 = (f32[5,4,8,128]{3,2,1,0:T(8,128)S(1)}, f32[5,4,8,128]{3,2,1,0:T(8,128)S(1)}, u32[]{:S(2)}, u32[]{:S(2)}) collective-permute-start(f32[5,4,8,128]{3,2,1,0:T(8,128)S(1)} %get-tuple-element.49), channel_id=1, source_target_pairs={{16,0},{24,8},{32,16},{40,24},{48,32},{56,40},{0,48},{8,56},{17,1}... | collective-permute-start | bytes 245768 | tf_op jit(solution)/shard_map/ppermute | solution.py:688
  76.8 1.0 collective-permute-done.15.lo_ref
  77.8 1.7 %collective-permute-done.14.far_ref = f32[5,4,8,128]{3,2,1,0:T(8,128)S(1)} collective-permute-done((f32[5,4,8,128]{3,2,1,0:T(8,128)S(1)}, f32[5,4,8,128]{3,2,1,0:T(8,128)S(1)}, u32[]{:S(2)}, u32[]{:S(2)}) %collective-permute-start.14) | collective-permute-done | bytes 81952 | tf_op jit(solution)/shard_map/ppermute | solution.py:688
  79.4 0.6 collective-permute-done.13.hi_ref
  80.0 0.7 pack2.1
  80.8 1.8 %collective-permute-start.16 = (f32[5,2,32,128]{3,2,1,0:T(8,128)S(1)}, f32[5,2,32,128]{3,2,1,0:T(8,128)S(1)}, u32[]{:S(2)}, u32[]{:S(2)}) collective-permute-start(f32[5,2,32,128]{3,2,1,0:T(8,128)S(1)} %get-tuple-element.52), channel_id=1, source_target_pairs={{7,0},{0,1},{1,2},{2,3},{3,4},{4,5},{5,6},{6,7},{15,8},{8,9},{9,10... | collective-permute-start | bytes 491528 | tf_op jit(solution)/shard_map/ppermute | solution.py:688
  82.6 0.3 collective-permute-start.17
  82.9 3.3 %collective-permute-done.16.zlo_ref = f32[5,2,32,128]{3,2,1,0:T(8,128)S(1)} collective-permute-done((f32[5,2,32,128]{3,2,1,0:T(8,128)S(1)}, f32[5,2,32,128]{3,2,1,0:T(8,128)S(1)}, u32[]{:S(2)}, u32[]{:S(2)}) %collective-permute-start.16) | collective-permute-done | bytes 163872 | tf_op jit(solution)/shard_map/ppermute | solution.py:688
  86.2 1.8 %collective-permute-done.17.zhi_ref = f32[5,2,32,128]{3,2,1,0:T(8,128)S(1)} collective-permute-done((f32[5,2,32,128]{3,2,1,0:T(8,128)S(1)}, f32[5,2,32,128]{3,2,1,0:T(8,128)S(1)}, u32[]{:S(2)}, u32[]{:S(2)}) %collective-permute-start.17) | collective-permute-done | bytes 163872 | tf_op jit(solution)/shard_map/ppermute | solution.py:688
  87.9 2.7 %low_down.1 = (f32[16,32,128]{2,1,0:T(8,128)S(1)}, f32[16,32,128]{2,1,0:T(8,128)S(1)}, f32[16,32,128]{2,1,0:T(8,128)S(1)}, f32[16,32,128]{2,1,0:T(8,128)S(1)}, f...) custom-call(f32[5,4,32,128]{3,2,1,0:T(8,128)S(1)} %get-tuple-element.51.w_ref, ...), custom_call_target="tpu_custom_call" | custom-call | tf_op jit(solution)/shard_map/low_down/pallas_call | solution.py:674
  90.6 15.3 %all_to_all.5.g_ref = f32[8,5,16,128]{3,2,1,0:T(8,128)S(1)} all-to-all(f32[8,5,16,128]{3,2,1,0:T(8,128)S(1)} %broadcast_in_dim.2), channel_id=1, replica_groups=mesh['gx'=4,'gy'=8,'gz'=8] {'gz'}, dimensions={0} | all-to-all | bytes 655360 | tf_op jit(solution)/shard_map/all_to_all | solution.py:756
  105.9 13.8 %up.1 = (f32[16,16,128]{2,1,0:T(8,128)}, f32[16,16,128]{2,1,0:T(8,128)}) custom-call(f32[8,5,16,128]{3,2,1,0:T(8,128)S(1)} %all_to_all.5.g_ref, f32[16,32,128]{2,1,0:T(8,128)S(1)} %get-tuple-element.55.refs_0_, f32[16,32,128]{2,1,0:T(8,128)S(1)} %get-tuple-element.56.refs_1_, f32[16,32,128]{2,1,0:T(8,128)S(1)} %get-tuple-element.57.refs_2_, ...), custom_call_target="tpu_custom_call" | custom-call | tf_op jit(solution)/shard_map/up/pallas_call | solution.py:674
  (17 shorter events, 0.3 us)
Async XLA Ops:
  0.6 0.9 copy-start
  1.5 0.9 copy-start.1
  2.8 6.7 %collective-permute-start = (f32[17,16,128]{2,1,0:T(8,128)S(1)}, f32[17,16,128]{2,1,0:T(8,128)S(1)}, u32[]{:S(2)}, u32[]{:S(2)}) collective-permute-start(f32[17,16,128]{2,1,0:T(8,128)S(1)} %get-tuple-element.38), channel_id=1, source_target_pairs={{192,0},{0,64},{64,128},{128,192},{193,1},{1,65},{65,129},{129,193... | collective-permute-start | bytes 417800 | tf_op jit(solution)/shard_map/ppermute | solution.py:688
  4.4 5.1 %collective-permute-start.1 = (f32[17,16,128]{2,1,0:T(8,128)S(1)}, f32[17,16,128]{2,1,0:T(8,128)S(1)}, u32[]{:S(2)}, u32[]{:S(2)}) collective-permute-start(f32[17,16,128]{2,1,0:T(8,128)S(1)} %get-tuple-element.39), channel_id=1, source_target_pairs={{64,0},{128,64},{192,128},{0,192},{65,1},{129,65},{193,129},{1,193... | collective-permute-start | bytes 417800 | tf_op jit(solution)/shard_map/ppermute | solution.py:688
  9.5 3.2 %copy-start.3 = (f32[17,16,128]{2,1,0:T(8,128)}, f32[17,16,128]{2,1,0:T(8,128)S(1)}, u32[]{:S(2)}) copy-start(f32[17,16,128]{2,1,0:T(8,128)S(1)} %collective-permute-done) | copy-start | bytes 417796
  9.5 3.2 %copy-start.4 = (f32[17,16,128]{2,1,0:T(8,128)}, f32[17,16,128]{2,1,0:T(8,128)S(1)}, u32[]{:S(2)}) copy-start(f32[17,16,128]{2,1,0:T(8,128)S(1)} %collective-permute-done.1) | copy-start | bytes 417796
  9.6 3.1 %copy-start.2 = (f32[34,16,128]{2,1,0:T(8,128)}, f32[34,16,128]{2,1,0:T(8,128)S(1)}, u32[]{:S(2)}) copy-start(f32[34,16,128]{2,1,0:T(8,128)S(1)} %pad_maximum_fusion.1) | copy-start | bytes 835588
  9.7 7.1 %collective-permute-start.3 = (f32[66,8,128]{2,1,0:T(8,128)S(1)}, f32[66,8,128]{2,1,0:T(8,128)S(1)}, u32[]{:S(2)}, u32[]{:S(2)}) collective-permute-start(f32[66,8,128]{2,1,0:T(8,128)S(1)} %pad_maximum_fusion.3), channel_id=1, source_target_pairs={{56,0},{0,8},{8,16},{16,24},{24,32},{32,40},{40,48},{48,56},{57,1}... | collective-permute-start | bytes 811016 | tf_op jit(solution)/shard_map/ppermute | solution.py:688
  9.8 7.1 %collective-permute-start.2 = (f32[66,8,128]{2,1,0:T(8,128)S(1)}, f32[66,8,128]{2,1,0:T(8,128)S(1)}, u32[]{:S(2)}, u32[]{:S(2)}) collective-permute-start(f32[66,8,128]{2,1,0:T(8,128)S(1)} %pad_maximum_fusion.2), channel_id=1, source_target_pairs={{8,0},{16,8},{24,16},{32,24},{40,32},{48,40},{56,48},{0,56},{9,1},... | collective-permute-start | bytes 811016 | tf_op jit(solution)/shard_map/ppermute | solution.py:688
  12.7 4.2 %slice-start = ((f32[34,16,128]{2,1,0:T(8,128)}), f32[32,16,128]{2,1,0:T(8,128)S(1)}, s32[]{:S(2)}) async-start(f32[34,16,128]{2,1,0:T(8,128)} %copy-done.2), calls=%async_computation.1 | async-start | bytes 524288 | tf_op jit(solution)/shard_map/slice | solution.py:708
  12.7 4.2 %slice-start.1 = ((f32[17,16,128]{2,1,0:T(8,128)}), f32[1,16,128]{2,1,0:T(8,128)S(1)}, s32[]{:S(2)}) async-start(f32[17,16,128]{2,1,0:T(8,128)} %copy-done.3), calls=%async_computation.2 | async-start | bytes 16384 | tf_op jit(solution)/shard_map/slice | solution.py:709
  12.8 4.2 %slice-start.2 = ((f32[17,16,128]{2,1,0:T(8,128)}), f32[1,16,128]{2,1,0:T(8,128)S(1)}, s32[]{:S(2)}) async-start(f32[17,16,128]{2,1,0:T(8,128)} %copy-done.4), calls=%async_computation.3 | async-start | bytes 16384 | tf_op jit(solution)/shard_map/slice | solution.py:710
  17.6 4.9 %collective-permute-start.4 = (f32[5,32,128]{2,1,0:T(8,128)S(1)}, f32[5,32,128]{2,1,0:T(8,128)S(1)}, u32[]{:S(2)}, u32[]{:S(2)}) collective-permute-start(f32[5,32,128]{2,1,0:T(8,128)S(1)} %get-tuple-element.40), channel_id=1, source_target_pairs={{7,0},{0,1},{1,2},{2,3},{3,4},{4,5},{5,6},{6,7},{15,8},{8,9},{9,10... | collective-permute-start | bytes 245768 | tf_op jit(solution)/shard_map/ppermute | solution.py:688
  19.6 4.7 %collective-permute-start.5 = (f32[5,32,128]{2,1,0:T(8,128)S(1)}, f32[5,32,128]{2,1,0:T(8,128)S(1)}, u32[]{:S(2)}, u32[]{:S(2)}) collective-permute-start(f32[5,32,128]{2,1,0:T(8,128)S(1)} %get-tuple-element.41), channel_id=1, source_target_pairs={{1,0},{2,1},{3,2},{4,3},{5,4},{6,5},{7,6},{0,7},{9,8},{10,9},{11,1... | collective-permute-start | bytes 245768 | tf_op jit(solution)/shard_map/ppermute | solution.py:688
  31.8 7.2 %collective-permute-start.8 = (f32[5,4,16,128]{3,2,1,0:T(8,128)S(1)}, f32[5,4,16,128]{3,2,1,0:T(8,128)S(1)}, u32[]{:S(2)}, u32[]{:S(2)}) collective-permute-start(f32[5,4,16,128]{3,2,1,0:T(8,128)S(1)} %get-tuple-element.42.x0), channel_id=1, source_target_pairs={{192,0},{0,64},{64,128},{128,192},{193,1},{1,65},{65,129},{129,193... | collective-permute-start | bytes 491528 | tf_op jit(solution)/shard_map/ppermute | solution.py:688
  33.3 10.1 %collective-permute-start.7 = (f32[5,4,16,128]{3,2,1,0:T(8,128)S(1)}, f32[5,4,16,128]{3,2,1,0:T(8,128)S(1)}, u32[]{:S(2)}, u32[]{:S(2)}) collective-permute-start(f32[5,4,16,128]{3,2,1,0:T(8,128)S(1)} %get-tuple-element.42.x0), channel_id=1, source_target_pairs={{128,0},{192,64},{0,128},{64,192},{129,1},{193,65},{1,129},{65,193... | collective-permute-start | bytes 491528 | tf_op jit(solution)/shard_map/ppermute | solution.py:688
  36.3 7.2 %collective-permute-start.6 = (f32[5,4,16,128]{3,2,1,0:T(8,128)S(1)}, f32[5,4,16,128]{3,2,1,0:T(8,128)S(1)}, u32[]{:S(2)}, u32[]{:S(2)}) collective-permute-start(f32[5,4,16,128]{3,2,1,0:T(8,128)S(1)} %get-tuple-element.42.x0), channel_id=1, source_target_pairs={{64,0},{128,64},{192,128},{0,192},{65,1},{129,65},{193,129},{1,193... | collective-permute-start | bytes 491528 | tf_op jit(solution)/shard_map/ppermute | solution.py:688
  43.5 9.5 %collective-permute-start.9 = (f32[5,24,8,128]{3,2,1,0:T(8,128)S(1)}, f32[5,24,8,128]{3,2,1,0:T(8,128)S(1)}, u32[]{:S(2)}, u32[]{:S(2)}) collective-permute-start(f32[5,24,8,128]{3,2,1,0:T(8,128)S(1)} %get-tuple-element.43), channel_id=1, source_target_pairs={{56,0},{0,8},{8,16},{16,24},{24,32},{32,40},{40,48},{48,56},{57,1}... | collective-permute-start | bytes 1474568 | tf_op jit(solution)/shard_map/ppermute | solution.py:688
  43.5 9.5 %collective-permute-start.10 = (f32[5,24,8,128]{3,2,1,0:T(8,128)S(1)}, f32[5,24,8,128]{3,2,1,0:T(8,128)S(1)}, u32[]{:S(2)}, u32[]{:S(2)}) collective-permute-start(f32[5,24,8,128]{3,2,1,0:T(8,128)S(1)} %get-tuple-element.44), channel_id=1, source_target_pairs={{8,0},{16,8},{24,16},{32,24},{40,32},{48,40},{56,48},{0,56},{9,1},... | collective-permute-start | bytes 1474568 | tf_op jit(solution)/shard_map/ppermute | solution.py:688
  54.4 8.8 %collective-permute-start.11 = (f32[5,3,32,128]{3,2,1,0:T(8,128)S(1)}, f32[5,3,32,128]{3,2,1,0:T(8,128)S(1)}, u32[]{:S(2)}, u32[]{:S(2)}) collective-permute-start(f32[5,3,32,128]{3,2,1,0:T(8,128)S(1)} %get-tuple-element.46), channel_id=1, source_target_pairs={{7,0},{0,1},{1,2},{2,3},{3,4},{4,5},{5,6},{6,7},{15,8},{8,9},{9,10... | collective-permute-start | bytes 737288 | tf_op jit(solution)/shard_map/ppermute | solution.py:688
  57.7 9.0 %collective-permute-start.12 = (f32[5,3,32,128]{3,2,1,0:T(8,128)S(1)}, f32[5,3,32,128]{3,2,1,0:T(8,128)S(1)}, u32[]{:S(2)}, u32[]{:S(2)}) collective-permute-start(f32[5,3,32,128]{3,2,1,0:T(8,128)S(1)} %get-tuple-element.47), channel_id=1, source_target_pairs={{1,0},{2,1},{3,2},{4,3},{5,4},{6,5},{7,6},{0,7},{9,8},{10,9},{11,1... | collective-permute-start | bytes 737288 | tf_op jit(solution)/shard_map/ppermute | solution.py:688
  71.7 6.1 %collective-permute-start.15 = (f32[5,4,8,128]{3,2,1,0:T(8,128)S(1)}, f32[5,4,8,128]{3,2,1,0:T(8,128)S(1)}, u32[]{:S(2)}, u32[]{:S(2)}) collective-permute-start(f32[5,4,8,128]{3,2,1,0:T(8,128)S(1)} %get-tuple-element.50), channel_id=1, source_target_pairs={{48,0},{56,8},{0,16},{8,24},{16,32},{24,40},{32,48},{40,56},{49,1}... | collective-permute-start | bytes 245768 | tf_op jit(solution)/shard_map/ppermute | solution.py:688
  71.8 7.6 %collective-permute-start.14 = (f32[5,4,8,128]{3,2,1,0:T(8,128)S(1)}, f32[5,4,8,128]{3,2,1,0:T(8,128)S(1)}, u32[]{:S(2)}, u32[]{:S(2)}) collective-permute-start(f32[5,4,8,128]{3,2,1,0:T(8,128)S(1)} %get-tuple-element.49), channel_id=1, source_target_pairs={{32,0},{40,8},{48,16},{56,24},{0,32},{8,40},{16,48},{24,56},{33,1}... | collective-permute-start | bytes 245768 | tf_op jit(solution)/shard_map/ppermute | solution.py:688
  75.0 5.0 %collective-permute-start.13 = (f32[5,4,8,128]{3,2,1,0:T(8,128)S(1)}, f32[5,4,8,128]{3,2,1,0:T(8,128)S(1)}, u32[]{:S(2)}, u32[]{:S(2)}) collective-permute-start(f32[5,4,8,128]{3,2,1,0:T(8,128)S(1)} %get-tuple-element.49), channel_id=1, source_target_pairs={{16,0},{24,8},{32,16},{40,24},{48,32},{56,40},{0,48},{8,56},{17,1}... | collective-permute-start | bytes 245768 | tf_op jit(solution)/shard_map/ppermute | solution.py:688
  80.8 5.4 %collective-permute-start.16 = (f32[5,2,32,128]{3,2,1,0:T(8,128)S(1)}, f32[5,2,32,128]{3,2,1,0:T(8,128)S(1)}, u32[]{:S(2)}, u32[]{:S(2)}) collective-permute-start(f32[5,2,32,128]{3,2,1,0:T(8,128)S(1)} %get-tuple-element.52), channel_id=1, source_target_pairs={{7,0},{0,1},{1,2},{2,3},{3,4},{4,5},{5,6},{6,7},{15,8},{8,9},{9,10... | collective-permute-start | bytes 491528 | tf_op jit(solution)/shard_map/ppermute | solution.py:688
  82.6 5.3 %collective-permute-start.17 = (f32[5,2,32,128]{3,2,1,0:T(8,128)S(1)}, f32[5,2,32,128]{3,2,1,0:T(8,128)S(1)}, u32[]{:S(2)}, u32[]{:S(2)}) collective-permute-start(f32[5,2,32,128]{3,2,1,0:T(8,128)S(1)} %get-tuple-element.53), channel_id=1, source_target_pairs={{1,0},{2,1},{3,2},{4,3},{5,4},{6,5},{7,6},{0,7},{9,8},{10,9},{11,1... | collective-permute-start | bytes 491528 | tf_op jit(solution)/shard_map/ppermute | solution.py:688

commit v2 on v1

--- a/solution.py
+++ b/solution.py
@@ -11,7 +11,7 @@
 F32 = jnp.float32
 CSWEEPS = 32
 MIB = 1024 * 1024
-WIDE = 4
+NEAR, FULL = 8, 16
 
 
 def chebyshev_terms(sweep_count, lower_bound, upper_bound):
@@ -44,7 +44,13 @@
 
 
 def exact_dot(a, m):
-    return jnp.dot(a, m, precision=lax.Precision.HIGHEST, preferred_element_type=F32)
+    m = m.astype(jnp.bfloat16)
+    high = a.astype(jnp.bfloat16)
+    rest = a - high.astype(F32)
+    mid = rest.astype(jnp.bfloat16)
+    low = (rest - mid.astype(F32)).astype(jnp.bfloat16)
+    parts = [jnp.dot(p, m, preferred_element_type=F32) for p in (high, mid, low)]
+    return parts[0] + (parts[1] + parts[2])
 
 
 def signed(index, size, cut):
@@ -52,15 +58,17 @@
 
 
 def loop(lo, hi, unroll, body):
-    count = hi - lo
-    unroll = max(u for u in range(1, unroll * WIDE + 1) if count % u == 0)
+    rounds = (hi - lo) // unroll
 
     def step(t, carry):
         for u in range(unroll):
             body(lo + t * unroll + u)
         return carry
 
-    lax.fori_loop(0, count // unroll, step, 0)
+    if rounds:
+        lax.fori_loop(0, rounds, step, 0)
+    for i in range(lo + rounds * unroll, hi):
+        body(i)
 
 
 def copies_of(sources, targets, sems):
@@ -116,58 +124,120 @@
     return out
 
 
-def packx0(f_ref, b_ref, up_ref, down_ref, *sems):
-    pairs = (
-        (f_ref.at[8:16], up_ref.at[0:8]),
-        (b_ref.at[7:16], up_ref.at[8:17]),
-        (f_ref.at[0:8], down_ref.at[0:8]),
-        (b_ref.at[0:9], down_ref.at[8:17]),
-    )
-    moves = [pltpu.make_async_copy(a, b, s) for (a, b), s in zip(pairs, sems)]
-    for m in moves:
-        m.start()
-    for m in moves:
-        m.wait()
-
-
-def pack0(f_ref, b_ref, up_ref, down_ref):
-    for ref, start_f, start_b in ((up_ref, 120, 119), (down_ref, 0, 0)):
-        (tiles,) = z_pack(lambda p: (f_ref[p], 0), 32, 32, (start_f,), 8, 16)
-        for g, t in enumerate(tiles):
-            ref[g] = t
-        (tiles,) = z_pack(lambda p: (b_ref[p + 1], 0), 32, 32, (start_b,), 9, 14)
-        for g, t in enumerate(tiles):
-            ref[2 + g] = t
-
-
-def fine_down(
-    f_ref, b_ref, ylo_ref, yhi_ref, zlo_ref, zhi_ref,
-    u_far, cx_far, cy_far, cz_far, inv_far, rhs_far, diag_ref, xp_ref,
-    u_ref, cx_ref, cy_ref, cz_ref, inv_ref, rhs_ref,
-    bw, ew, va, vb, upd, cxw, dw, scr, *sems,
+def x_plane(own_ref, lo_ref, hi_ref, first, width, p):
+    if p < width:
+        return lo_ref, first + p
+    if p < width + 16:
+        return own_ref, p - width
+    return hi_ref, first + p - width - 16
+
+
+def f_plane(f_ref, lo_ref, hi_ref, p):
+    return x_plane(f_ref, lo_ref, hi_ref, 0, 8, p)
+
+
+def b_plane(b_ref, lo_ref, hi_ref, p):
+    return x_plane(b_ref, lo_ref, hi_ref, 8, 9, p)
+
+
+def packy0(f_ref, b_ref, lo_ref, hi_ref, up_ref, down_ref):
+    for p in range(32):
+        for at, (ref, q) in (
+            (p, f_plane(f_ref, lo_ref, hi_ref, p)),
+            (32 + p, b_plane(b_ref, lo_ref, hi_ref, p + 1)),
+        ):
+            up_ref[at] = ref[q, 8:16, :]
+            down_ref[at] = ref[q, 0:8, :]
+    row = iota((8, 128), 0)
+    for ref, edge in ((up_ref, 7), (down_ref, 8)):
+        for t in range(2):
+            acc = jnp.zeros((8, 128), F32)
+            for r in range(8):
+                line = jnp.broadcast_to(b_ref[8 * t + r, edge : edge + 1, :], (8, 128))
+                acc = jnp.where(row == r, line, acc)
+            ref[64 + t] = acc
+
+
+def pack0(
+    f_ref, b_ref, xlo_ref, xhi_ref, ylo_ref, yhi_ref, up_ref, down_ref, fw_ref, bw_ref
 ):
-    saves = copies_of(
-        (cx_ref, cy_ref, cz_ref, inv_ref, rhs_ref, u_ref),
-        (cx_far, cy_far, cz_far, inv_far, rhs_far, u_far),
-        sems,
-    )
+    for p in range(32):
+        ref, q = f_plane(f_ref, xlo_ref, xhi_ref, p)
+        fw_ref[p, 0:16, :] = ref[q]
+        fw_ref[p, 16:24, :] = yhi_ref[p]
+        fw_ref[p, 24:32, :] = ylo_ref[p]
+    for p in range(34):
+        ref, q = b_plane(b_ref, xlo_ref, xhi_ref, p)
+        bw_ref[p, 0:16, :] = ref[q]
+        if 0 < p < 33:
+            bw_ref[p, 16:24, :] = yhi_ref[31 + p]
+            bw_ref[p, 24:32, :] = ylo_ref[31 + p]
+        else:
+            bw_ref[p, 16:32, :] = ref[q]
+    ups, downs = z_pack(lambda p: (fw_ref[p], 0), 32, 32, (104, 0), 24, 5)
+    more = z_pack(lambda p: (bw_ref[p + 1], 0), 32, 32, (103, 0), 25, 5)
+    for g in range(7):
+        up_ref[g] = ups[g]
+        down_ref[g] = downs[g]
+        up_ref[7 + g] = more[0][g]
+        down_ref[7 + g] = more[1][g]
+
+
+def fold_lanes(scr, count, slots, xp_ref):
+    fine_lane = iota((256, 128), 0)
+    coarse_lane = iota((256, 128), 1)
+    both = jnp.where((fine_lane >> 1) == coarse_lane, 1.0, 0.0)
+    even = jnp.where(fine_lane == 2 * coarse_lane, 1.0, 0.0)
+    lane = iota((8, 128), 1)
+    half = lane < 64
+    for a, kind in enumerate(slots):
+        def rows_of(offset):
+            return jnp.concatenate(
+                [scr[a, t, pl.ds(offset, 128, stride=2), :] for t in range(2)], axis=1
+            )
+
+        folded = rows_of(0)
+        if kind != "y":
+            folded = folded + rows_of(1)
+        res = exact_dot(folded, even if kind == "z" else both)
+        for j in range(4):
+            for t in range(2):
+                lo = res[j * 16 + t * 8 : j * 16 + t * 8 + 8]
+                hi = res[(j + 4) * 16 + t * 8 : (j + 4) * 16 + t * 8 + 8]
+                xp_ref[a, j, t * 8 : t * 8 + 8, :] = jnp.where(half, lo, roll(hi, 64, 1))
+        for g in range(2):
+            for t in range(2):
+                acc = None
+                for q in range(4):
+                    at = (4 * g + q) * 16 + t * 8
+                    plane = res[at : at + 8]
+                    part = jnp.where(lane < 80, plane, roll(plane, -32, 1))
+                    part = roll(part, 32 * q - 64, 1)
+                    acc = part if acc is None else jnp.where(lane >= 32 * q, part, acc)
+                xp_ref[a, 4 + g, t * 8 : t * 8 + 8, :] = acc
+
+
+def put_lanes(scr, a, p, value):
+    scr[a, 0, p * 32 : p * 32 + 32, :] = value[:, 0:128]
+    scr[a, 1, p * 32 : p * 32 + 32, :] = value[:, 128:256]
+
+
+def fine_coef(
+    b_ref, ylo_ref, yhi_ref, zlo_ref, zhi_ref,
+    cx_ref, cy_ref, cz_ref, inv_ref, dw, xp_ref,
+    bw, ew, cxw, scr,
+):
     px, py, pz = lax.axis_index("gx"), lax.axis_index("gy"), lax.axis_index("gz")
     lane1 = iota((32, 128), 1)
     lane = iota((32, 256), 1)
     row = iota((32, 256), 0)
     for i in range(34):
         q = min(max(i - 1, 0), 31)
-        g, at = q // 14, (q % 14) * 9
-        right = roll(zhi_ref[2 + g], -at, 1)
-        left = roll(zlo_ref[2 + g], 119 - at, 1)
+        g, at = 7 + q // 5, (q % 5) * 25
+        right = roll(zhi_ref[g], -at, 1)
+        left = roll(zlo_ref[g], 103 - at, 1)
         bw[i, :, 0:128] = b_ref[i]
-        bw[i, :, 128:256] = jnp.where(lane1 < 9, right, jnp.where(lane1 >= 119, left, 1.0))
-    for i in range(32):
-        g, at = i // 16, (i % 16) * 8
-        right = roll(zhi_ref[g], -at, 1)
-        left = roll(zlo_ref[g], 120 - at, 1)
-        va[i, :, 0:128] = f_ref[i]
-        va[i, :, 128:256] = jnp.where(lane1 < 8, right, jnp.where(lane1 >= 120, left, 0.0))
+        bw[i, :, 128:256] = jnp.where(lane1 < 25, right, jnp.where(lane1 >= 103, left, 1.0))
     y_at = (16 * py + signed(row, 32, 24)) & 127
     z_at = (128 * pz + signed(lane, 256, 192)) & 1023
     y_open = jnp.where(y_at == 0, 0.0, 1.0)
@@ -182,7 +252,7 @@
         open_x = jnp.where(x_at(i) == 0, 0.0, 1.0).astype(F32)
         cxw[i] = open_x * harmonic(bw[i + 1], bw[i])
 
-    loop(0, 33, 1, face_x)
+    loop(0, 33, 3, face_x)
 
     def coefficients(i):
         b = bw[i + 1]
@@ -210,32 +280,55 @@
         inv_ref[i] = inv
         ew[i] = e
         dw[i] = d
-        g = va[i] * inv
-        rhs_ref[i] = g
-        first = FIRST * g
-        upd[i] = first
-        va[i] = first
 
     y_next = (16 * py + 24) & 127
     y_open_next = jnp.where(y_next == 0, 0.0, 1.0).astype(F32)
-    loop(0, 32, 2, coefficients)
-    for m in saves[:5]:
+    loop(0, 32, 4, coefficients)
+    for p in range(8):
+        i = 8 + 2 * p
+        put_lanes(scr, 0, p, 0.25 * cx_ref[i])
+        put_lanes(scr, 1, p, 0.25 * (cy_ref[i] + cy_ref[i + 1]))
+        put_lanes(scr, 2, p, 0.25 * (cz_ref[i] + cz_ref[i + 1]))
+        put_lanes(scr, 3, p, 0.25 * (ew[i] + ew[i + 1]))
+    fold_lanes(scr, 4, ("x", "y", "z", "e"), xp_ref)
+
+
+def fine_down(
+    f_ref, zlo_ref, zhi_ref, cx_ref, cy_ref, cz_ref, inv_ref, dw,
+    u_far, cx_far, cy_far, cz_far, inv_far, rhs_far, diag_ref, xp_ref,
+    u_ref, rhs_ref, va, vb, upd, scr, *sems,
+):
+    saves = copies_of(
+        (cx_ref, cy_ref, cz_ref, inv_ref, rhs_ref, u_ref),
+        (cx_far, cy_far, cz_far, inv_far, rhs_far, u_far),
+        sems,
+    )
+    for m in saves[:4]:
         m.start()
+    lane1 = iota((32, 128), 1)
+    for i in range(32):
+        g, at = i // 5, (i % 5) * 24
+        right = roll(zhi_ref[g], -at, 1)
+        left = roll(zlo_ref[g], 104 - at, 1)
+        halo = jnp.where(lane1 < 24, right, jnp.where(lane1 >= 104, left, 0.0))
+        for t, part in enumerate((f_ref[i], halo)):
+            at = slice(128 * t, 128 * t + 128)
+            scaled = part * inv_ref[i, :, at]
+            rhs_ref[i, :, at] = scaled
+            scaled = FIRST * scaled
+            upd[i, :, at] = scaled
+            va[i, :, at] = scaled
+    saves[4].start()
     level = Level(cx_ref, cy_ref, cz_ref, inv_ref, rhs_ref, 0)
-    sweep(level, va, vb, upd, 1, 31, 2, *TERMS[0])
-    sweep(level, vb, va, upd, 2, 30, 2, *TERMS[1])
-    sweep(level, va, u_ref, upd, 3, 29, 2, *TERMS[2], store_update=False)
+    sweep(level, va, vb, upd, 1, 31, NEAR, *TERMS[0])
+    sweep(level, vb, va, upd, 2, 30, NEAR, *TERMS[1])
+    sweep(level, va, u_ref, upd, 3, 29, NEAR, *TERMS[2], store_update=False)
     saves[5].start()
 
     def save_diag(i):
         diag_ref[i] = dw[i + 8, 0:16, 0:128]
 
     loop(0, 16, 4, save_diag)
-
-    def put(a, p, value):
-        scr[a, 0, p * 32 : p * 32 + 32, :] = value[:, 0:128]
-        scr[a, 1, p * 32 : p * 32 + 32, :] = value[:, 128:256]
-
     for p in range(8):
         i = 8 + 2 * p
         total = None
@@ -243,73 +336,41 @@
             _, d = level.defect(u_ref, k)
             r = dw[k] * d
             total = r if total is None else total + r
-        put(0, p, 0.125 * total)
-        put(1, p, 0.25 * cx_ref[i])
-        put(2, p, 0.25 * (cy_ref[i] + cy_ref[i + 1]))
-        put(3, p, 0.25 * (cz_ref[i] + cz_ref[i + 1]))
-        put(4, p, 0.25 * (ew[i] + ew[i + 1]))
-    fine_lane = iota((256, 128), 0)
-    coarse_lane = iota((256, 128), 1)
-    both = jnp.where((fine_lane >> 1) == coarse_lane, 1.0, 0.0)
-    even = jnp.where(fine_lane == 2 * coarse_lane, 1.0, 0.0)
-    half = iota((8, 128), 1) < 64
-    for a in range(5):
-        def rows_of(offset):
-            return jnp.concatenate(
-                [scr[a, t, pl.ds(offset, 128, stride=2), :] for t in range(2)], axis=1
-            )
-
-        folded = rows_of(0)
-        if a != 2:
-            folded = folded + rows_of(1)
-        res = exact_dot(folded, even if a == 3 else both)
-        for j in range(4):
-            for t in range(2):
-                lo = res[j * 16 + t * 8 : j * 16 + t * 8 + 8]
-                hi = res[(j + 4) * 16 + t * 8 : (j + 4) * 16 + t * 8 + 8]
-                xp_ref[a, j, t * 8 : t * 8 + 8, :] = jnp.where(half, lo, roll(hi, 64, 1))
+        put_lanes(scr, 0, p, 0.125 * total)
+    fold_lanes(scr, 1, ("f",), xp_ref)
     for m in saves:
         m.wait()
+
+
+TILES = 6
 
 
 def packy1(x0, x1, x2, x3, up_ref, down_ref):
     low = iota((8, 128), 0) < 4
     xs = (x0, x1, x2, x3)
-    for a in range(5):
-        for q in range(16):
-            own = xs[q // 4][a, q % 4, 0:8, :]
+    half = 2 * TILES
+    for a in range(x0.shape[0]):
+        for q in range(2 * half):
+            own = xs[q // TILES][a, q % TILES, 0:8, :]
             up_ref[a, q] = own
             down_ref[a, q] = own
-        for q in range(8):
-            one = xs[q // 4][a, q % 4, 8:16, :]
-            two = xs[2 + q // 4][a, q % 4, 8:16, :]
-            up_ref[a, 16 + q] = jnp.where(low, roll(one, 4, 0), two)
-            down_ref[a, 16 + q] = jnp.where(low, one, roll(two, 4, 0))
-
-
-def pack1(x0, x1, x2, x3, lo_ref, hi_ref, up_ref, down_ref, w_ref):
+        for q in range(half):
+            one = xs[q // TILES][a, q % TILES, 8:16, :]
+            two = xs[2 + q // TILES][a, q % TILES, 8:16, :]
+            up_ref[a, 2 * half + q] = jnp.where(low, roll(one, 4, 0), two)
+            down_ref[a, 2 * half + q] = jnp.where(low, one, roll(two, 4, 0))
+
+
+def unpack1(xs, lo_ref, hi_ref, a, q):
     low = iota((8, 128), 0) < 4
-    xs = (x0, x1, x2, x3)
-    for a in range(5):
-        for q in range(16):
-            right, left = hi_ref[a, 16 + q % 8], lo_ref[a, 16 + q % 8]
-            if q < 8:
-                edge = jnp.where(low, right, roll(left, 4, 0))
-            else:
-                edge = jnp.where(low, roll(right, 4, 0), left)
-            w_ref[a, q, 0:8, :] = xs[q // 4][a, q % 4, 0:8, :]
-            w_ref[a, q, 8:16, :] = hi_ref[a, q]
-            w_ref[a, q, 16:24, :] = edge
-            w_ref[a, q, 24:32, :] = lo_ref[a, q]
-
-        def get(p):
-            k, j = p // 8, p % 8
-            return w_ref[a, 4 * k + j % 4], 64 * (j // 4)
-
-        ups, downs = z_pack(get, 32, 32, (53, 0), 11, 11)
-        for g in range(3):
-            up_ref[a, g] = ups[g]
-            down_ref[a, g] = downs[g]
+    half = 2 * TILES
+    right, left = hi_ref[a, 2 * half + q % half], lo_ref[a, 2 * half + q % half]
+    if q < half:
+        edge = jnp.where(low, right, roll(left, 4, 0))
+    else:
+        edge = jnp.where(low, roll(right, 4, 0), left)
+    own = xs[q // TILES][a, q % TILES, 0:8, :]
+    return jnp.concatenate([own, hi_ref[a, q], edge, lo_ref[a, q]], axis=0)
 
 
 def pair_matrices(cut, size_in=128):
@@ -332,7 +393,7 @@
 
 
 def mid_down(
-    w_ref, zlo_ref, zhi_ref,
+    c0, c1, c2, c3, clo_ref, chi_ref, f0, f1, f2, f3, flo_ref, fhi_ref,
     u_far, cx_far, cy_far, cz_far, inv_far, rhs_far, own_ref, ym_ref, yp_ref,
     u_ref, cx_ref, cy_ref, cz_ref, inv_ref, rhs_ref,
     va, vb, upd, ew, dw, scr, *sems,
@@ -343,19 +404,21 @@
         sems,
     )
     lane = iota((32, 128), 1)
-    targets = (va, cx_ref, cy_ref, cz_ref, ew)
-    for a in range(5):
-        fill = 1.0 if a == 4 else 0.0
-        for p in range(32):
-            k, j = p // 8, p % 8
-            base = w_ref[a, 4 * k + j % 4]
-            if j >= 4:
-                base = roll(base, 64, 1)
-            g, at = p // 11, (p % 11) * 11
-            right = roll(zhi_ref[a, g], 64 - at, 1)
-            left = roll(zlo_ref[a, g], 117 - at, 1)
-            halo = jnp.where(lane < 75, right, jnp.where(lane >= 117, left, fill))
-            targets[a][p] = jnp.where(lane < 64, base, halo)
+    coarse = ((c0, c1, c2, c3), clo_ref, chi_ref)
+    pieces = [(cx_ref, 0.0) + coarse + (0,), (cy_ref, 0.0) + coarse + (1,)]
+    pieces += [(cz_ref, 0.0) + coarse + (2,), (ew, 1.0) + coarse + (3,)]
+    pieces += [(va, 0.0, (f0, f1, f2, f3), flo_ref, fhi_ref, 0)]
+    for target, fill, xs, lo_ref, hi_ref, a in pieces:
+        for k in range(4):
+            sides = [unpack1(xs, lo_ref, hi_ref, a, TILES * k + 4 + g) for g in range(2)]
+            for j in range(4):
+                base = unpack1(xs, lo_ref, hi_ref, a, TILES * k + j)
+                for g in range(2):
+                    own = roll(base, 64, 1) if g else base
+                    right = roll(sides[g], 64 - 32 * j, 1)
+                    left = roll(sides[g], 96 - 32 * j, 1)
+                    halo = jnp.where(lane < 80, right, jnp.where(lane >= 112, left, fill))
+                    target[8 * k + 4 * g + j] = jnp.where(lane < 64, own, halo)
 
     def coefficients(i):
         above = (i + 1) & 31
@@ -370,13 +433,13 @@
         upd[i] = first
         va[i] = first
 
-    loop(0, 32, 4, coefficients)
+    loop(0, 32, 8, coefficients)
     for m in saves[:5]:
         m.start()
     level = Level(cx_ref, cy_ref, cz_ref, inv_ref, rhs_ref, 32)
-    sweep(level, va, vb, upd, 0, 32, 4, *TERMS[0])
-    sweep(level, vb, va, upd, 0, 32, 4, *TERMS[1])
-    sweep(level, va, u_ref, upd, 0, 32, 4, *TERMS[2], store_update=False)
+    sweep(level, va, vb, upd, 0, 32, FULL, *TERMS[0])
+    sweep(level, vb, va, upd, 0, 32, FULL, *TERMS[1])
+    sweep(level, va, u_ref, upd, 0, 32, FULL, *TERMS[2], store_update=False)
     saves[5].start()
     for p in range(16):
         i = 2 * p
@@ -460,13 +523,13 @@
         upd[i] = first
         va[i] = first
 
-    loop(0, 16, 4, coefficients)
+    loop(0, 16, 8, coefficients)
     for m in saves[:5]:
         m.start()
     level = Level(cx_ref, cy_ref, cz_ref, inv_ref, rhs_ref, 16)
-    sweep(level, va, vb, upd, 0, 16, 4, *TERMS[0])
-    sweep(level, vb, va, upd, 0, 16, 4, *TERMS[1])
-    sweep(level, va, u_ref, upd, 0, 16, 4, *TERMS[2], store_update=False)
+    sweep(level, va, vb, upd, 0, 16, FULL, *TERMS[0])
+    sweep(level, vb, va, upd, 0, 16, FULL, *TERMS[1])
+    sweep(level, va, u_ref, upd, 0, 16, FULL, *TERMS[2], store_update=False)
     saves[5].start()
 
     def edge(i):
@@ -633,7 +696,7 @@
         p = i // 2
         va2[i] = u2[i] + wide[32 * p : 32 * p + 32]
     level = Level(cx2, cy2, cz2, inv2, rhs2, 16)
-    post(level, va2, vb2, upd2, [(0, 16)] * 4, 4)
+    post(level, va2, vb2, upd2, [(0, 16)] * 4, FULL)
     for m in loads[6:12]:
         m.wait()
     w2 = jnp.concatenate([va2[:, 0:8, :], va2[:, 24:32, :]], axis=1).reshape(256, 128)
@@ -642,7 +705,7 @@
         p = i // 2
         va1[i] = u1[i] + wide[32 * p : 32 * p + 32]
     level = Level(cx1, cy1, cz1, inv1, rhs1, 32)
-    post(level, va1, vb1, upd1, [(0, 32)] * 4, 4)
+    post(level, va1, vb1, upd1, [(0, 32)] * 4, FULL)
     for m in loads[12:]:
         m.wait()
     rows = [
@@ -654,14 +717,14 @@
         p = i // 2
         va0[i] = u0[i] + wide[32 * p : 32 * p + 32]
     level = Level(cx0, cy0, cz0, inv0, rhs0, 0)
-    post(level, va0, vb0, upd0, [(4, 28), (5, 27), (6, 26), (7, 25)], 2)
+    post(level, va0, vb0, upd0, [(4, 28), (5, 27), (6, 26), (7, 25)], NEAR)
 
     def finish(i):
         here, d = level.defect(va0, i)
         sol_ref[i - 8] = here[0:16, 0:128]
         res_ref[i - 8] = diag0[i - 8] * d[0:16, 0:128]
 
-    loop(8, 24, 2, finish)
+    loop(8, 24, NEAR, finish)
 
 
 def mix_rows(ref, i):
@@ -669,7 +732,7 @@
     return jnp.where(low, ref[i, 8:16, :], ref[i, 24:32, :])
 
 
-def call(body, args, outs, scratch=(), limit=16, far_in=(), far_out=(), copies=0):
+def call(body, args, outs, scratch=(), limit=16, far_in=(), far_out=(), copies=0, us=1):
     near, far = pl.BlockSpec(memory_space=pltpu.VMEM), pl.BlockSpec(memory_space=pltpu.HBM)
     return pl.pallas_call(
         body,
@@ -680,6 +743,9 @@
         + [pltpu.SemaphoreType.DMA] * copies,
         compiler_params=pltpu.CompilerParams(vmem_limit_bytes=limit * MIB),
         name=body.__name__,
+        cost_estimate=pl.CostEstimate(
+            flops=0, bytes_accessed=us * 3_000_000, transcendentals=0
+        ),
     )(*args)
 
 
@@ -690,49 +756,47 @@
 
 def local(source, conductivity):
     f, b = source, conductivity
-    to_hi, to_lo = call(
-        packx0, (f, b), [(17, 16, 128)] * 2, far_in=(0, 1), copies=4
-    )
-    from_lo, from_hi = move(to_hi, "gx", -1), move(to_lo, "gx", 1)
-    fx = jnp.concatenate([from_lo[:8], f, from_hi[:8]])
-    bx = jnp.concatenate([from_lo[8:], b, from_hi[8:]])
-
-    def y_slab(at, edge):
-        return jnp.concatenate(
-            [fx[:, at : at + 8], bx[1:33, at : at + 8], bx[9:25, edge].reshape(2, 8, 128)]
-        )
-
-    from_lo = move(y_slab(8, 7), "gy", -1)
-    from_hi = move(y_slab(0, 8), "gy", 1)
-    fw = jnp.concatenate([fx, from_hi[:32], from_lo[:32]], axis=1)
-    inner = jnp.concatenate([bx[1:33], from_hi[32:64], from_lo[32:64]], axis=1)
-    first = jnp.concatenate([bx[:1], bx[:1]], axis=1)
-    last = jnp.concatenate([bx[33:], bx[33:]], axis=1)
-    bw = jnp.concatenate([first, inner, last])
-    ylo, yhi = from_lo[64:].reshape(16, 128), from_hi[64:].reshape(16, 128)
-    up0, down0 = call(pack0, (fw, bw), [(5, 32, 128)] * 2)
-    zlo, zhi = move(up0, "gz", -1), move(down0, "gz", 1)
+    ends = lax.optimization_barrier(jnp.concatenate([f[8:16], b[7:16], f[0:8], b[0:9]]))
+    to_hi, to_lo = ends[:17], ends[17:]
+    xs = [move(to_hi, "gx", -1), move(to_lo, "gx", 1)]
+    to_hi, to_lo = call(packy0, [f, b] + xs, [(66, 8, 128)] * 2)
+    ys = [move(to_hi, "gy", -1), move(to_lo, "gy", 1)]
+    to_hi, to_lo, fw, bw = call(
+        pack0, [f, b] + xs + ys, [(14, 32, 128)] * 2 + [(32, 32, 128), (34, 32, 128)]
+    )
+    zs = [move(to_hi, "gz", -1), move(to_lo, "gz", 1)]
     big = (32, 32, 256)
-    u0, cx0, cy0, cz0, inv0, rhs0, diag0, xp = call(
+    cx0, cy0, cz0, inv0, d0, xpc = call(
+        fine_coef,
+        [bw] + [e[64:].reshape(16, 128) for e in ys] + zs,
+        [big] * 5 + [(4, TILES, 16, 128)],
+        [(34, 32, 256), big, (33, 32, 256), (4, 2, 256, 128)],
+        24,
+    )
+    u0, cx0, cy0, cz0, inv0, rhs0, diag0, xpf = call(
         fine_down,
-        (fw, bw, ylo, yhi, zlo, zhi),
-        [big] * 6 + [(16, 16, 128), (5, 4, 16, 128)],
-        [big] * 6 + [(34, 32, 256), big, big, big, big, (33, 32, 256), big, (5, 2, 256, 128)],
-        28,
+        [fw] + zs + [cx0, cy0, cz0, inv0, d0],
+        [big] * 6 + [(16, 16, 128), (1, TILES, 16, 128)],
+        [big] * 5 + [(1, 2, 256, 128)],
+        24,
         far_out=range(6),
         copies=6,
-    )
-    xs = [xp] + [move(xp, "gx", k) for k in (1, 2, 3)]
-    to_hi, to_lo = call(packy1, xs, [(5, 24, 8, 128)] * 2)
-    from_lo, from_hi = move(to_hi, "gy", -1), move(to_lo, "gy", 1)
-    up1, down1, w1 = call(
-        pack1, xs + [from_lo, from_hi], [(5, 3, 32, 128)] * 2 + [(5, 16, 32, 128)]
-    )
-    zlo, zhi = move(up1, "gz", -1), move(down1, "gz", 1)
+        us=20,
+    )
+
+    def along_x(xp):
+        return [xp] + [move(xp, "gx", k) for k in (1, 2, 3)]
+
+    def along_y(xs):
+        to_hi, to_lo = call(packy1, xs, [(xs[0].shape[0], 6 * TILES, 8, 128)] * 2)
+        return xs + [move(to_hi, "gy", -1), move(to_lo, "gy", 1)]
+
+    coarse, xpf = lax.optimization_barrier((along_x(xpc), xpf))
+    coarse, right_side = along_y(coarse), along_y(along_x(xpf))
     mid = (32, 32, 128)
     u1, cx1, cy1, cz1, inv1, rhs1, own2, ym, yp = call(
         mid_down,
-        (w1, zlo, zhi),
+        coarse + right_side,
         [mid] * 6 + [(5, 4, 16, 128), (5, 4, 8, 128), (5, 4, 8, 128)],
         [mid] * 11 + [(5, 512, 128)],
         far_out=range(6),

time: 121 us -> 116 us (0.959)
  Pallas kernels: 32.1 us -> 28 us
  starting transfers between devices: 27.2 us -> 25.1 us
  blocking collectives: 15.3 us -> 17.1 us
    pallas_call x9 -> x10, Pallas kernels: 32.1 us -> 28 us  [call(): pl.pallas_call(body, out_shape=[jax.ShapeDtypeStruct(s, F32) for s in out...]
    ppermute x18 -> x21, starting transfers between devices: 27.2 us -> 25.1 us  [move(): lax.ppermute(values, axis, [((i + shift) % size, i) for i in range(size)])]
    unnamed x10 -> x4, local copies, waits for them, and re-layouts: 1.81 us -> 0.01 us
    all_to_all x1, blocking collectives: 15.3 us -> 17.1 us  [local(): gathered = lax.all_to_all(everyone, 'gz', 0, 0)]
    ppermute x18 -> x21, waiting for transfers between devices: 42.1 us -> 43 us  [move(): lax.ppermute(values, axis, [((i + shift) % size, i) for i in range(size)])]
  transfers between devices with their start and end apart: 18 -> 21, of which waited for: 14 -> 16; matrix products, arithmetic and copies ran while one was open for 0% -> 0% of each run, Pallas kernels for 0% -> 4%
where the time goes in v2:
time: 116 us; the launch traced here: 115 us
  waiting for transfers between devices  43 us (37%)
  Pallas kernels  28 us (24%)
  starting transfers between devices  25.1 us (22%)
  blocking collectives  17.1 us (15%)
    ppermute x21, waiting for transfers between devices, move(): lax.ppermute(values, axis, [((i + shift) % size, i) for i in range(size)])  43 us
    pallas_call x10, Pallas kernels, call(): pl.pallas_call(body, out_shape=[jax.ShapeDtypeStruct(s, F32) for s in out...  28 us
    ppermute x21, starting transfers between devices, move(): lax.ppermute(values, axis, [((i + shift) % size, i) for i in range(size)])  25.1 us
    all_to_all x1, blocking collectives, local(): gathered = lax.all_to_all(everyone, 'gz', 0, 0)  17.1 us
  transfers between devices with their start and end apart: 21, of which 16 were waited for; matrix products, arithmetic and copies ran while one was open for 0% of the time, Pallas kernels for 4%

profile of v2, /device:TPU:32, one launch (start us, length us, event | category | flops | bytes accessed | tf_op | source)
XLA Modules:
  0.0 115.2 jit_solution(12487186423607201367)
XLA Ops:
  0.6 0.0 copy-start.1
  0.6 1.0 fusion.2
  1.6 0.0 copy-done.1
  1.7 0.0 copy-start
  1.7 1.6 %collective-permute-start = (f32[17,16,128]{2,1,0:T(8,128)S(1)}, f32[17,16,128]{2,1,0:T(8,128)S(1)}, u32[]{:S(2)}, u32[]{:S(2)}) collective-permute-start(f32[17,16,128]{2,1,0:T(8,128)S(1)} %get-tuple-element.99), channel_id=1, source_target_pairs={{192,0},{0,64},{64,128},{128,192},{193,1},{1,65},{65,129},{129,193... | collective-permute-start | bytes 417800 | tf_op jit(solution)/shard_map/ppermute | solution.py:754
  3.3 1.7 %collective-permute-start.1 = (f32[17,16,128]{2,1,0:T(8,128)S(1)}, f32[17,16,128]{2,1,0:T(8,128)S(1)}, u32[]{:S(2)}, u32[]{:S(2)}) collective-permute-start(f32[17,16,128]{2,1,0:T(8,128)S(1)} %get-tuple-element.98), channel_id=1, source_target_pairs={{64,0},{128,64},{192,128},{0,192},{65,1},{129,65},{193,129},{1,193... | collective-permute-start | bytes 417800 | tf_op jit(solution)/shard_map/ppermute | solution.py:754
  5.0 3.4 %collective-permute-done.lo_ref.xlo_ref = f32[17,16,128]{2,1,0:T(8,128)S(1)} collective-permute-done((f32[17,16,128]{2,1,0:T(8,128)S(1)}, f32[17,16,128]{2,1,0:T(8,128)S(1)}, u32[]{:S(2)}, u32[]{:S(2)}) %collective-permute-start) | collective-permute-done | bytes 139296 | tf_op jit(solution)/shard_map/ppermute | solution.py:754
  8.4 0.0 collective-permute-done.1.hi_ref.xhi_ref
  8.4 0.0 copy-done
  8.5 0.0 collective-permute-start.2
  8.5 2.9 %collective-permute-start.3 = (f32[66,8,128]{2,1,0:T(8,128)S(1)}, f32[66,8,128]{2,1,0:T(8,128)S(1)}, u32[]{:S(2)}, u32[]{:S(2)}) collective-permute-start(f32[66,8,128]{2,1,0:T(8,128)S(1)} %get-tuple-element.51), channel_id=1, source_target_pairs={{8,0},{16,8},{24,16},{32,24},{40,32},{48,40},{56,48},{0,56},{9,1},... | collective-permute-start | bytes 811016 | tf_op jit(solution)/shard_map/ppermute | solution.py:754
  11.4 4.1 %collective-permute-done.2.ylo_ref = f32[66,8,128]{2,1,0:T(8,128)S(1)} collective-permute-done((f32[66,8,128]{2,1,0:T(8,128)S(1)}, f32[66,8,128]{2,1,0:T(8,128)S(1)}, u32[]{:S(2)}, u32[]{:S(2)}) %collective-permute-start.2) | collective-permute-done | bytes 270368 | tf_op jit(solution)/shard_map/ppermute | solution.py:754
  15.6 0.0 collective-permute-done.3.yhi_ref
  15.6 0.6 pack0.1
  16.1 2.0 %collective-permute-start.4 = (f32[14,32,128]{2,1,0:T(8,128)S(1)}, f32[14,32,128]{2,1,0:T(8,128)S(1)}, u32[]{:S(2)}, u32[]{:S(2)}) collective-permute-start(f32[14,32,128]{2,1,0:T(8,128)S(1)} %get-tuple-element.53), channel_id=1, source_target_pairs={{7,0},{0,1},{1,2},{2,3},{3,4},{4,5},{5,6},{6,7},{15,8},{8,9},{9,10... | collective-permute-start | bytes 688136 | tf_op jit(solution)/shard_map/ppermute | solution.py:754
  18.1 0.1 collective-permute-start.5
  18.3 6.0 %collective-permute-done.4.zlo_ref = f32[14,32,128]{2,1,0:T(8,128)S(1)} collective-permute-done((f32[14,32,128]{2,1,0:T(8,128)S(1)}, f32[14,32,128]{2,1,0:T(8,128)S(1)}, u32[]{:S(2)}, u32[]{:S(2)}) %collective-permute-start.4) | collective-permute-done | bytes 229408 | tf_op jit(solution)/shard_map/ppermute | solution.py:754
  24.2 1.8 %collective-permute-done.5.zhi_ref = f32[14,32,128]{2,1,0:T(8,128)S(1)} collective-permute-done((f32[14,32,128]{2,1,0:T(8,128)S(1)}, f32[14,32,128]{2,1,0:T(8,128)S(1)}, u32[]{:S(2)}, u32[]{:S(2)}) %collective-permute-start.5) | collective-permute-done | bytes 229408 | tf_op jit(solution)/shard_map/ppermute | solution.py:754
  26.0 2.9 %fine_coef.1 = (f32[32,32,256]{2,1,0:T(8,128)S(1)}, f32[32,32,256]{2,1,0:T(8,128)S(1)}, f32[32,32,256]{2,1,0:T(8,128)S(1)}, f32[32,32,256]{2,1,0:T(8,128)S(1)}, ...) custom-call(f32[34,32,128]{2,1,0:T(8,128)S(1)} %get-tuple-element.52.b_ref, ...), custom_call_target="tpu_custom_call" | custom-call | bytes 3000000 | tf_op jit(solution)/shard_map/fine_coef/pallas_call | solution.py:737
  28.9 3.0 %collective-permute-start.6 = (f32[4,6,16,128]{3,2,1,0:T(8,128)S(1)}, f32[4,6,16,128]{3,2,1,0:T(8,128)S(1)}, u32[]{:S(2)}, u32[]{:S(2)}) collective-permute-start(f32[4,6,16,128]{3,2,1,0:T(8,128)S(1)} %get-tuple-element.63.x0.c0), channel_id=1, source_target_pairs={{64,0},{128,64},{192,128},{0,192},{65,1},{129,65},{193,129},{1,193... | collective-permute-start | bytes 589832 | tf_op jit(solution)/shard_map/ppermute | solution.py:754
  31.9 0.6 collective-permute-start.7
  32.5 0.6 collective-permute-start.8
  33.1 4.4 %fine_down.1 = (f32[32,32,256]{2,1,0:T(8,128)S(1)}, f32[32,32,256]{2,1,0:T(8,128)S(1)}, f32[32,32,256]{2,1,0:T(8,128)S(1)}, f32[32,32,256]{2,1,0:T(8,128)S(1)}, ...) custom-call(f32[32,32,128]{2,1,0:T(8,128)S(1)} %get-tuple-element.56, ...), custom_call_target="tpu_custom_call" | custom-call | bytes 60000000 | tf_op jit(solution)/shard_map/fine_down/pallas_call | solution.py:737
  37.5 2.5 %collective-permute-done.6.x1.c1 = f32[4,6,16,128]{3,2,1,0:T(8,128)S(1)} collective-permute-done((f32[4,6,16,128]{3,2,1,0:T(8,128)S(1)}, f32[4,6,16,128]{3,2,1,0:T(8,128)S(1)}, u32[]{:S(2)}, u32[]{:S(2)}) %collective-permute-start.6) | collective-permute-done | bytes 196640 | tf_op jit(solution)/shard_map/ppermute | solution.py:754
  40.0 1.3 %collective-permute-done.7.x2.c2 = f32[4,6,16,128]{3,2,1,0:T(8,128)S(1)} collective-permute-done((f32[4,6,16,128]{3,2,1,0:T(8,128)S(1)}, f32[4,6,16,128]{3,2,1,0:T(8,128)S(1)}, u32[]{:S(2)}, u32[]{:S(2)}) %collective-permute-start.7) | collective-permute-done | bytes 196640 | tf_op jit(solution)/shard_map/ppermute | solution.py:754
  41.3 2.4 %collective-permute-done.8.x3.c3 = f32[4,6,16,128]{3,2,1,0:T(8,128)S(1)} collective-permute-done((f32[4,6,16,128]{3,2,1,0:T(8,128)S(1)}, f32[4,6,16,128]{3,2,1,0:T(8,128)S(1)}, u32[]{:S(2)}, u32[]{:S(2)}) %collective-permute-start.8) | collective-permute-done | bytes 196640 | tf_op jit(solution)/shard_map/ppermute | solution.py:754
  43.7 0.1 packy1.2
  43.8 2.3 %collective-permute-start.10 = (f32[4,36,8,128]{3,2,1,0:T(8,128)S(1)}, f32[4,36,8,128]{3,2,1,0:T(8,128)S(1)}, u32[]{:S(2)}, u32[]{:S(2)}) collective-permute-start(f32[4,36,8,128]{3,2,1,0:T(8,128)S(1)} %get-tuple-element.68), channel_id=1, source_target_pairs={{8,0},{16,8},{24,16},{32,24},{40,32},{48,40},{56,48},{0,56},{9,1},... | collective-permute-start | bytes 1769480 | tf_op jit(solution)/shard_map/ppermute | solution.py:754
  46.1 0.0 collective-permute-start.9
  46.1 0.0 collective-permute-start.11
  46.1 0.6 collective-permute-start.12
  46.7 1.4 %collective-permute-start.13 = (f32[1,6,16,128]{3,2,1,0:T(8,128)S(1)}, f32[1,6,16,128]{3,2,1,0:T(8,128)S(1)}, u32[]{:S(2)}, u32[]{:S(2)}) collective-permute-start(f32[1,6,16,128]{3,2,1,0:T(8,128)S(1)} %get-tuple-element.69.x0.f0), channel_id=1, source_target_pairs={{192,0},{0,64},{64,128},{128,192},{193,1},{1,65},{65,129},{129,193... | collective-permute-start | bytes 147464 | tf_op jit(solution)/shard_map/ppermute | solution.py:754
  48.1 2.1 %collective-permute-done.11.x1.f1 = f32[1,6,16,128]{3,2,1,0:T(8,128)S(1)} collective-permute-done((f32[1,6,16,128]{3,2,1,0:T(8,128)S(1)}, f32[1,6,16,128]{3,2,1,0:T(8,128)S(1)}, u32[]{:S(2)}, u32[]{:S(2)}) %collective-permute-start.11) | collective-permute-done | bytes 49184 | tf_op jit(solution)/shard_map/ppermute | solution.py:754
  50.2 1.5 %collective-permute-done.12.x2.f2 = f32[1,6,16,128]{3,2,1,0:T(8,128)S(1)} collective-permute-done((f32[1,6,16,128]{3,2,1,0:T(8,128)S(1)}, f32[1,6,16,128]{3,2,1,0:T(8,128)S(1)}, u32[]{:S(2)}, u32[]{:S(2)}) %collective-permute-start.12) | collective-permute-done | bytes 49184 | tf_op jit(solution)/shard_map/ppermute | solution.py:754
  51.7 1.2 %collective-permute-done.13.x3.f3 = f32[1,6,16,128]{3,2,1,0:T(8,128)S(1)} collective-permute-done((f32[1,6,16,128]{3,2,1,0:T(8,128)S(1)}, f32[1,6,16,128]{3,2,1,0:T(8,128)S(1)}, u32[]{:S(2)}, u32[]{:S(2)}) %collective-permute-start.13) | collective-permute-done | bytes 49184 | tf_op jit(solution)/shard_map/ppermute | solution.py:754
  52.9 0.0 collective-permute-start.14
  52.9 2.9 %collective-permute-start.15 = (f32[1,36,8,128]{3,2,1,0:T(8,128)S(1)}, f32[1,36,8,128]{3,2,1,0:T(8,128)S(1)}, u32[]{:S(2)}, u32[]{:S(2)}) collective-permute-start(f32[1,36,8,128]{3,2,1,0:T(8,128)S(1)} %get-tuple-element.71), channel_id=1, source_target_pairs={{8,0},{16,8},{24,16},{32,24},{40,32},{48,40},{56,48},{0,56},{9,1},... | collective-permute-start | bytes 442376 | tf_op jit(solution)/shard_map/ppermute | solution.py:754
  55.9 2.8 %collective-permute-done.14.flo_ref = f32[1,36,8,128]{3,2,1,0:T(8,128)S(1)} collective-permute-done((f32[1,36,8,128]{3,2,1,0:T(8,128)S(1)}, f32[1,36,8,128]{3,2,1,0:T(8,128)S(1)}, u32[]{:S(2)}, u32[]{:S(2)}) %collective-permute-start.14) | collective-permute-done | bytes 147488 | tf_op jit(solution)/shard_map/ppermute | solution.py:754
  58.7 0.0 collective-permute-done.15.fhi_ref
  58.7 0.0 collective-permute-done.10.chi_ref
  58.7 0.0 collective-permute-done.9.clo_ref
  58.7 4.2 %mid_down.1 = (f32[32,32,128]{2,1,0:T(8,128)S(1)}, f32[32,32,128]{2,1,0:T(8,128)S(1)}, f32[32,32,128]{2,1,0:T(8,128)S(1)}, f32[32,32,128]{2,1,0:T(8,128)S(1)}, f...) custom-call(f32[4,6,16,128]{3,2,1,0:T(8,128)S(1)} %get-tuple-element, ...), custom_call_target="tpu_custom_call" | custom-call | bytes 3000000 | tf_op jit(solution)/shard_map/mid_down/pallas_call | solution.py:737
  62.9 0.3 collective-permute-start.16
  63.1 1.1 collective-permute-start.17
  64.2 0.8 collective-permute-start.18
  65.0 2.4 %collective-permute-done.16.hi_ref = f32[5,4,8,128]{3,2,1,0:T(8,128)S(1)} collective-permute-done((f32[5,4,8,128]{3,2,1,0:T(8,128)S(1)}, f32[5,4,8,128]{3,2,1,0:T(8,128)S(1)}, u32[]{:S(2)}, u32[]{:S(2)}) %collective-permute-start.16) | collective-permute-done | bytes 81952 | tf_op jit(solution)/shard_map/ppermute | solution.py:754
  67.4 1.7 %collective-permute-done.17.far_ref = f32[5,4,8,128]{3,2,1,0:T(8,128)S(1)} collective-permute-done((f32[5,4,8,128]{3,2,1,0:T(8,128)S(1)}, f32[5,4,8,128]{3,2,1,0:T(8,128)S(1)}, u32[]{:S(2)}, u32[]{:S(2)}) %collective-permute-start.17) | collective-permute-done | bytes 81952 | tf_op jit(solution)/shard_map/ppermute | solution.py:754
  69.1 2.0 %collective-permute-done.18.lo_ref = f32[5,4,8,128]{3,2,1,0:T(8,128)S(1)} collective-permute-done((f32[5,4,8,128]{3,2,1,0:T(8,128)S(1)}, f32[5,4,8,128]{3,2,1,0:T(8,128)S(1)}, u32[]{:S(2)}, u32[]{:S(2)}) %collective-permute-start.18) | collective-permute-done | bytes 81952 | tf_op jit(solution)/shard_map/ppermute | solution.py:754
  71.1 0.7 pack2.1
  71.8 3.1 %collective-permute-start.19 = (f32[5,2,32,128]{3,2,1,0:T(8,128)S(1)}, f32[5,2,32,128]{3,2,1,0:T(8,128)S(1)}, u32[]{:S(2)}, u32[]{:S(2)}) collective-permute-start(f32[5,2,32,128]{3,2,1,0:T(8,128)S(1)} %get-tuple-element.76), channel_id=1, source_target_pairs={{7,0},{0,1},{1,2},{2,3},{3,4},{4,5},{5,6},{6,7},{15,8},{8,9},{9,10... | collective-permute-start | bytes 491528 | tf_op jit(solution)/shard_map/ppermute | solution.py:754
  74.9 0.0 collective-permute-start.20
  74.9 4.2 %collective-permute-done.19.zlo_ref = f32[5,2,32,128]{3,2,1,0:T(8,128)S(1)} collective-permute-done((f32[5,2,32,128]{3,2,1,0:T(8,128)S(1)}, f32[5,2,32,128]{3,2,1,0:T(8,128)S(1)}, u32[]{:S(2)}, u32[]{:S(2)}) %collective-permute-start.19) | collective-permute-done | bytes 163872 | tf_op jit(solution)/shard_map/ppermute | solution.py:754
  79.1 3.7 %collective-permute-done.20.zhi_ref = f32[5,2,32,128]{3,2,1,0:T(8,128)S(1)} collective-permute-done((f32[5,2,32,128]{3,2,1,0:T(8,128)S(1)}, f32[5,2,32,128]{3,2,1,0:T(8,128)S(1)}, u32[]{:S(2)}, u32[]{:S(2)}) %collective-permute-start.20) | collective-permute-done | bytes 163872 | tf_op jit(solution)/shard_map/ppermute | solution.py:754
  82.8 2.6 %low_down.1 = (f32[16,32,128]{2,1,0:T(8,128)S(1)}, f32[16,32,128]{2,1,0:T(8,128)S(1)}, f32[16,32,128]{2,1,0:T(8,128)S(1)}, f32[16,32,128]{2,1,0:T(8,128)S(1)}, f...) custom-call(f32[5,4,32,128]{3,2,1,0:T(8,128)S(1)} %get-tuple-element.75.w_ref, ...), custom_call_target="tpu_custom_call" | custom-call | bytes 3000000 | tf_op jit(solution)/shard_map/low_down/pallas_call | solution.py:737
  85.4 17.1 %all_to_all.5.g_ref = f32[8,5,16,128]{3,2,1,0:T(8,128)S(1)} all-to-all(f32[8,5,16,128]{3,2,1,0:T(8,128)S(1)} %broadcast_in_dim.2), channel_id=1, replica_groups=mesh['gx'=4,'gy'=8,'gz'=8] {'gz'}, dimensions={0} | all-to-all | bytes 655360 | tf_op jit(solution)/shard_map/all_to_all | solution.py:820
  102.5 12.5 %up.1 = (f32[16,16,128]{2,1,0:T(8,128)}, f32[16,16,128]{2,1,0:T(8,128)}) custom-call(f32[8,5,16,128]{3,2,1,0:T(8,128)S(1)} %all_to_all.5.g_ref, f32[16,32,128]{2,1,0:T(8,128)S(1)} %get-tuple-element.79.refs_0_, f32[16,32,128]{2,1,0:T(8,128)S(1)} %get-tuple-element.80.refs_1_, f32[16,32,128]{2,1,0:T(8,128)S(1)} %get-tuple-element.81.refs_2_, ...), custom_call_target="tpu_custom_call" | custom-call | bytes 3000000 | tf_op jit(solution)/shard_map/up/pallas_call | solution.py:737
  (8 shorter events, 0.1 us)
Async XLA Ops:
  0.6 1.0 copy-start.1
  1.7 6.7 %copy-start = (f32[16,16,128]{2,1,0:T(8,128)S(1)}, f32[16,16,128]{2,1,0:T(8,128)}, u32[]{:S(2)}) copy-start(f32[16,16,128]{2,1,0:T(8,128)} %b_ref.3) | copy-start | bytes 393220
  1.7 6.7 %collective-permute-start = (f32[17,16,128]{2,1,0:T(8,128)S(1)}, f32[17,16,128]{2,1,0:T(8,128)S(1)}, u32[]{:S(2)}, u32[]{:S(2)}) collective-permute-start(f32[17,16,128]{2,1,0:T(8,128)S(1)} %get-tuple-element.99), channel_id=1, source_target_pairs={{192,0},{0,64},{64,128},{128,192},{193,1},{1,65},{65,129},{129,193... | collective-permute-start | bytes 417800 | tf_op jit(solution)/shard_map/ppermute | solution.py:754
  3.3 5.1 %collective-permute-start.1 = (f32[17,16,128]{2,1,0:T(8,128)S(1)}, f32[17,16,128]{2,1,0:T(8,128)S(1)}, u32[]{:S(2)}, u32[]{:S(2)}) collective-permute-start(f32[17,16,128]{2,1,0:T(8,128)S(1)} %get-tuple-element.98), channel_id=1, source_target_pairs={{64,0},{128,64},{192,128},{0,192},{65,1},{129,65},{193,129},{1,193... | collective-permute-start | bytes 417800 | tf_op jit(solution)/shard_map/ppermute | solution.py:754
  8.5 7.1 %collective-permute-start.2 = (f32[66,8,128]{2,1,0:T(8,128)S(1)}, f32[66,8,128]{2,1,0:T(8,128)S(1)}, u32[]{:S(2)}, u32[]{:S(2)}) collective-permute-start(f32[66,8,128]{2,1,0:T(8,128)S(1)} %get-tuple-element.50), channel_id=1, source_target_pairs={{56,0},{0,8},{8,16},{16,24},{24,32},{32,40},{40,48},{48,56},{57,1}... | collective-permute-start | bytes 811016 | tf_op jit(solution)/shard_map/ppermute | solution.py:754
  8.5 7.1 %collective-permute-start.3 = (f32[66,8,128]{2,1,0:T(8,128)S(1)}, f32[66,8,128]{2,1,0:T(8,128)S(1)}, u32[]{:S(2)}, u32[]{:S(2)}) collective-permute-start(f32[66,8,128]{2,1,0:T(8,128)S(1)} %get-tuple-element.51), channel_id=1, source_target_pairs={{8,0},{16,8},{24,16},{32,24},{40,32},{48,40},{56,48},{0,56},{9,1},... | collective-permute-start | bytes 811016 | tf_op jit(solution)/shard_map/ppermute | solution.py:754
  16.1 8.1 %collective-permute-start.4 = (f32[14,32,128]{2,1,0:T(8,128)S(1)}, f32[14,32,128]{2,1,0:T(8,128)S(1)}, u32[]{:S(2)}, u32[]{:S(2)}) collective-permute-start(f32[14,32,128]{2,1,0:T(8,128)S(1)} %get-tuple-element.53), channel_id=1, source_target_pairs={{7,0},{0,1},{1,2},{2,3},{3,4},{4,5},{5,6},{6,7},{15,8},{8,9},{9,10... | collective-permute-start | bytes 688136 | tf_op jit(solution)/shard_map/ppermute | solution.py:754
  18.1 7.9 %collective-permute-start.5 = (f32[14,32,128]{2,1,0:T(8,128)S(1)}, f32[14,32,128]{2,1,0:T(8,128)S(1)}, u32[]{:S(2)}, u32[]{:S(2)}) collective-permute-start(f32[14,32,128]{2,1,0:T(8,128)S(1)} %get-tuple-element.54), channel_id=1, source_target_pairs={{1,0},{2,1},{3,2},{4,3},{5,4},{6,5},{7,6},{0,7},{9,8},{10,9},{11,1... | collective-permute-start | bytes 688136 | tf_op jit(solution)/shard_map/ppermute | solution.py:754
  28.9 11.1 %collective-permute-start.6 = (f32[4,6,16,128]{3,2,1,0:T(8,128)S(1)}, f32[4,6,16,128]{3,2,1,0:T(8,128)S(1)}, u32[]{:S(2)}, u32[]{:S(2)}) collective-permute-start(f32[4,6,16,128]{3,2,1,0:T(8,128)S(1)} %get-tuple-element.63.x0.c0), channel_id=1, source_target_pairs={{64,0},{128,64},{192,128},{0,192},{65,1},{129,65},{193,129},{1,193... | collective-permute-start | bytes 589832 | tf_op jit(solution)/shard_map/ppermute | solution.py:754
  31.9 9.4 %collective-permute-start.7 = (f32[4,6,16,128]{3,2,1,0:T(8,128)S(1)}, f32[4,6,16,128]{3,2,1,0:T(8,128)S(1)}, u32[]{:S(2)}, u32[]{:S(2)}) collective-permute-start(f32[4,6,16,128]{3,2,1,0:T(8,128)S(1)} %get-tuple-element.63.x0.c0), channel_id=1, source_target_pairs={{128,0},{192,64},{0,128},{64,192},{129,1},{193,65},{1,129},{65,193... | collective-permute-start | bytes 589832 | tf_op jit(solution)/shard_map/ppermute | solution.py:754
  32.5 11.2 %collective-permute-start.8 = (f32[4,6,16,128]{3,2,1,0:T(8,128)S(1)}, f32[4,6,16,128]{3,2,1,0:T(8,128)S(1)}, u32[]{:S(2)}, u32[]{:S(2)}) collective-permute-start(f32[4,6,16,128]{3,2,1,0:T(8,128)S(1)} %get-tuple-element.63.x0.c0), channel_id=1, source_target_pairs={{192,0},{0,64},{64,128},{128,192},{193,1},{1,65},{65,129},{129,193... | collective-permute-start | bytes 589832 | tf_op jit(solution)/shard_map/ppermute | solution.py:754
  43.8 14.9 %collective-permute-start.10 = (f32[4,36,8,128]{3,2,1,0:T(8,128)S(1)}, f32[4,36,8,128]{3,2,1,0:T(8,128)S(1)}, u32[]{:S(2)}, u32[]{:S(2)}) collective-permute-start(f32[4,36,8,128]{3,2,1,0:T(8,128)S(1)} %get-tuple-element.68), channel_id=1, source_target_pairs={{8,0},{16,8},{24,16},{32,24},{40,32},{48,40},{56,48},{0,56},{9,1},... | collective-permute-start | bytes 1769480 | tf_op jit(solution)/shard_map/ppermute | solution.py:754
  46.1 12.6 %collective-permute-start.9 = (f32[4,36,8,128]{3,2,1,0:T(8,128)S(1)}, f32[4,36,8,128]{3,2,1,0:T(8,128)S(1)}, u32[]{:S(2)}, u32[]{:S(2)}) collective-permute-start(f32[4,36,8,128]{3,2,1,0:T(8,128)S(1)} %get-tuple-element.67), channel_id=1, source_target_pairs={{56,0},{0,8},{8,16},{16,24},{24,32},{32,40},{40,48},{48,56},{57,1}... | collective-permute-start | bytes 1769480 | tf_op jit(solution)/shard_map/ppermute | solution.py:754
  46.1 4.1 %collective-permute-start.11 = (f32[1,6,16,128]{3,2,1,0:T(8,128)S(1)}, f32[1,6,16,128]{3,2,1,0:T(8,128)S(1)}, u32[]{:S(2)}, u32[]{:S(2)}) collective-permute-start(f32[1,6,16,128]{3,2,1,0:T(8,128)S(1)} %get-tuple-element.69.x0.f0), channel_id=1, source_target_pairs={{64,0},{128,64},{192,128},{0,192},{65,1},{129,65},{193,129},{1,193... | collective-permute-start | bytes 147464 | tf_op jit(solution)/shard_map/ppermute | solution.py:754
  46.1 5.6 %collective-permute-start.12 = (f32[1,6,16,128]{3,2,1,0:T(8,128)S(1)}, f32[1,6,16,128]{3,2,1,0:T(8,128)S(1)}, u32[]{:S(2)}, u32[]{:S(2)}) collective-permute-start(f32[1,6,16,128]{3,2,1,0:T(8,128)S(1)} %get-tuple-element.69.x0.f0), channel_id=1, source_target_pairs={{128,0},{192,64},{0,128},{64,192},{129,1},{193,65},{1,129},{65,193... | collective-permute-start | bytes 147464 | tf_op jit(solution)/shard_map/ppermute | solution.py:754
  46.7 6.2 %collective-permute-start.13 = (f32[1,6,16,128]{3,2,1,0:T(8,128)S(1)}, f32[1,6,16,128]{3,2,1,0:T(8,128)S(1)}, u32[]{:S(2)}, u32[]{:S(2)}) collective-permute-start(f32[1,6,16,128]{3,2,1,0:T(8,128)S(1)} %get-tuple-element.69.x0.f0), channel_id=1, source_target_pairs={{192,0},{0,64},{64,128},{128,192},{193,1},{1,65},{65,129},{129,193... | collective-permute-start | bytes 147464 | tf_op jit(solution)/shard_map/ppermute | solution.py:754
  52.9 5.8 %collective-permute-start.14 = (f32[1,36,8,128]{3,2,1,0:T(8,128)S(1)}, f32[1,36,8,128]{3,2,1,0:T(8,128)S(1)}, u32[]{:S(2)}, u32[]{:S(2)}) collective-permute-start(f32[1,36,8,128]{3,2,1,0:T(8,128)S(1)} %get-tuple-element.70), channel_id=1, source_target_pairs={{56,0},{0,8},{8,16},{16,24},{24,32},{32,40},{40,48},{48,56},{57,1}... | collective-permute-start | bytes 442376 | tf_op jit(solution)/shard_map/ppermute | solution.py:754
  52.9 5.8 %collective-permute-start.15 = (f32[1,36,8,128]{3,2,1,0:T(8,128)S(1)}, f32[1,36,8,128]{3,2,1,0:T(8,128)S(1)}, u32[]{:S(2)}, u32[]{:S(2)}) collective-permute-start(f32[1,36,8,128]{3,2,1,0:T(8,128)S(1)} %get-tuple-element.71), channel_id=1, source_target_pairs={{8,0},{16,8},{24,16},{32,24},{40,32},{48,40},{56,48},{0,56},{9,1},... | collective-permute-start | bytes 442376 | tf_op jit(solution)/shard_map/ppermute | solution.py:754
  62.9 4.5 %collective-permute-start.16 = (f32[5,4,8,128]{3,2,1,0:T(8,128)S(1)}, f32[5,4,8,128]{3,2,1,0:T(8,128)S(1)}, u32[]{:S(2)}, u32[]{:S(2)}) collective-permute-start(f32[5,4,8,128]{3,2,1,0:T(8,128)S(1)} %get-tuple-element.73), channel_id=1, source_target_pairs={{16,0},{24,8},{32,16},{40,24},{48,32},{56,40},{0,48},{8,56},{17,1}... | collective-permute-start | bytes 245768 | tf_op jit(solution)/shard_map/ppermute | solution.py:754
  63.1 5.9 %collective-permute-start.17 = (f32[5,4,8,128]{3,2,1,0:T(8,128)S(1)}, f32[5,4,8,128]{3,2,1,0:T(8,128)S(1)}, u32[]{:S(2)}, u32[]{:S(2)}) collective-permute-start(f32[5,4,8,128]{3,2,1,0:T(8,128)S(1)} %get-tuple-element.73), channel_id=1, source_target_pairs={{32,0},{40,8},{48,16},{56,24},{0,32},{8,40},{16,48},{24,56},{33,1}... | collective-permute-start | bytes 245768 | tf_op jit(solution)/shard_map/ppermute | solution.py:754
  64.2 6.9 %collective-permute-start.18 = (f32[5,4,8,128]{3,2,1,0:T(8,128)S(1)}, f32[5,4,8,128]{3,2,1,0:T(8,128)S(1)}, u32[]{:S(2)}, u32[]{:S(2)}) collective-permute-start(f32[5,4,8,128]{3,2,1,0:T(8,128)S(1)} %get-tuple-element.74), channel_id=1, source_target_pairs={{48,0},{56,8},{0,16},{8,24},{16,32},{24,40},{32,48},{40,56},{49,1}... | collective-permute-start | bytes 245768 | tf_op jit(solution)/shard_map/ppermute | solution.py:754
  71.8 7.3 %collective-permute-start.19 = (f32[5,2,32,128]{3,2,1,0:T(8,128)S(1)}, f32[5,2,32,128]{3,2,1,0:T(8,128)S(1)}, u32[]{:S(2)}, u32[]{:S(2)}) collective-permute-start(f32[5,2,32,128]{3,2,1,0:T(8,128)S(1)} %get-tuple-element.76), channel_id=1, source_target_pairs={{7,0},{0,1},{1,2},{2,3},{3,4},{4,5},{5,6},{6,7},{15,8},{8,9},{9,10... | collective-permute-start | bytes 491528 | tf_op jit(solution)/shard_map/ppermute | solution.py:754
  74.9 7.9 %collective-permute-start.20 = (f32[5,2,32,128]{3,2,1,0:T(8,128)S(1)}, f32[5,2,32,128]{3,2,1,0:T(8,128)S(1)}, u32[]{:S(2)}, u32[]{:S(2)}) collective-permute-start(f32[5,2,32,128]{3,2,1,0:T(8,128)S(1)} %get-tuple-element.77), channel_id=1, source_target_pairs={{1,0},{2,1},{3,2},{4,3},{5,4},{6,5},{7,6},{0,7},{9,8},{10,9},{11,1... | collective-permute-start | bytes 491528 | tf_op jit(solution)/shard_map/ppermute | solution.py:754

commit v3 on v2

--- a/solution.py
+++ b/solution.py
@@ -11,7 +11,7 @@
 F32 = jnp.float32
 CSWEEPS = 32
 MIB = 1024 * 1024
-NEAR, FULL = 8, 16
+NEAR, FULL = 12, 32
 
 
 def chebyshev_terms(sweep_count, lower_bound, upper_bound):
@@ -183,30 +183,36 @@
         down_ref[7 + g] = more[1][g]
 
 
-def fold_lanes(scr, count, slots, xp_ref):
+def fine_matrices():
     fine_lane = iota((256, 128), 0)
     coarse_lane = iota((256, 128), 1)
     both = jnp.where((fine_lane >> 1) == coarse_lane, 1.0, 0.0)
     even = jnp.where(fine_lane == 2 * coarse_lane, 1.0, 0.0)
+    return both, even
+
+
+def folded_rows(scr, a, count, pairs):
+    def rows_of(offset):
+        return jnp.concatenate(
+            [scr[a, t, pl.ds(offset, count, stride=2), :] for t in range(2)], axis=1
+        )
+
+    return rows_of(0) + rows_of(1) if pairs else rows_of(0)
+
+
+def fold_lanes(scr, slots, xp_ref):
+    both, even = fine_matrices()
     lane = iota((8, 128), 1)
     half = lane < 64
     for a, kind in enumerate(slots):
-        def rows_of(offset):
-            return jnp.concatenate(
-                [scr[a, t, pl.ds(offset, 128, stride=2), :] for t in range(2)], axis=1
-            )
-
-        folded = rows_of(0)
-        if kind != "y":
-            folded = folded + rows_of(1)
-        res = exact_dot(folded, even if kind == "z" else both)
-        for j in range(4):
-            for t in range(2):
+        res = exact_dot(folded_rows(scr, a, 128, kind != "y"), even if kind == "z" else both)
+        for t in range(2):
+            rows = slice(t * 8, t * 8 + 8)
+            for j in range(4):
                 lo = res[j * 16 + t * 8 : j * 16 + t * 8 + 8]
                 hi = res[(j + 4) * 16 + t * 8 : (j + 4) * 16 + t * 8 + 8]
-                xp_ref[a, j, t * 8 : t * 8 + 8, :] = jnp.where(half, lo, roll(hi, 64, 1))
-        for g in range(2):
-            for t in range(2):
+                xp_ref[a * TILES + j, rows, :] = jnp.where(half, lo, roll(hi, 64, 1))
+            for g in range(2):
                 acc = None
                 for q in range(4):
                     at = (4 * g + q) * 16 + t * 8
@@ -214,7 +220,7 @@
                     part = jnp.where(lane < 80, plane, roll(plane, -32, 1))
                     part = roll(part, 32 * q - 64, 1)
                     acc = part if acc is None else jnp.where(lane >= 32 * q, part, acc)
-                xp_ref[a, 4 + g, t * 8 : t * 8 + 8, :] = acc
+                xp_ref[a * TILES + 4 + g, rows, :] = acc
 
 
 def put_lanes(scr, a, p, value):
@@ -225,7 +231,7 @@
 def fine_coef(
     b_ref, ylo_ref, yhi_ref, zlo_ref, zhi_ref,
     cx_ref, cy_ref, cz_ref, inv_ref, dw, xp_ref,
-    bw, ew, cxw, scr,
+    bw, cyw, czw, cxw, scr,
 ):
     px, py, pz = lax.axis_index("gx"), lax.axis_index("gy"), lax.axis_index("gz")
     lane1 = iota((32, 128), 1)
@@ -242,15 +248,14 @@
     z_at = (128 * pz + signed(lane, 256, 192)) & 1023
     y_open = jnp.where(y_at == 0, 0.0, 1.0)
     z_open = jnp.where(z_at == 0, 0.0, 1.0)
-    y_edge = jnp.where((y_at == 0) | (y_at == 127), 1.0, 0.0)
-    z_edge = jnp.where((z_at == 0) | (z_at == 1023), 1.0, 0.0)
-
-    def x_at(i):
-        return (16 * px + (i + 56)) & 63
+    y_low, y_high = (row == 0) & (py == 0), (row == 16) & (py == 7)
+    z_low, z_high = (lane == 0) & (pz == 0), (lane == 128) & (pz == 7)
 
     def face_x(i):
-        open_x = jnp.where(x_at(i) == 0, 0.0, 1.0).astype(F32)
-        cxw[i] = open_x * harmonic(bw[i + 1], bw[i])
+        here, below = bw[i + 1], bw[i]
+        inner = jnp.where((px == 0) & (i == 8), here, below)
+        outer = jnp.where((px == 3) & (i == 24), below, here)
+        cxw[i] = harmonic(outer, inner)
 
     loop(0, 33, 3, face_x)
 
@@ -262,35 +267,48 @@
         below = jnp.concatenate([below, below], axis=1)
         above = jnp.concatenate([above, above], axis=1)
         before = jnp.where(row == 24, jnp.broadcast_to(below, (32, 256)), roll(b, 1, 0))
-        cy = y_open * harmonic(b, before)
-        outer = harmonic(b[16:24], jnp.broadcast_to(above, (8, 256))) * y_open_next
+        cy = harmonic(jnp.where(y_high, before, b), jnp.where(y_low, b, before))
+        outer = harmonic(b[16:24], jnp.broadcast_to(above, (8, 256)))
         after = roll(cy, -1, 0)
         after = jnp.concatenate(
             [after[0:16], jnp.where(row[16:24] == 23, outer, after[16:24]), after[24:32]], axis=0
         )
-        cz = z_open * harmonic(b, roll(b, 1, 1))
-        own = harmonic(b, b)
-        x_edge = jnp.where((x_at(i) == 0) | (x_at(i) == 63), 1.0, 0.0).astype(F32)
-        e = own * (y_edge + z_edge + x_edge)
-        d = cxw[i] + cxw[i + 1] + (cy + after) + (cz + roll(cz, -1, 1)) + e
-        inv = 1.0 / d
-        cx_ref[i] = cxw[i]
-        cy_ref[i] = cy
-        cz_ref[i] = cz
-        inv_ref[i] = inv
-        ew[i] = e
+        before = roll(b, 1, 1)
+        cz = harmonic(jnp.where(z_high, before, b), jnp.where(z_low, b, before))
+        d = cxw[i] + cxw[i + 1] + (cy + after) + (cz + roll(cz, -1, 1))
+        x_open = jnp.where(((16 * px + i + 56) & 63) == 0, 0.0, 1.0).astype(F32)
+        cx_ref[i] = x_open * cxw[i]
+        cy_ref[i] = y_open * cy
+        cz_ref[i] = z_open * cz
+        cyw[i] = cy
+        czw[i] = cz
+        inv_ref[i] = 1.0 / d
         dw[i] = d
 
-    y_next = (16 * py + 24) & 127
-    y_open_next = jnp.where(y_next == 0, 0.0, 1.0).astype(F32)
     loop(0, 32, 4, coefficients)
     for p in range(8):
         i = 8 + 2 * p
-        put_lanes(scr, 0, p, 0.25 * cx_ref[i])
-        put_lanes(scr, 1, p, 0.25 * (cy_ref[i] + cy_ref[i + 1]))
-        put_lanes(scr, 2, p, 0.25 * (cz_ref[i] + cz_ref[i + 1]))
-        put_lanes(scr, 3, p, 0.25 * (ew[i] + ew[i + 1]))
-    fold_lanes(scr, 4, ("x", "y", "z", "e"), xp_ref)
+        put_lanes(scr, 0, p, 0.25 * cxw[i])
+        put_lanes(scr, 1, p, 0.25 * (cyw[i] + cyw[i + 1]))
+        put_lanes(scr, 2, p, 0.25 * (czw[i] + czw[i + 1]))
+    put_lanes(scr, 3, 0, 0.25 * cxw[24])
+
+    def beyond(i):
+        b = bw[i + 1]
+        far = jnp.where(py == 0, roll(b, 1, 0)[0:8], b[16:24])
+        return harmonic(far, far)
+
+    for p in range(8):
+        i = 8 + 2 * p
+        far = 0.25 * (beyond(i) + beyond(i + 1))
+        scr[3, 0, 32 + 8 * p : 40 + 8 * p, :] = far[:, 0:128]
+        scr[3, 1, 32 + 8 * p : 40 + 8 * p, :] = far[:, 128:256]
+    fold_lanes(scr, ("x", "y", "z"), xp_ref)
+    both, _ = fine_matrices()
+    xp_ref[3 * TILES] = exact_dot(folded_rows(scr, 3, 16, True), both)
+    far = jnp.concatenate([scr[3, t, pl.ds(32, 8, stride=8), :] for t in range(2)], axis=1)
+    xp_ref[3 * TILES + 1, 0:8, :] = exact_dot(far, both)
+    xp_ref[3 * TILES + 1, 8:16, :] = jnp.zeros((8, 128), F32)
 
 
 def fine_down(
@@ -337,7 +355,7 @@
             r = dw[k] * d
             total = r if total is None else total + r
         put_lanes(scr, 0, p, 0.125 * total)
-    fold_lanes(scr, 1, ("f",), xp_ref)
+    fold_lanes(scr, ("f",), xp_ref)
     for m in saves:
         m.wait()
 
@@ -348,29 +366,32 @@
 def packy1(x0, x1, x2, x3, up_ref, down_ref):
     low = iota((8, 128), 0) < 4
     xs = (x0, x1, x2, x3)
-    half = 2 * TILES
-    for a in range(x0.shape[0]):
-        for q in range(2 * half):
-            own = xs[q // TILES][a, q % TILES, 0:8, :]
-            up_ref[a, q] = own
-            down_ref[a, q] = own
-        for q in range(half):
-            one = xs[q // TILES][a, q % TILES, 8:16, :]
-            two = xs[2 + q // TILES][a, q % TILES, 8:16, :]
-            up_ref[a, 2 * half + q] = jnp.where(low, roll(one, 4, 0), two)
-            down_ref[a, 2 * half + q] = jnp.where(low, one, roll(two, 4, 0))
-
-
-def unpack1(xs, lo_ref, hi_ref, a, q):
-    low = iota((8, 128), 0) < 4
-    half = 2 * TILES
-    right, left = hi_ref[a, 2 * half + q % half], lo_ref[a, 2 * half + q % half]
+    tiles = up_ref.shape[0] // 6
+    half = 2 * tiles
+    for q in range(2 * half):
+        own = xs[q // tiles][q % tiles, 0:8, :]
+        up_ref[q] = own
+        down_ref[q] = own
+    for q in range(half):
+        one = xs[q // tiles][q % tiles, 8:16, :]
+        two = xs[2 + q // tiles][q % tiles, 8:16, :]
+        up_ref[2 * half + q] = jnp.where(low, roll(one, 4, 0), two)
+        down_ref[2 * half + q] = jnp.where(low, one, roll(two, 4, 0))
+
+
+def unpack1(xs, lo_ref, hi_ref, k, t, own_face=False):
+    row = iota((8, 128), 0)
+    tiles = hi_ref.shape[0] // 6
+    q, half = k * tiles + t, 2 * tiles
+    right, left = hi_ref[2 * half + q % half], lo_ref[2 * half + q % half]
     if q < half:
-        edge = jnp.where(low, right, roll(left, 4, 0))
+        edge = jnp.where(row < 4, right, roll(left, 4, 0))
     else:
-        edge = jnp.where(low, roll(right, 4, 0), left)
-    own = xs[q // TILES][a, q % TILES, 0:8, :]
-    return jnp.concatenate([own, hi_ref[a, q], edge, lo_ref[a, q]], axis=0)
+        edge = jnp.where(row < 4, roll(right, 4, 0), left)
+    after = hi_ref[q]
+    if own_face:
+        after = jnp.where(row == 0, xs[k][t, 8:16, :], after)
+    return jnp.concatenate([xs[k][t, 0:8, :], after, edge, lo_ref[q]], axis=0)
 
 
 def pair_matrices(cut, size_in=128):
@@ -382,9 +403,9 @@
     return both, even
 
 
-def restrict(scr, both, even, count):
+def restrict(scr, both, even, count, arrays=5):
     out = []
-    for a in range(5):
+    for a in range(arrays):
         folded = scr[a, pl.ds(0, count, stride=2), :]
         if a != 2:
             folded = folded + scr[a, pl.ds(1, count, stride=2), :]
@@ -396,7 +417,7 @@
     c0, c1, c2, c3, clo_ref, chi_ref, f0, f1, f2, f3, flo_ref, fhi_ref,
     u_far, cx_far, cy_far, cz_far, inv_far, rhs_far, own_ref, ym_ref, yp_ref,
     u_ref, cx_ref, cy_ref, cz_ref, inv_ref, rhs_ref,
-    va, vb, upd, ew, dw, scr, *sems,
+    va, vb, upd, dw, ux, uy, uz, hx, oth, scr, *sems,
 ):
     saves = copies_of(
         (cx_ref, cy_ref, cz_ref, inv_ref, rhs_ref, u_ref),
@@ -404,26 +425,46 @@
         sems,
     )
     lane = iota((32, 128), 1)
+    px, py, pz = lax.axis_index("gx"), lax.axis_index("gy"), lax.axis_index("gz")
+    row = iota((32, 128), 0)
     coarse = ((c0, c1, c2, c3), clo_ref, chi_ref)
-    pieces = [(cx_ref, 0.0) + coarse + (0,), (cy_ref, 0.0) + coarse + (1,)]
-    pieces += [(cz_ref, 0.0) + coarse + (2,), (ew, 1.0) + coarse + (3,)]
+    pieces = [(ux, 0.0) + coarse + (0,), (uy, 0.0) + coarse + (1,), (uz, 1.0) + coarse + (2,)]
     pieces += [(va, 0.0, (f0, f1, f2, f3), flo_ref, fhi_ref, 0)]
     for target, fill, xs, lo_ref, hi_ref, a in pieces:
+        face = target is uy
         for k in range(4):
-            sides = [unpack1(xs, lo_ref, hi_ref, a, TILES * k + 4 + g) for g in range(2)]
+            sides = [
+                unpack1(xs, lo_ref, hi_ref, k, TILES * a + 4 + g, face) for g in range(2)
+            ]
             for j in range(4):
-                base = unpack1(xs, lo_ref, hi_ref, a, TILES * k + j)
+                base = unpack1(xs, lo_ref, hi_ref, k, TILES * a + j, face)
                 for g in range(2):
                     own = roll(base, 64, 1) if g else base
                     right = roll(sides[g], 64 - 32 * j, 1)
                     left = roll(sides[g], 96 - 32 * j, 1)
                     halo = jnp.where(lane < 80, right, jnp.where(lane >= 112, left, fill))
                     target[8 * k + 4 * g + j] = jnp.where(lane < 64, own, halo)
+    high_x = None
+    for k in range(4):
+        part = unpack1(coarse[0], clo_ref, chi_ref, k, 3 * TILES)
+        high_x = part if high_x is None else jnp.where(px == 3 - k, part, high_x)
+    hx[...] = high_x
+    for k in range(4):
+        oth[8 * k : 8 * k + 8, :] = coarse[0][k][3 * TILES + 1, 0:8, :]
+    y_open = jnp.where(((8 * py + signed(row, 32, 20)) & 63) == 0, 0.0, 1.0)
+    z_open = jnp.where(((64 * pz + signed(lane, 128, 96)) & 511) == 0, 0.0, 1.0)
 
     def coefficients(i):
-        above = (i + 1) & 31
-        cy, cz = cy_ref[i], cz_ref[i]
-        d = cx_ref[i] + cx_ref[above] + (cy + roll(cy, -1, 0)) + (cz + roll(cz, -1, 1)) + ew[i]
+        x_at = (8 * px + i) & 31
+        cx, cy, cz = ux[i], uy[i], uz[i]
+        above = jnp.where(x_at == 31, hx[...], ux[(i + 1) & 31])
+        other = jnp.broadcast_to(oth[pl.ds(i, 1), :], (32, 128))
+        here = jnp.where((row == 8) & (py == 7), other, cy)
+        after = jnp.where((row == 31) & (py == 0), other, roll(cy, -1, 0))
+        d = cx + above + (here + after) + (cz + roll(cz, -1, 1))
+        cx_ref[i] = jnp.where(x_at == 0, 0.0, 1.0).astype(F32) * cx
+        cy_ref[i] = y_open * cy
+        cz_ref[i] = z_open * cz
         inv = 1.0 / d
         inv_ref[i] = inv
         dw[i] = d
@@ -447,17 +488,26 @@
         _, d1 = level.defect(u_ref, i + 1)
         at = slice(32 * p, 32 * p + 32)
         scr[0, at, :] = 0.03125 * (dw[i] * d0 + dw[i + 1] * d1)
-        scr[1, at, :] = 0.25 * cx_ref[i]
-        scr[2, at, :] = 0.25 * (cy_ref[i] + cy_ref[i + 1])
-        scr[3, at, :] = 0.25 * (cz_ref[i] + cz_ref[i + 1])
-        scr[4, at, :] = 0.25 * (ew[i] + ew[i + 1])
+        scr[1, at, :] = 0.25 * ux[i]
+        scr[2, at, :] = 0.25 * (uy[i] + uy[i + 1])
+        scr[3, at, :] = 0.25 * (uz[i] + uz[i + 1])
+    scr[4, 0:32, :] = 0.25 * hx[...]
     both, even = pair_matrices(96)
-    f, cx, cy, cz, e = [r.reshape(16, 16, 128) for r in restrict(scr, both, even, 256)]
-    cx_next = jnp.concatenate([cx[1:], cx[:1]], axis=0)
+    f, cx, cy, cz = [r.reshape(16, 16, 128) for r in restrict(scr, both, even, 256, 4)]
+    high_x = exact_dot(scr[4, pl.ds(0, 16, stride=2), :] + scr[4, pl.ds(1, 16, stride=2), :], both)
+    y_open = jnp.where(((4 * py + signed(row[:16], 16, 10)) & 31) == 0, 0.0, 1.0)
+    z_open = jnp.where(((32 * pz + signed(lane[:16], 128, 96)) & 255) == 0, 0.0, 1.0)
+    others = exact_dot(oth[pl.ds(0, 16, stride=2), :] + oth[pl.ds(1, 16, stride=2), :], both)
     planes = []
     for p in range(16):
-        d = cx[p] + cx_next[p] + (cy[p] + roll(cy[p], -1, 0)) + (cz[p] + roll(cz[p], -1, 1)) + e[p]
-        planes.append((f[p], cx[p], cy[p], cz[p], d))
+        x_at = (4 * px + p) & 15
+        other = jnp.broadcast_to(0.25 * others[p : p + 1], (16, 128))
+        here = jnp.where((row[:16] == 4) & (py == 7), other, cy[p])
+        after = jnp.where((row[:16] == 15) & (py == 0), other, roll(cy[p], -1, 0))
+        above = jnp.where(x_at == 15, high_x, cx[(p + 1) % 16])
+        d = cx[p] + above + (here + after) + (cz[p] + roll(cz[p], -1, 1))
+        x_open = jnp.where(x_at == 0, 0.0, 1.0).astype(F32)
+        planes.append((f[p], x_open * cx[p], y_open * cy[p], z_open * cz[p], d))
     lane8 = iota((16, 128), 1)
     row8 = iota((8, 128), 0)
     for a in range(5):
@@ -482,13 +532,13 @@
             w_ref[a, j, 16:24, :] = jnp.where(row < 5, far, lo)
             w_ref[a, j, 24:32, :] = jnp.where(row < 5, lo, own_ref[a, j, 8:16, :])
 
-        def get(p):
-            return w_ref[a, p % 4], 32 * (p // 4)
-
-        ups, downs = z_pack(get, 16, 32, (21, 0), 11, 11)
-        for g in range(2):
-            up_ref[a, g] = ups[g]
-            down_ref[a, g] = downs[g]
+    def get(p):
+        return w_ref[p // 16, p % 4], 32 * (p % 16 // 4)
+
+    ups, downs = z_pack(get, 80, 32, (21, 0), 11, 11)
+    for g in range(8):
+        up_ref[g] = ups[g]
+        down_ref[g] = downs[g]
 
 
 def low_down(
@@ -508,9 +558,9 @@
         fill = 1.0 if a == 4 else 0.0
         for p in range(16):
             base = roll(w_ref[a, p % 4], -32 * (p // 4), 1)
-            g, at = p // 11, (p % 11) * 11
-            right = roll(zhi_ref[a, g], 32 - at, 1)
-            left = roll(zlo_ref[a, g], 117 - at, 1)
+            g, at = (16 * a + p) // 11, (16 * a + p) % 11 * 11
+            right = roll(zhi_ref[g], 32 - at, 1)
+            left = roll(zlo_ref[g], 117 - at, 1)
             halo = jnp.where(lane < 43, right, jnp.where(lane >= 117, left, fill))
             targets[a][p] = jnp.where(lane < 32, base, halo)
 
@@ -769,14 +819,14 @@
     cx0, cy0, cz0, inv0, d0, xpc = call(
         fine_coef,
         [bw] + [e[64:].reshape(16, 128) for e in ys] + zs,
-        [big] * 5 + [(4, TILES, 16, 128)],
-        [(34, 32, 256), big, (33, 32, 256), (4, 2, 256, 128)],
+        [big] * 5 + [(3 * TILES + 2, 16, 128)],
+        [(34, 32, 256), big, big, (33, 32, 256), (4, 2, 256, 128)],
         24,
     )
     u0, cx0, cy0, cz0, inv0, rhs0, diag0, xpf = call(
         fine_down,
         [fw] + zs + [cx0, cy0, cz0, inv0, d0],
-        [big] * 6 + [(16, 16, 128), (1, TILES, 16, 128)],
+        [big] * 6 + [(16, 16, 128), (TILES, 16, 128)],
         [big] * 5 + [(1, 2, 256, 128)],
         24,
         far_out=range(6),
@@ -787,24 +837,24 @@
     def along_x(xp):
         return [xp] + [move(xp, "gx", k) for k in (1, 2, 3)]
 
-    def along_y(xs):
-        to_hi, to_lo = call(packy1, xs, [(xs[0].shape[0], 6 * TILES, 8, 128)] * 2)
+    def along_y(xs, tiles, us):
+        to_hi, to_lo = call(packy1, xs, [(6 * tiles, 8, 128)] * 2, us=us)
         return xs + [move(to_hi, "gy", -1), move(to_lo, "gy", 1)]
 
     coarse, xpf = lax.optimization_barrier((along_x(xpc), xpf))
-    coarse, right_side = along_y(coarse), along_y(along_x(xpf))
+    coarse, right_side = along_y(coarse, 3 * TILES + 1, 20), along_y(along_x(xpf), TILES, 1)
     mid = (32, 32, 128)
     u1, cx1, cy1, cz1, inv1, rhs1, own2, ym, yp = call(
         mid_down,
         coarse + right_side,
         [mid] * 6 + [(5, 4, 16, 128), (5, 4, 8, 128), (5, 4, 8, 128)],
-        [mid] * 11 + [(5, 512, 128)],
+        [mid] * 13 + [(32, 128), (32, 128), (5, 512, 128)],
         far_out=range(6),
         copies=6,
     )
     from_hi, from_lo, far = move(ym, "gy", 2), move(yp, "gy", -2), move(ym, "gy", 4)
     up2, down2, w2 = call(
-        pack2, (own2, from_hi, far, from_lo), [(5, 2, 32, 128)] * 2 + [(5, 4, 32, 128)]
+        pack2, (own2, from_hi, far, from_lo), [(8, 32, 128)] * 2 + [(5, 4, 32, 128)]
     )
     zlo, zhi = move(up2, "gz", -1), move(down2, "gz", 1)
     low = (16, 32, 128)

time: 116 us -> 112 us (0.966)
  Pallas kernels: 28 us -> 25.8 us
  waiting for transfers between devices: 43 us -> 41 us
    pallas_call x10, Pallas kernels: 28 us -> 25.8 us  [call(): pl.pallas_call(body, out_shape=[jax.ShapeDtypeStruct(s, F32) for s in out...]
    ppermute x21, waiting for transfers between devices: 43 us -> 41 us  [move(): lax.ppermute(values, axis, [((i + shift) % size, i) for i in range(size)])]
where the time goes in v3:
time: 112 us; the launch traced here: 111 us
  waiting for transfers between devices  41 us (37%)
  Pallas kernels  25.8 us (23%)
  starting transfers between devices  25.1 us (22%)
  blocking collectives  17.1 us (15%)
    ppermute x21, waiting for transfers between devices, move(): lax.ppermute(values, axis, [((i + shift) % size, i) for i in range(size)])  41 us
    pallas_call x10, Pallas kernels, call(): pl.pallas_call(body, out_shape=[jax.ShapeDtypeStruct(s, F32) for s in out...  25.8 us
    ppermute x21, starting transfers between devices, move(): lax.ppermute(values, axis, [((i + shift) % size, i) for i in range(size)])  25.1 us
    all_to_all x1, blocking collectives, local(): gathered = lax.all_to_all(everyone, 'gz', 0, 0)  17.1 us
  transfers between devices with their start and end apart: 21, of which 16 were waited for; matrix products, arithmetic and copies ran while one was open for 0% of the time, Pallas kernels for 4%

profile of v3, /device:TPU:32, one launch (start us, length us, event | category | flops | bytes accessed | tf_op | source)
XLA Modules:
  0.0 110.9 jit_solution(1306284916043585675)
XLA Ops:
  0.6 0.0 copy-start.1
  0.6 1.0 fusion.2
  1.6 0.0 copy-done.1
  1.7 0.0 copy-start
  1.7 1.6 %collective-permute-start = (f32[17,16,128]{2,1,0:T(8,128)S(1)}, f32[17,16,128]{2,1,0:T(8,128)S(1)}, u32[]{:S(2)}, u32[]{:S(2)}) collective-permute-start(f32[17,16,128]{2,1,0:T(8,128)S(1)} %get-tuple-element.99), channel_id=1, source_target_pairs={{192,0},{0,64},{64,128},{128,192},{193,1},{1,65},{65,129},{129,193... | collective-permute-start | bytes 417800 | tf_op jit(solution)/shard_map/ppermute | solution.py:804
  3.3 1.7 %collective-permute-start.1 = (f32[17,16,128]{2,1,0:T(8,128)S(1)}, f32[17,16,128]{2,1,0:T(8,128)S(1)}, u32[]{:S(2)}, u32[]{:S(2)}) collective-permute-start(f32[17,16,128]{2,1,0:T(8,128)S(1)} %get-tuple-element.98), channel_id=1, source_target_pairs={{64,0},{128,64},{192,128},{0,192},{65,1},{129,65},{193,129},{1,193... | collective-permute-start | bytes 417800 | tf_op jit(solution)/shard_map/ppermute | solution.py:804
  5.0 3.4 %collective-permute-done.lo_ref.xlo_ref = f32[17,16,128]{2,1,0:T(8,128)S(1)} collective-permute-done((f32[17,16,128]{2,1,0:T(8,128)S(1)}, f32[17,16,128]{2,1,0:T(8,128)S(1)}, u32[]{:S(2)}, u32[]{:S(2)}) %collective-permute-start) | collective-permute-done | bytes 139296 | tf_op jit(solution)/shard_map/ppermute | solution.py:804
  8.4 0.0 collective-permute-done.1.hi_ref.xhi_ref
  8.4 0.0 copy-done
  8.5 0.0 collective-permute-start.2
  8.5 2.9 %collective-permute-start.3 = (f32[66,8,128]{2,1,0:T(8,128)S(1)}, f32[66,8,128]{2,1,0:T(8,128)S(1)}, u32[]{:S(2)}, u32[]{:S(2)}) collective-permute-start(f32[66,8,128]{2,1,0:T(8,128)S(1)} %get-tuple-element.51), channel_id=1, source_target_pairs={{8,0},{16,8},{24,16},{32,24},{40,32},{48,40},{56,48},{0,56},{9,1},... | collective-permute-start | bytes 811016 | tf_op jit(solution)/shard_map/ppermute | solution.py:804
  11.4 4.1 %collective-permute-done.2.ylo_ref = f32[66,8,128]{2,1,0:T(8,128)S(1)} collective-permute-done((f32[66,8,128]{2,1,0:T(8,128)S(1)}, f32[66,8,128]{2,1,0:T(8,128)S(1)}, u32[]{:S(2)}, u32[]{:S(2)}) %collective-permute-start.2) | collective-permute-done | bytes 270368 | tf_op jit(solution)/shard_map/ppermute | solution.py:804
  15.6 0.0 collective-permute-done.3.yhi_ref
  15.6 0.6 pack0.1
  16.1 2.0 %collective-permute-start.4 = (f32[14,32,128]{2,1,0:T(8,128)S(1)}, f32[14,32,128]{2,1,0:T(8,128)S(1)}, u32[]{:S(2)}, u32[]{:S(2)}) collective-permute-start(f32[14,32,128]{2,1,0:T(8,128)S(1)} %get-tuple-element.53), channel_id=1, source_target_pairs={{7,0},{0,1},{1,2},{2,3},{3,4},{4,5},{5,6},{6,7},{15,8},{8,9},{9,10... | collective-permute-start | bytes 688136 | tf_op jit(solution)/shard_map/ppermute | solution.py:804
  18.1 0.1 collective-permute-start.5
  18.3 6.0 %collective-permute-done.4.zlo_ref = f32[14,32,128]{2,1,0:T(8,128)S(1)} collective-permute-done((f32[14,32,128]{2,1,0:T(8,128)S(1)}, f32[14,32,128]{2,1,0:T(8,128)S(1)}, u32[]{:S(2)}, u32[]{:S(2)}) %collective-permute-start.4) | collective-permute-done | bytes 229408 | tf_op jit(solution)/shard_map/ppermute | solution.py:804
  24.2 1.8 %collective-permute-done.5.zhi_ref = f32[14,32,128]{2,1,0:T(8,128)S(1)} collective-permute-done((f32[14,32,128]{2,1,0:T(8,128)S(1)}, f32[14,32,128]{2,1,0:T(8,128)S(1)}, u32[]{:S(2)}, u32[]{:S(2)}) %collective-permute-start.5) | collective-permute-done | bytes 229408 | tf_op jit(solution)/shard_map/ppermute | solution.py:804
  26.0 2.8 %fine_coef.1 = (f32[32,32,256]{2,1,0:T(8,128)S(1)}, f32[32,32,256]{2,1,0:T(8,128)S(1)}, f32[32,32,256]{2,1,0:T(8,128)S(1)}, f32[32,32,256]{2,1,0:T(8,128)S(1)}, ...) custom-call(f32[34,32,128]{2,1,0:T(8,128)S(1)} %get-tuple-element.52.b_ref, ...), custom_call_target="tpu_custom_call" | custom-call | bytes 3000000 | tf_op jit(solution)/shard_map/fine_coef/pallas_call | solution.py:787
  28.8 3.0 %collective-permute-start.6 = (f32[20,16,128]{2,1,0:T(8,128)S(1)}, f32[20,16,128]{2,1,0:T(8,128)S(1)}, u32[]{:S(2)}, u32[]{:S(2)}) collective-permute-start(f32[20,16,128]{2,1,0:T(8,128)S(1)} %get-tuple-element.63.x0.c0), channel_id=1, source_target_pairs={{64,0},{128,64},{192,128},{0,192},{65,1},{129,65},{193,129},{1,193... | collective-permute-start | bytes 491528 | tf_op jit(solution)/shard_map/ppermute | solution.py:804
  31.8 0.6 collective-permute-start.7
  32.4 0.6 collective-permute-start.8
  33.0 4.3 %fine_down.1 = (f32[32,32,256]{2,1,0:T(8,128)S(1)}, f32[32,32,256]{2,1,0:T(8,128)S(1)}, f32[32,32,256]{2,1,0:T(8,128)S(1)}, f32[32,32,256]{2,1,0:T(8,128)S(1)}, ...) custom-call(f32[32,32,128]{2,1,0:T(8,128)S(1)} %get-tuple-element.56, ...), custom_call_target="tpu_custom_call" | custom-call | bytes 60000000 | tf_op jit(solution)/shard_map/fine_down/pallas_call | solution.py:787
  37.4 1.2 %collective-permute-done.6.x1.c1 = f32[20,16,128]{2,1,0:T(8,128)S(1)} collective-permute-done((f32[20,16,128]{2,1,0:T(8,128)S(1)}, f32[20,16,128]{2,1,0:T(8,128)S(1)}, u32[]{:S(2)}, u32[]{:S(2)}) %collective-permute-start.6) | collective-permute-done | bytes 163872 | tf_op jit(solution)/shard_map/ppermute | solution.py:804
  38.5 1.9 %collective-permute-done.7.x2.c2 = f32[20,16,128]{2,1,0:T(8,128)S(1)} collective-permute-done((f32[20,16,128]{2,1,0:T(8,128)S(1)}, f32[20,16,128]{2,1,0:T(8,128)S(1)}, u32[]{:S(2)}, u32[]{:S(2)}) %collective-permute-start.7) | collective-permute-done | bytes 163872 | tf_op jit(solution)/shard_map/ppermute | solution.py:804
  40.5 1.8 %collective-permute-done.8.x3.c3 = f32[20,16,128]{2,1,0:T(8,128)S(1)} collective-permute-done((f32[20,16,128]{2,1,0:T(8,128)S(1)}, f32[20,16,128]{2,1,0:T(8,128)S(1)}, u32[]{:S(2)}, u32[]{:S(2)}) %collective-permute-start.8) | collective-permute-done | bytes 163872 | tf_op jit(solution)/shard_map/ppermute | solution.py:804
  42.3 0.1 packy1.2
  42.3 2.3 %collective-permute-start.10 = (f32[114,8,128]{2,1,0:T(8,128)S(1)}, f32[114,8,128]{2,1,0:T(8,128)S(1)}, u32[]{:S(2)}, u32[]{:S(2)}) collective-permute-start(f32[114,8,128]{2,1,0:T(8,128)S(1)} %get-tuple-element.68), channel_id=1, source_target_pairs={{8,0},{16,8},{24,16},{32,24},{40,32},{48,40},{56,48},{0,56},{9,1},... | collective-permute-start | bytes 1400840 | tf_op jit(solution)/shard_map/ppermute | solution.py:804
  44.6 0.0 collective-permute-start.9
  44.6 0.0 collective-permute-start.11
  44.6 0.6 collective-permute-start.12
  45.2 1.4 %collective-permute-start.13 = (f32[6,16,128]{2,1,0:T(8,128)S(1)}, f32[6,16,128]{2,1,0:T(8,128)S(1)}, u32[]{:S(2)}, u32[]{:S(2)}) collective-permute-start(f32[6,16,128]{2,1,0:T(8,128)S(1)} %get-tuple-element.69.x0.f0), channel_id=1, source_target_pairs={{192,0},{0,64},{64,128},{128,192},{193,1},{1,65},{65,129},{129,193... | collective-permute-start | bytes 147464 | tf_op jit(solution)/shard_map/ppermute | solution.py:804
  46.6 2.1 %collective-permute-done.11.x1.f1 = f32[6,16,128]{2,1,0:T(8,128)S(1)} collective-permute-done((f32[6,16,128]{2,1,0:T(8,128)S(1)}, f32[6,16,128]{2,1,0:T(8,128)S(1)}, u32[]{:S(2)}, u32[]{:S(2)}) %collective-permute-start.11) | collective-permute-done | bytes 49184 | tf_op jit(solution)/shard_map/ppermute | solution.py:804
  48.7 1.5 %collective-permute-done.12.x2.f2 = f32[6,16,128]{2,1,0:T(8,128)S(1)} collective-permute-done((f32[6,16,128]{2,1,0:T(8,128)S(1)}, f32[6,16,128]{2,1,0:T(8,128)S(1)}, u32[]{:S(2)}, u32[]{:S(2)}) %collective-permute-start.12) | collective-permute-done | bytes 49184 | tf_op jit(solution)/shard_map/ppermute | solution.py:804
  50.2 1.2 %collective-permute-done.13.x3.f3 = f32[6,16,128]{2,1,0:T(8,128)S(1)} collective-permute-done((f32[6,16,128]{2,1,0:T(8,128)S(1)}, f32[6,16,128]{2,1,0:T(8,128)S(1)}, u32[]{:S(2)}, u32[]{:S(2)}) %collective-permute-start.13) | collective-permute-done | bytes 49184 | tf_op jit(solution)/shard_map/ppermute | solution.py:804
  51.4 0.0 collective-permute-start.14
  51.4 2.9 %collective-permute-start.15 = (f32[36,8,128]{2,1,0:T(8,128)S(1)}, f32[36,8,128]{2,1,0:T(8,128)S(1)}, u32[]{:S(2)}, u32[]{:S(2)}) collective-permute-start(f32[36,8,128]{2,1,0:T(8,128)S(1)} %get-tuple-element.71), channel_id=1, source_target_pairs={{8,0},{16,8},{24,16},{32,24},{40,32},{48,40},{56,48},{0,56},{9,1},... | collective-permute-start | bytes 442376 | tf_op jit(solution)/shard_map/ppermute | solution.py:804
  54.4 2.8 %collective-permute-done.14.flo_ref = f32[36,8,128]{2,1,0:T(8,128)S(1)} collective-permute-done((f32[36,8,128]{2,1,0:T(8,128)S(1)}, f32[36,8,128]{2,1,0:T(8,128)S(1)}, u32[]{:S(2)}, u32[]{:S(2)}) %collective-permute-start.14) | collective-permute-done | bytes 147488 | tf_op jit(solution)/shard_map/ppermute | solution.py:804
  57.2 0.0 collective-permute-done.15.fhi_ref
  57.2 0.0 collective-permute-done.10.chi_ref
  57.2 0.0 collective-permute-done.9.clo_ref
  57.2 3.7 %mid_down.1 = (f32[32,32,128]{2,1,0:T(8,128)S(1)}, f32[32,32,128]{2,1,0:T(8,128)S(1)}, f32[32,32,128]{2,1,0:T(8,128)S(1)}, f32[32,32,128]{2,1,0:T(8,128)S(1)}, f...) custom-call(f32[20,16,128]{2,1,0:T(8,128)S(1)} %get-tuple-element.63, ...), custom_call_target="tpu_custom_call" | custom-call | bytes 3000000 | tf_op jit(solution)/shard_map/mid_down/pallas_call | solution.py:787
  60.9 0.3 collective-permute-start.16
  61.2 1.1 collective-permute-start.17
  62.3 0.8 collective-permute-start.18
  63.0 2.4 %collective-permute-done.16.hi_ref = f32[5,4,8,128]{3,2,1,0:T(8,128)S(1)} collective-permute-done((f32[5,4,8,128]{3,2,1,0:T(8,128)S(1)}, f32[5,4,8,128]{3,2,1,0:T(8,128)S(1)}, u32[]{:S(2)}, u32[]{:S(2)}) %collective-permute-start.16) | collective-permute-done | bytes 81952 | tf_op jit(solution)/shard_map/ppermute | solution.py:804
  65.4 1.7 %collective-permute-done.17.far_ref = f32[5,4,8,128]{3,2,1,0:T(8,128)S(1)} collective-permute-done((f32[5,4,8,128]{3,2,1,0:T(8,128)S(1)}, f32[5,4,8,128]{3,2,1,0:T(8,128)S(1)}, u32[]{:S(2)}, u32[]{:S(2)}) %collective-permute-start.17) | collective-permute-done | bytes 81952 | tf_op jit(solution)/shard_map/ppermute | solution.py:804
  67.1 2.0 %collective-permute-done.18.lo_ref = f32[5,4,8,128]{3,2,1,0:T(8,128)S(1)} collective-permute-done((f32[5,4,8,128]{3,2,1,0:T(8,128)S(1)}, f32[5,4,8,128]{3,2,1,0:T(8,128)S(1)}, u32[]{:S(2)}, u32[]{:S(2)}) %collective-permute-start.18) | collective-permute-done | bytes 81952 | tf_op jit(solution)/shard_map/ppermute | solution.py:804
  69.1 0.7 pack2.1
  69.9 3.1 %collective-permute-start.19 = (f32[8,32,128]{2,1,0:T(8,128)S(1)}, f32[8,32,128]{2,1,0:T(8,128)S(1)}, u32[]{:S(2)}, u32[]{:S(2)}) collective-permute-start(f32[8,32,128]{2,1,0:T(8,128)S(1)} %get-tuple-element.76), channel_id=1, source_target_pairs={{7,0},{0,1},{1,2},{2,3},{3,4},{4,5},{5,6},{6,7},{15,8},{8,9},{9,10... | collective-permute-start | bytes 393224 | tf_op jit(solution)/shard_map/ppermute | solution.py:804
  73.0 0.0 collective-permute-start.20
  73.0 3.5 %collective-permute-done.19.zlo_ref = f32[8,32,128]{2,1,0:T(8,128)S(1)} collective-permute-done((f32[8,32,128]{2,1,0:T(8,128)S(1)}, f32[8,32,128]{2,1,0:T(8,128)S(1)}, u32[]{:S(2)}, u32[]{:S(2)}) %collective-permute-start.19) | collective-permute-done | bytes 131104 | tf_op jit(solution)/shard_map/ppermute | solution.py:804
  76.4 3.7 %collective-permute-done.20.zhi_ref = f32[8,32,128]{2,1,0:T(8,128)S(1)} collective-permute-done((f32[8,32,128]{2,1,0:T(8,128)S(1)}, f32[8,32,128]{2,1,0:T(8,128)S(1)}, u32[]{:S(2)}, u32[]{:S(2)}) %collective-permute-start.20) | collective-permute-done | bytes 131104 | tf_op jit(solution)/shard_map/ppermute | solution.py:804
  80.1 2.6 %low_down.1 = (f32[16,32,128]{2,1,0:T(8,128)S(1)}, f32[16,32,128]{2,1,0:T(8,128)S(1)}, f32[16,32,128]{2,1,0:T(8,128)S(1)}, f32[16,32,128]{2,1,0:T(8,128)S(1)}, f...) custom-call(f32[5,4,32,128]{3,2,1,0:T(8,128)S(1)} %get-tuple-element.75.w_ref, ...), custom_call_target="tpu_custom_call" | custom-call | bytes 3000000 | tf_op jit(solution)/shard_map/low_down/pallas_call | solution.py:787
  82.8 17.1 %all_to_all.5.g_ref = f32[8,5,16,128]{3,2,1,0:T(8,128)S(1)} all-to-all(f32[8,5,16,128]{3,2,1,0:T(8,128)S(1)} %broadcast_in_dim.2), channel_id=1, replica_groups=mesh['gx'=4,'gy'=8,'gz'=8] {'gz'}, dimensions={0} | all-to-all | bytes 655360 | tf_op jit(solution)/shard_map/all_to_all | solution.py:870
  99.8 10.9 %up.1 = (f32[16,16,128]{2,1,0:T(8,128)}, f32[16,16,128]{2,1,0:T(8,128)}) custom-call(f32[8,5,16,128]{3,2,1,0:T(8,128)S(1)} %all_to_all.5.g_ref, f32[16,32,128]{2,1,0:T(8,128)S(1)} %get-tuple-element.79.refs_0_, f32[16,32,128]{2,1,0:T(8,128)S(1)} %get-tuple-element.80.refs_1_, f32[16,32,128]{2,1,0:T(8,128)S(1)} %get-tuple-element.81.refs_2_, ...), custom_call_target="tpu_custom_call" | custom-call | bytes 3000000 | tf_op jit(solution)/shard_map/up/pallas_call | solution.py:787
  (8 shorter events, 0.1 us)
Async XLA Ops:
  0.6 1.0 copy-start.1
  1.7 6.7 %copy-start = (f32[16,16,128]{2,1,0:T(8,128)S(1)}, f32[16,16,128]{2,1,0:T(8,128)}, u32[]{:S(2)}) copy-start(f32[16,16,128]{2,1,0:T(8,128)} %b_ref.3) | copy-start | bytes 393220
  1.7 6.7 %collective-permute-start = (f32[17,16,128]{2,1,0:T(8,128)S(1)}, f32[17,16,128]{2,1,0:T(8,128)S(1)}, u32[]{:S(2)}, u32[]{:S(2)}) collective-permute-start(f32[17,16,128]{2,1,0:T(8,128)S(1)} %get-tuple-element.99), channel_id=1, source_target_pairs={{192,0},{0,64},{64,128},{128,192},{193,1},{1,65},{65,129},{129,193... | collective-permute-start | bytes 417800 | tf_op jit(solution)/shard_map/ppermute | solution.py:804
  3.3 5.1 %collective-permute-start.1 = (f32[17,16,128]{2,1,0:T(8,128)S(1)}, f32[17,16,128]{2,1,0:T(8,128)S(1)}, u32[]{:S(2)}, u32[]{:S(2)}) collective-permute-start(f32[17,16,128]{2,1,0:T(8,128)S(1)} %get-tuple-element.98), channel_id=1, source_target_pairs={{64,0},{128,64},{192,128},{0,192},{65,1},{129,65},{193,129},{1,193... | collective-permute-start | bytes 417800 | tf_op jit(solution)/shard_map/ppermute | solution.py:804
  8.5 7.1 %collective-permute-start.2 = (f32[66,8,128]{2,1,0:T(8,128)S(1)}, f32[66,8,128]{2,1,0:T(8,128)S(1)}, u32[]{:S(2)}, u32[]{:S(2)}) collective-permute-start(f32[66,8,128]{2,1,0:T(8,128)S(1)} %get-tuple-element.50), channel_id=1, source_target_pairs={{56,0},{0,8},{8,16},{16,24},{24,32},{32,40},{40,48},{48,56},{57,1}... | collective-permute-start | bytes 811016 | tf_op jit(solution)/shard_map/ppermute | solution.py:804
  8.5 7.1 %collective-permute-start.3 = (f32[66,8,128]{2,1,0:T(8,128)S(1)}, f32[66,8,128]{2,1,0:T(8,128)S(1)}, u32[]{:S(2)}, u32[]{:S(2)}) collective-permute-start(f32[66,8,128]{2,1,0:T(8,128)S(1)} %get-tuple-element.51), channel_id=1, source_target_pairs={{8,0},{16,8},{24,16},{32,24},{40,32},{48,40},{56,48},{0,56},{9,1},... | collective-permute-start | bytes 811016 | tf_op jit(solution)/shard_map/ppermute | solution.py:804
  16.1 8.1 %collective-permute-start.4 = (f32[14,32,128]{2,1,0:T(8,128)S(1)}, f32[14,32,128]{2,1,0:T(8,128)S(1)}, u32[]{:S(2)}, u32[]{:S(2)}) collective-permute-start(f32[14,32,128]{2,1,0:T(8,128)S(1)} %get-tuple-element.53), channel_id=1, source_target_pairs={{7,0},{0,1},{1,2},{2,3},{3,4},{4,5},{5,6},{6,7},{15,8},{8,9},{9,10... | collective-permute-start | bytes 688136 | tf_op jit(solution)/shard_map/ppermute | solution.py:804
  18.1 7.9 %collective-permute-start.5 = (f32[14,32,128]{2,1,0:T(8,128)S(1)}, f32[14,32,128]{2,1,0:T(8,128)S(1)}, u32[]{:S(2)}, u32[]{:S(2)}) collective-permute-start(f32[14,32,128]{2,1,0:T(8,128)S(1)} %get-tuple-element.54), channel_id=1, source_target_pairs={{1,0},{2,1},{3,2},{4,3},{5,4},{6,5},{7,6},{0,7},{9,8},{10,9},{11,1... | collective-permute-start | bytes 688136 | tf_op jit(solution)/shard_map/ppermute | solution.py:804
  28.8 9.7 %collective-permute-start.6 = (f32[20,16,128]{2,1,0:T(8,128)S(1)}, f32[20,16,128]{2,1,0:T(8,128)S(1)}, u32[]{:S(2)}, u32[]{:S(2)}) collective-permute-start(f32[20,16,128]{2,1,0:T(8,128)S(1)} %get-tuple-element.63.x0.c0), channel_id=1, source_target_pairs={{64,0},{128,64},{192,128},{0,192},{65,1},{129,65},{193,129},{1,193... | collective-permute-start | bytes 491528 | tf_op jit(solution)/shard_map/ppermute | solution.py:804
  31.8 8.7 %collective-permute-start.7 = (f32[20,16,128]{2,1,0:T(8,128)S(1)}, f32[20,16,128]{2,1,0:T(8,128)S(1)}, u32[]{:S(2)}, u32[]{:S(2)}) collective-permute-start(f32[20,16,128]{2,1,0:T(8,128)S(1)} %get-tuple-element.63.x0.c0), channel_id=1, source_target_pairs={{128,0},{192,64},{0,128},{64,192},{129,1},{193,65},{1,129},{65,193... | collective-permute-start | bytes 491528 | tf_op jit(solution)/shard_map/ppermute | solution.py:804
  32.4 9.8 %collective-permute-start.8 = (f32[20,16,128]{2,1,0:T(8,128)S(1)}, f32[20,16,128]{2,1,0:T(8,128)S(1)}, u32[]{:S(2)}, u32[]{:S(2)}) collective-permute-start(f32[20,16,128]{2,1,0:T(8,128)S(1)} %get-tuple-element.63.x0.c0), channel_id=1, source_target_pairs={{192,0},{0,64},{64,128},{128,192},{193,1},{1,65},{65,129},{129,193... | collective-permute-start | bytes 491528 | tf_op jit(solution)/shard_map/ppermute | solution.py:804
  42.3 14.9 %collective-permute-start.10 = (f32[114,8,128]{2,1,0:T(8,128)S(1)}, f32[114,8,128]{2,1,0:T(8,128)S(1)}, u32[]{:S(2)}, u32[]{:S(2)}) collective-permute-start(f32[114,8,128]{2,1,0:T(8,128)S(1)} %get-tuple-element.68), channel_id=1, source_target_pairs={{8,0},{16,8},{24,16},{32,24},{40,32},{48,40},{56,48},{0,56},{9,1},... | collective-permute-start | bytes 1400840 | tf_op jit(solution)/shard_map/ppermute | solution.py:804
  44.6 12.6 %collective-permute-start.9 = (f32[114,8,128]{2,1,0:T(8,128)S(1)}, f32[114,8,128]{2,1,0:T(8,128)S(1)}, u32[]{:S(2)}, u32[]{:S(2)}) collective-permute-start(f32[114,8,128]{2,1,0:T(8,128)S(1)} %get-tuple-element.67), channel_id=1, source_target_pairs={{56,0},{0,8},{8,16},{16,24},{24,32},{32,40},{40,48},{48,56},{57,1}... | collective-permute-start | bytes 1400840 | tf_op jit(solution)/shard_map/ppermute | solution.py:804
  44.6 4.1 %collective-permute-start.11 = (f32[6,16,128]{2,1,0:T(8,128)S(1)}, f32[6,16,128]{2,1,0:T(8,128)S(1)}, u32[]{:S(2)}, u32[]{:S(2)}) collective-permute-start(f32[6,16,128]{2,1,0:T(8,128)S(1)} %get-tuple-element.69.x0.f0), channel_id=1, source_target_pairs={{64,0},{128,64},{192,128},{0,192},{65,1},{129,65},{193,129},{1,193... | collective-permute-start | bytes 147464 | tf_op jit(solution)/shard_map/ppermute | solution.py:804
  44.6 5.6 %collective-permute-start.12 = (f32[6,16,128]{2,1,0:T(8,128)S(1)}, f32[6,16,128]{2,1,0:T(8,128)S(1)}, u32[]{:S(2)}, u32[]{:S(2)}) collective-permute-start(f32[6,16,128]{2,1,0:T(8,128)S(1)} %get-tuple-element.69.x0.f0), channel_id=1, source_target_pairs={{128,0},{192,64},{0,128},{64,192},{129,1},{193,65},{1,129},{65,193... | collective-permute-start | bytes 147464 | tf_op jit(solution)/shard_map/ppermute | solution.py:804
  45.2 6.2 %collective-permute-start.13 = (f32[6,16,128]{2,1,0:T(8,128)S(1)}, f32[6,16,128]{2,1,0:T(8,128)S(1)}, u32[]{:S(2)}, u32[]{:S(2)}) collective-permute-start(f32[6,16,128]{2,1,0:T(8,128)S(1)} %get-tuple-element.69.x0.f0), channel_id=1, source_target_pairs={{192,0},{0,64},{64,128},{128,192},{193,1},{1,65},{65,129},{129,193... | collective-permute-start | bytes 147464 | tf_op jit(solution)/shard_map/ppermute | solution.py:804
  51.4 5.8 %collective-permute-start.14 = (f32[36,8,128]{2,1,0:T(8,128)S(1)}, f32[36,8,128]{2,1,0:T(8,128)S(1)}, u32[]{:S(2)}, u32[]{:S(2)}) collective-permute-start(f32[36,8,128]{2,1,0:T(8,128)S(1)} %get-tuple-element.70), channel_id=1, source_target_pairs={{56,0},{0,8},{8,16},{16,24},{24,32},{32,40},{40,48},{48,56},{57,1}... | collective-permute-start | bytes 442376 | tf_op jit(solution)/shard_map/ppermute | solution.py:804
  51.4 5.8 %collective-permute-start.15 = (f32[36,8,128]{2,1,0:T(8,128)S(1)}, f32[36,8,128]{2,1,0:T(8,128)S(1)}, u32[]{:S(2)}, u32[]{:S(2)}) collective-permute-start(f32[36,8,128]{2,1,0:T(8,128)S(1)} %get-tuple-element.71), channel_id=1, source_target_pairs={{8,0},{16,8},{24,16},{32,24},{40,32},{48,40},{56,48},{0,56},{9,1},... | collective-permute-start | bytes 442376 | tf_op jit(solution)/shard_map/ppermute | solution.py:804
  60.9 4.5 %collective-permute-start.16 = (f32[5,4,8,128]{3,2,1,0:T(8,128)S(1)}, f32[5,4,8,128]{3,2,1,0:T(8,128)S(1)}, u32[]{:S(2)}, u32[]{:S(2)}) collective-permute-start(f32[5,4,8,128]{3,2,1,0:T(8,128)S(1)} %get-tuple-element.73), channel_id=1, source_target_pairs={{16,0},{24,8},{32,16},{40,24},{48,32},{56,40},{0,48},{8,56},{17,1}... | collective-permute-start | bytes 245768 | tf_op jit(solution)/shard_map/ppermute | solution.py:804
  61.2 5.9 %collective-permute-start.17 = (f32[5,4,8,128]{3,2,1,0:T(8,128)S(1)}, f32[5,4,8,128]{3,2,1,0:T(8,128)S(1)}, u32[]{:S(2)}, u32[]{:S(2)}) collective-permute-start(f32[5,4,8,128]{3,2,1,0:T(8,128)S(1)} %get-tuple-element.73), channel_id=1, source_target_pairs={{32,0},{40,8},{48,16},{56,24},{0,32},{8,40},{16,48},{24,56},{33,1}... | collective-permute-start | bytes 245768 | tf_op jit(solution)/shard_map/ppermute | solution.py:804
  62.3 6.9 %collective-permute-start.18 = (f32[5,4,8,128]{3,2,1,0:T(8,128)S(1)}, f32[5,4,8,128]{3,2,1,0:T(8,128)S(1)}, u32[]{:S(2)}, u32[]{:S(2)}) collective-permute-start(f32[5,4,8,128]{3,2,1,0:T(8,128)S(1)} %get-tuple-element.74), channel_id=1, source_target_pairs={{48,0},{56,8},{0,16},{8,24},{16,32},{24,40},{32,48},{40,56},{49,1}... | collective-permute-start | bytes 245768 | tf_op jit(solution)/shard_map/ppermute | solution.py:804
  69.9 6.6 %collective-permute-start.19 = (f32[8,32,128]{2,1,0:T(8,128)S(1)}, f32[8,32,128]{2,1,0:T(8,128)S(1)}, u32[]{:S(2)}, u32[]{:S(2)}) collective-permute-start(f32[8,32,128]{2,1,0:T(8,128)S(1)} %get-tuple-element.76), channel_id=1, source_target_pairs={{7,0},{0,1},{1,2},{2,3},{3,4},{4,5},{5,6},{6,7},{15,8},{8,9},{9,10... | collective-permute-start | bytes 393224 | tf_op jit(solution)/shard_map/ppermute | solution.py:804
  73.0 7.2 %collective-permute-start.20 = (f32[8,32,128]{2,1,0:T(8,128)S(1)}, f32[8,32,128]{2,1,0:T(8,128)S(1)}, u32[]{:S(2)}, u32[]{:S(2)}) collective-permute-start(f32[8,32,128]{2,1,0:T(8,128)S(1)} %get-tuple-element.77), channel_id=1, source_target_pairs={{1,0},{2,1},{3,2},{4,3},{5,4},{6,5},{7,6},{0,7},{9,8},{10,9},{11,1... | collective-permute-start | bytes 393224 | tf_op jit(solution)/shard_map/ppermute | solution.py:804

commit v4 on v3

--- a/solution.py
+++ b/solution.py
@@ -158,29 +158,31 @@
             ref[64 + t] = acc
 
 
-def pack0(
-    f_ref, b_ref, xlo_ref, xhi_ref, ylo_ref, yhi_ref, up_ref, down_ref, fw_ref, bw_ref
-):
-    for p in range(32):
-        ref, q = f_plane(f_ref, xlo_ref, xhi_ref, p)
-        fw_ref[p, 0:16, :] = ref[q]
-        fw_ref[p, 16:24, :] = yhi_ref[p]
-        fw_ref[p, 24:32, :] = ylo_ref[p]
+def pack0b(b_ref, xlo_ref, xhi_ref, ylo_ref, yhi_ref, up_ref, down_ref, w_ref):
     for p in range(34):
         ref, q = b_plane(b_ref, xlo_ref, xhi_ref, p)
-        bw_ref[p, 0:16, :] = ref[q]
+        w_ref[p, 0:16, :] = ref[q]
         if 0 < p < 33:
-            bw_ref[p, 16:24, :] = yhi_ref[31 + p]
-            bw_ref[p, 24:32, :] = ylo_ref[31 + p]
+            w_ref[p, 16:24, :] = yhi_ref[31 + p]
+            w_ref[p, 24:32, :] = ylo_ref[31 + p]
         else:
-            bw_ref[p, 16:32, :] = ref[q]
-    ups, downs = z_pack(lambda p: (fw_ref[p], 0), 32, 32, (104, 0), 24, 5)
-    more = z_pack(lambda p: (bw_ref[p + 1], 0), 32, 32, (103, 0), 25, 5)
+            w_ref[p, 16:32, :] = ref[q]
+    ups, downs = z_pack(lambda p: (w_ref[p + 1], 0), 32, 32, (103, 0), 25, 5)
     for g in range(7):
         up_ref[g] = ups[g]
         down_ref[g] = downs[g]
-        up_ref[7 + g] = more[0][g]
-        down_ref[7 + g] = more[1][g]
+
+
+def pack0f(f_ref, xlo_ref, xhi_ref, ylo_ref, yhi_ref, up_ref, down_ref, w_ref):
+    for p in range(32):
+        ref, q = f_plane(f_ref, xlo_ref, xhi_ref, p)
+        w_ref[p, 0:16, :] = ref[q]
+        w_ref[p, 16:24, :] = yhi_ref[p]
+        w_ref[p, 24:32, :] = ylo_ref[p]
+    ups, downs = z_pack(lambda p: (w_ref[p], 0), 32, 32, (104, 0), 24, 5)
+    for g in range(7):
+        up_ref[g] = ups[g]
+        down_ref[g] = downs[g]
 
 
 def fine_matrices():
@@ -239,7 +241,7 @@
     row = iota((32, 256), 0)
     for i in range(34):
         q = min(max(i - 1, 0), 31)
-        g, at = 7 + q // 5, (q % 5) * 25
+        g, at = q // 5, (q % 5) * 25
         right = roll(zhi_ref[g], -at, 1)
         left = roll(zlo_ref[g], 103 - at, 1)
         bw[i, :, 0:128] = b_ref[i]
@@ -642,10 +644,10 @@
     g_ref, *refs,
 ):
     fars, refs = refs[:19], refs[19:]
-    (sol_ref, res_ref), refs = refs[:2], refs[2:]
+    (sol_far, res_far), refs = refs[:2], refs[2:]
     (l3, inv3, rhs3, u3, va3, vb3, upd3, scr3), refs = refs[:8], refs[8:]
     (va2, vb2, upd2, dup2, va1, vb1, upd1, dup1, va0, vb0, upd0, dup0), refs = refs[:12], refs[12:]
-    nears, sems = refs[:19], refs[19:]
+    nears, (sol_ref, res_ref), sems = refs[:19], refs[19:21], refs[21:]
     u2, cx2, cy2, cz2, inv2, rhs2 = nears[:6]
     u1, cx1, cy1, cz1, inv1, rhs1 = nears[6:12]
     u0, cx0, cy0, cz0, inv0, rhs0, diag0 = nears[12:]
@@ -769,12 +771,19 @@
     level = Level(cx0, cy0, cz0, inv0, rhs0, 0)
     post(level, va0, vb0, upd0, [(4, 28), (5, 27), (6, 26), (7, 25)], NEAR)
 
+    for i in range(16):
+        sol_ref[i] = va0[i + 8, 0:16, 0:128]
+    ends = copies_of((sol_ref, res_ref), (sol_far, res_far), sems[19:])
+    ends[0].start()
+
     def finish(i):
-        here, d = level.defect(va0, i)
-        sol_ref[i - 8] = here[0:16, 0:128]
+        _, d = level.defect(va0, i)
         res_ref[i - 8] = diag0[i - 8] * d[0:16, 0:128]
 
-    loop(8, 24, NEAR, finish)
+    loop(8, 24, 16, finish)
+    ends[1].start()
+    for m in ends:
+        m.wait()
 
 
 def mix_rows(ref, i):
@@ -811,21 +820,27 @@
     xs = [move(to_hi, "gx", -1), move(to_lo, "gx", 1)]
     to_hi, to_lo = call(packy0, [f, b] + xs, [(66, 8, 128)] * 2)
     ys = [move(to_hi, "gy", -1), move(to_lo, "gy", 1)]
-    to_hi, to_lo, fw, bw = call(
-        pack0, [f, b] + xs + ys, [(14, 32, 128)] * 2 + [(32, 32, 128), (34, 32, 128)]
-    )
-    zs = [move(to_hi, "gz", -1), move(to_lo, "gz", 1)]
+    to_hi, to_lo, bw = call(
+        pack0b, [b] + xs + ys, [(7, 32, 128)] * 2 + [(34, 32, 128)]
+    )
+    zb = [move(to_hi, "gz", -1), move(to_lo, "gz", 1)]
+    to_hi, to_lo, fw = call(
+        pack0f, [f] + xs + ys, [(7, 32, 128)] * 2 + [(32, 32, 128)]
+    )
+    zf = [move(to_hi, "gz", -1), move(to_lo, "gz", 1)]
     big = (32, 32, 256)
     cx0, cy0, cz0, inv0, d0, xpc = call(
         fine_coef,
-        [bw] + [e[64:].reshape(16, 128) for e in ys] + zs,
+        [bw] + [e[64:].reshape(16, 128) for e in ys] + zb,
         [big] * 5 + [(3 * TILES + 2, 16, 128)],
         [(34, 32, 256), big, big, (33, 32, 256), (4, 2, 256, 128)],
         24,
-    )
+        us=20,
+    )
+    xpc, zf = lax.optimization_barrier((xpc, zf))
     u0, cx0, cy0, cz0, inv0, rhs0, diag0, xpf = call(
         fine_down,
-        [fw] + zs + [cx0, cy0, cz0, inv0, d0],
+        [fw] + zf + [cx0, cy0, cz0, inv0, d0],
         [big] * 6 + [(16, 16, 128), (TILES, 16, 128)],
         [big] * 5 + [(1, 2, 256, 128)],
         24,
@@ -881,10 +896,11 @@
             [(16, 16, 128)] * 2,
             [(5,) + tiny] + [tiny] * 6 + [(5, 64, 128)]
             + [low] * 3 + [(256, 128)] + [mid] * 3 + [(512, 128)] + [big] * 3 + [(512, 128)]
-            + [low] * 6 + [mid] * 6 + [big] * 6 + [(16, 16, 128)],
+            + [low] * 6 + [mid] * 6 + [big] * 6 + [(16, 16, 128)] * 3,
             28,
             far_in=range(1, 20),
-            copies=19,
+            far_out=(0, 1),
+            copies=21,
         )
     )
 

time: 112 us -> 109 us (0.973)
  waiting for transfers between devices: 41 us -> 31.9 us
  starting transfers between devices: 25.1 us -> 32.7 us
    ppermute x21 -> x23, waiting for transfers between devices: 41 us -> 31.9 us  [move(): lax.ppermute(values, axis, [((i + shift) % size, i) for i in range(size)])]
    ppermute x21 -> x23, starting transfers between devices: 25.1 us -> 32.7 us  [move(): lax.ppermute(values, axis, [((i + shift) % size, i) for i in range(size)])]
    pallas_call x10 -> x11, Pallas kernels: 25.8 us -> 25.8 us  [call(): pl.pallas_call(body, out_shape=[jax.ShapeDtypeStruct(s, F32) for s in out...]
  transfers between devices with their start and end apart: 21 -> 23, of which waited for: 16 -> 14; matrix products, arithmetic and copies ran while one was open for 0% -> 0% of each run, Pallas kernels for 4% -> 7%
where the time goes in v4:
time: 109 us
  starting transfers between devices  32.7 us (30%)
  waiting for transfers between devices  31.9 us (29%)
  Pallas kernels  25.8 us (24%)
  blocking collectives  16.4 us (15%)
    ppermute x23, starting transfers between devices, move(): lax.ppermute(values, axis, [((i + shift) % size, i) for i in range(size)])  32.7 us
    ppermute x23, waiting for transfers between devices, move(): lax.ppermute(values, axis, [((i + shift) % size, i) for i in range(size)])  31.9 us
    pallas_call x11, Pallas kernels, call(): pl.pallas_call(body, out_shape=[jax.ShapeDtypeStruct(s, F32) for s in out...  25.8 us
    all_to_all x1, blocking collectives, local(): gathered = lax.all_to_all(everyone, 'gz', 0, 0)  16.4 us
  transfers between devices with their start and end apart: 23, of which 14 were waited for; matrix products, arithmetic and copies ran while one was open for 0% of the time, Pallas kernels for 7%

profile of v4, /device:TPU:32, one launch (start us, length us, event | category | flops | bytes accessed | tf_op | source)
XLA Modules:
  0.0 109.0 jit_solution(3197059818050395689)
XLA Ops:
  0.6 0.0 copy-start.1
  0.6 1.0 fusion.2
  1.6 0.0 copy-done.1
  1.7 0.0 copy-start
  1.7 1.6 %collective-permute-start = (f32[17,16,128]{2,1,0:T(8,128)S(1)}, f32[17,16,128]{2,1,0:T(8,128)S(1)}, u32[]{:S(2)}, u32[]{:S(2)}) collective-permute-start(f32[17,16,128]{2,1,0:T(8,128)S(1)} %get-tuple-element.109), channel_id=1, source_target_pairs={{192,0},{0,64},{64,128},{128,192},{193,1},{1,65},{65,129},{129,193... | collective-permute-start | bytes 417800 | tf_op jit(solution)/shard_map/ppermute | solution.py:813
  3.3 1.7 %collective-permute-start.1 = (f32[17,16,128]{2,1,0:T(8,128)S(1)}, f32[17,16,128]{2,1,0:T(8,128)S(1)}, u32[]{:S(2)}, u32[]{:S(2)}) collective-permute-start(f32[17,16,128]{2,1,0:T(8,128)S(1)} %get-tuple-element.108), channel_id=1, source_target_pairs={{64,0},{128,64},{192,128},{0,192},{65,1},{129,65},{193,129},{1,193... | collective-permute-start | bytes 417800 | tf_op jit(solution)/shard_map/ppermute | solution.py:813
  5.0 3.4 %collective-permute-done.lo_ref.xlo_ref = f32[17,16,128]{2,1,0:T(8,128)S(1)} collective-permute-done((f32[17,16,128]{2,1,0:T(8,128)S(1)}, f32[17,16,128]{2,1,0:T(8,128)S(1)}, u32[]{:S(2)}, u32[]{:S(2)}) %collective-permute-start) | collective-permute-done | bytes 139296 | tf_op jit(solution)/shard_map/ppermute | solution.py:813
  8.4 0.0 collective-permute-done.1.hi_ref.xhi_ref
  8.4 0.0 copy-done
  8.5 0.0 collective-permute-start.2
  8.5 2.9 %collective-permute-start.3 = (f32[66,8,128]{2,1,0:T(8,128)S(1)}, f32[66,8,128]{2,1,0:T(8,128)S(1)}, u32[]{:S(2)}, u32[]{:S(2)}) collective-permute-start(f32[66,8,128]{2,1,0:T(8,128)S(1)} %get-tuple-element.56), channel_id=1, source_target_pairs={{8,0},{16,8},{24,16},{32,24},{40,32},{48,40},{56,48},{0,56},{9,1},... | collective-permute-start | bytes 811016 | tf_op jit(solution)/shard_map/ppermute | solution.py:813
  11.4 4.1 %collective-permute-done.2.ylo_ref = f32[66,8,128]{2,1,0:T(8,128)S(1)} collective-permute-done((f32[66,8,128]{2,1,0:T(8,128)S(1)}, f32[66,8,128]{2,1,0:T(8,128)S(1)}, u32[]{:S(2)}, u32[]{:S(2)}) %collective-permute-start.2) | collective-permute-done | bytes 270368 | tf_op jit(solution)/shard_map/ppermute | solution.py:813
  15.6 0.0 collective-permute-done.3.yhi_ref
  15.6 0.3 pack0b.1
  15.9 2.0 %collective-permute-start.4 = (f32[7,32,128]{2,1,0:T(8,128)S(1)}, f32[7,32,128]{2,1,0:T(8,128)S(1)}, u32[]{:S(2)}, u32[]{:S(2)}) collective-permute-start(f32[7,32,128]{2,1,0:T(8,128)S(1)} %get-tuple-element.58), channel_id=1, source_target_pairs={{7,0},{0,1},{1,2},{2,3},{3,4},{4,5},{5,6},{6,7},{15,8},{8,9},{9,10... | collective-permute-start | bytes 344072 | tf_op jit(solution)/shard_map/ppermute | solution.py:813
  17.9 0.1 collective-permute-start.5
  18.0 0.3 pack0f.1
  18.3 2.0 %collective-permute-start.6 = (f32[7,32,128]{2,1,0:T(8,128)S(1)}, f32[7,32,128]{2,1,0:T(8,128)S(1)}, u32[]{:S(2)}, u32[]{:S(2)}) collective-permute-start(f32[7,32,128]{2,1,0:T(8,128)S(1)} %get-tuple-element.61), channel_id=1, source_target_pairs={{7,0},{0,1},{1,2},{2,3},{3,4},{4,5},{5,6},{6,7},{15,8},{8,9},{9,10... | collective-permute-start | bytes 344072 | tf_op jit(solution)/shard_map/ppermute | solution.py:813
  20.3 2.2 %collective-permute-start.7 = (f32[7,32,128]{2,1,0:T(8,128)S(1)}, f32[7,32,128]{2,1,0:T(8,128)S(1)}, u32[]{:S(2)}, u32[]{:S(2)}) collective-permute-start(f32[7,32,128]{2,1,0:T(8,128)S(1)} %get-tuple-element.62), channel_id=1, source_target_pairs={{1,0},{2,1},{3,2},{4,3},{5,4},{6,5},{7,6},{0,7},{9,8},{10,9},{11,1... | collective-permute-start | bytes 344072 | tf_op jit(solution)/shard_map/ppermute | solution.py:813
  22.5 0.0 collective-permute-done.4.zlo_ref
  22.5 0.8 collective-permute-done.5.zhi_ref
  23.3 2.8 %fine_coef.1 = (f32[32,32,256]{2,1,0:T(8,128)S(1)}, f32[32,32,256]{2,1,0:T(8,128)S(1)}, f32[32,32,256]{2,1,0:T(8,128)S(1)}, f32[32,32,256]{2,1,0:T(8,128)S(1)}, ...) custom-call(f32[34,32,128]{2,1,0:T(8,128)S(1)} %get-tuple-element.57.b_ref, ...), custom_call_target="tpu_custom_call" | custom-call | bytes 60000000 | tf_op jit(solution)/shard_map/fine_coef/pallas_call | solution.py:796
  26.1 0.0 collective-permute-done.6.zlo_ref
  26.1 0.5 collective-permute-done.7.zhi_ref
  26.6 1.5 %collective-permute-start.10 = (f32[20,16,128]{2,1,0:T(8,128)S(1)}, f32[20,16,128]{2,1,0:T(8,128)S(1)}, u32[]{:S(2)}, u32[]{:S(2)}) collective-permute-start(f32[20,16,128]{2,1,0:T(8,128)S(1)} %get-tuple-element.73.x0.c0), channel_id=1, source_target_pairs={{192,0},{0,64},{64,128},{128,192},{193,1},{1,65},{65,129},{129,193... | collective-permute-start | bytes 491528 | tf_op jit(solution)/shard_map/ppermute | solution.py:813
  28.1 1.7 %collective-permute-start.8 = (f32[20,16,128]{2,1,0:T(8,128)S(1)}, f32[20,16,128]{2,1,0:T(8,128)S(1)}, u32[]{:S(2)}, u32[]{:S(2)}) collective-permute-start(f32[20,16,128]{2,1,0:T(8,128)S(1)} %get-tuple-element.73.x0.c0), channel_id=1, source_target_pairs={{64,0},{128,64},{192,128},{0,192},{65,1},{129,65},{193,129},{1,193... | collective-permute-start | bytes 491528 | tf_op jit(solution)/shard_map/ppermute | solution.py:813
  29.8 1.5 %collective-permute-start.9 = (f32[20,16,128]{2,1,0:T(8,128)S(1)}, f32[20,16,128]{2,1,0:T(8,128)S(1)}, u32[]{:S(2)}, u32[]{:S(2)}) collective-permute-start(f32[20,16,128]{2,1,0:T(8,128)S(1)} %get-tuple-element.73.x0.c0), channel_id=1, source_target_pairs={{128,0},{192,64},{0,128},{64,192},{129,1},{193,65},{1,129},{65,193... | collective-permute-start | bytes 491528 | tf_op jit(solution)/shard_map/ppermute | solution.py:813
  31.3 4.3 %fine_down.1 = (f32[32,32,256]{2,1,0:T(8,128)S(1)}, f32[32,32,256]{2,1,0:T(8,128)S(1)}, f32[32,32,256]{2,1,0:T(8,128)S(1)}, f32[32,32,256]{2,1,0:T(8,128)S(1)}, ...) custom-call(f32[32,32,128]{2,1,0:T(8,128)S(1)} %get-tuple-element.64, ...), custom_call_target="tpu_custom_call" | custom-call | bytes 60000000 | tf_op jit(solution)/shard_map/fine_down/pallas_call | solution.py:796
  35.6 0.0 collective-permute-done.10.x3.c3
  35.7 0.0 collective-permute-done.8.x1.c1
  35.7 2.3 %collective-permute-done.9.x2.c2 = f32[20,16,128]{2,1,0:T(8,128)S(1)} collective-permute-done((f32[20,16,128]{2,1,0:T(8,128)S(1)}, f32[20,16,128]{2,1,0:T(8,128)S(1)}, u32[]{:S(2)}, u32[]{:S(2)}) %collective-permute-start.9) | collective-permute-done | bytes 163872 | tf_op jit(solution)/shard_map/ppermute | solution.py:813
  38.0 0.1 packy1.2
  38.0 0.0 collective-permute-start.11
  38.0 2.9 %collective-permute-start.12 = (f32[114,8,128]{2,1,0:T(8,128)S(1)}, f32[114,8,128]{2,1,0:T(8,128)S(1)}, u32[]{:S(2)}, u32[]{:S(2)}) collective-permute-start(f32[114,8,128]{2,1,0:T(8,128)S(1)} %get-tuple-element.78), channel_id=1, source_target_pairs={{8,0},{16,8},{24,16},{32,24},{40,32},{48,40},{56,48},{0,56},{9,1},... | collective-permute-start | bytes 1400840 | tf_op jit(solution)/shard_map/ppermute | solution.py:813
  41.0 1.8 %collective-permute-start.13 = (f32[6,16,128]{2,1,0:T(8,128)S(1)}, f32[6,16,128]{2,1,0:T(8,128)S(1)}, u32[]{:S(2)}, u32[]{:S(2)}) collective-permute-start(f32[6,16,128]{2,1,0:T(8,128)S(1)} %get-tuple-element.79.x0.f0), channel_id=1, source_target_pairs={{64,0},{128,64},{192,128},{0,192},{65,1},{129,65},{193,129},{1,193... | collective-permute-start | bytes 147464 | tf_op jit(solution)/shard_map/ppermute | solution.py:813
  42.8 1.4 %collective-permute-start.14 = (f32[6,16,128]{2,1,0:T(8,128)S(1)}, f32[6,16,128]{2,1,0:T(8,128)S(1)}, u32[]{:S(2)}, u32[]{:S(2)}) collective-permute-start(f32[6,16,128]{2,1,0:T(8,128)S(1)} %get-tuple-element.79.x0.f0), channel_id=1, source_target_pairs={{128,0},{192,64},{0,128},{64,192},{129,1},{193,65},{1,129},{65,193... | collective-permute-start | bytes 147464 | tf_op jit(solution)/shard_map/ppermute | solution.py:813
  44.2 0.0 collective-permute-start.15
  44.2 0.9 collective-permute-done.13.x1.f1
  45.1 3.3 %collective-permute-done.14.x2.f2 = f32[6,16,128]{2,1,0:T(8,128)S(1)} collective-permute-done((f32[6,16,128]{2,1,0:T(8,128)S(1)}, f32[6,16,128]{2,1,0:T(8,128)S(1)}, u32[]{:S(2)}, u32[]{:S(2)}) %collective-permute-start.14) | collective-permute-done | bytes 49184 | tf_op jit(solution)/shard_map/ppermute | solution.py:813
  48.4 1.1 collective-permute-done.15.x3.f3
  49.5 0.0 collective-permute-start.16
  49.5 2.9 %collective-permute-start.17 = (f32[36,8,128]{2,1,0:T(8,128)S(1)}, f32[36,8,128]{2,1,0:T(8,128)S(1)}, u32[]{:S(2)}, u32[]{:S(2)}) collective-permute-start(f32[36,8,128]{2,1,0:T(8,128)S(1)} %get-tuple-element.81), channel_id=1, source_target_pairs={{8,0},{16,8},{24,16},{32,24},{40,32},{48,40},{56,48},{0,56},{9,1},... | collective-permute-start | bytes 442376 | tf_op jit(solution)/shard_map/ppermute | solution.py:813
  52.5 2.8 %collective-permute-done.16.flo_ref = f32[36,8,128]{2,1,0:T(8,128)S(1)} collective-permute-done((f32[36,8,128]{2,1,0:T(8,128)S(1)}, f32[36,8,128]{2,1,0:T(8,128)S(1)}, u32[]{:S(2)}, u32[]{:S(2)}) %collective-permute-start.16) | collective-permute-done | bytes 147488 | tf_op jit(solution)/shard_map/ppermute | solution.py:813
  55.3 0.0 collective-permute-done.17.fhi_ref
  55.3 0.0 collective-permute-done.11.clo_ref
  55.3 0.0 collective-permute-done.12.chi_ref
  55.3 3.7 %mid_down.1 = (f32[32,32,128]{2,1,0:T(8,128)S(1)}, f32[32,32,128]{2,1,0:T(8,128)S(1)}, f32[32,32,128]{2,1,0:T(8,128)S(1)}, f32[32,32,128]{2,1,0:T(8,128)S(1)}, f...) custom-call(f32[20,16,128]{2,1,0:T(8,128)S(1)} %get-tuple-element.73, ...), custom_call_target="tpu_custom_call" | custom-call | bytes 3000000 | tf_op jit(solution)/shard_map/mid_down/pallas_call | solution.py:796
  59.0 0.7 collective-permute-start.18
  59.7 0.6 collective-permute-start.19
  60.3 1.1 %collective-permute-start.20 = (f32[5,4,8,128]{3,2,1,0:T(8,128)S(1)}, f32[5,4,8,128]{3,2,1,0:T(8,128)S(1)}, u32[]{:S(2)}, u32[]{:S(2)}) collective-permute-start(f32[5,4,8,128]{3,2,1,0:T(8,128)S(1)} %get-tuple-element.84), channel_id=1, source_target_pairs={{48,0},{56,8},{0,16},{8,24},{16,32},{24,40},{32,48},{40,56},{49,1}... | collective-permute-start | bytes 245768 | tf_op jit(solution)/shard_map/ppermute | solution.py:813
  61.4 2.1 %collective-permute-done.18.hi_ref = f32[5,4,8,128]{3,2,1,0:T(8,128)S(1)} collective-permute-done((f32[5,4,8,128]{3,2,1,0:T(8,128)S(1)}, f32[5,4,8,128]{3,2,1,0:T(8,128)S(1)}, u32[]{:S(2)}, u32[]{:S(2)}) %collective-permute-start.18) | collective-permute-done | bytes 81952 | tf_op jit(solution)/shard_map/ppermute | solution.py:813
  63.5 2.1 %collective-permute-done.19.far_ref = f32[5,4,8,128]{3,2,1,0:T(8,128)S(1)} collective-permute-done((f32[5,4,8,128]{3,2,1,0:T(8,128)S(1)}, f32[5,4,8,128]{3,2,1,0:T(8,128)S(1)}, u32[]{:S(2)}, u32[]{:S(2)}) %collective-permute-start.19) | collective-permute-done | bytes 81952 | tf_op jit(solution)/shard_map/ppermute | solution.py:813
  65.7 2.3 %collective-permute-done.20.lo_ref = f32[5,4,8,128]{3,2,1,0:T(8,128)S(1)} collective-permute-done((f32[5,4,8,128]{3,2,1,0:T(8,128)S(1)}, f32[5,4,8,128]{3,2,1,0:T(8,128)S(1)}, u32[]{:S(2)}, u32[]{:S(2)}) %collective-permute-start.20) | collective-permute-done | bytes 81952 | tf_op jit(solution)/shard_map/ppermute | solution.py:813
  67.9 0.7 pack2.1
  68.7 3.9 %collective-permute-start.21 = (f32[8,32,128]{2,1,0:T(8,128)S(1)}, f32[8,32,128]{2,1,0:T(8,128)S(1)}, u32[]{:S(2)}, u32[]{:S(2)}) collective-permute-start(f32[8,32,128]{2,1,0:T(8,128)S(1)} %get-tuple-element.86), channel_id=1, source_target_pairs={{7,0},{0,1},{1,2},{2,3},{3,4},{4,5},{5,6},{6,7},{15,8},{8,9},{9,10... | collective-permute-start | bytes 393224 | tf_op jit(solution)/shard_map/ppermute | solution.py:813
  72.5 0.0 collective-permute-start.22
  72.5 3.0 %collective-permute-done.21.zlo_ref = f32[8,32,128]{2,1,0:T(8,128)S(1)} collective-permute-done((f32[8,32,128]{2,1,0:T(8,128)S(1)}, f32[8,32,128]{2,1,0:T(8,128)S(1)}, u32[]{:S(2)}, u32[]{:S(2)}) %collective-permute-start.21) | collective-permute-done | bytes 131104 | tf_op jit(solution)/shard_map/ppermute | solution.py:813
  75.6 3.2 %collective-permute-done.22.zhi_ref = f32[8,32,128]{2,1,0:T(8,128)S(1)} collective-permute-done((f32[8,32,128]{2,1,0:T(8,128)S(1)}, f32[8,32,128]{2,1,0:T(8,128)S(1)}, u32[]{:S(2)}, u32[]{:S(2)}) %collective-permute-start.22) | collective-permute-done | bytes 131104 | tf_op jit(solution)/shard_map/ppermute | solution.py:813
  78.8 2.6 %low_down.1 = (f32[16,32,128]{2,1,0:T(8,128)S(1)}, f32[16,32,128]{2,1,0:T(8,128)S(1)}, f32[16,32,128]{2,1,0:T(8,128)S(1)}, f32[16,32,128]{2,1,0:T(8,128)S(1)}, f...) custom-call(f32[5,4,32,128]{3,2,1,0:T(8,128)S(1)} %get-tuple-element.85.w_ref, ...), custom_call_target="tpu_custom_call" | custom-call | bytes 3000000 | tf_op jit(solution)/shard_map/low_down/pallas_call | solution.py:796
  81.5 16.4 %all_to_all.5.g_ref = f32[8,5,16,128]{3,2,1,0:T(8,128)S(1)} all-to-all(f32[8,5,16,128]{3,2,1,0:T(8,128)S(1)} %broadcast_in_dim.2), channel_id=1, replica_groups=mesh['gx'=4,'gy'=8,'gz'=8] {'gz'}, dimensions={0} | all-to-all | bytes 655360 | tf_op jit(solution)/shard_map/all_to_all | solution.py:885
  97.8 10.9 %up.1 = (f32[16,16,128]{2,1,0:T(8,128)}, f32[16,16,128]{2,1,0:T(8,128)}) custom-call(f32[8,5,16,128]{3,2,1,0:T(8,128)S(1)} %all_to_all.5.g_ref, f32[16,32,128]{2,1,0:T(8,128)S(1)} %get-tuple-element.89.refs_0_, f32[16,32,128]{2,1,0:T(8,128)S(1)} %get-tuple-element.90.refs_1_, f32[16,32,128]{2,1,0:T(8,128)S(1)} %get-tuple-element.91.refs_2_, ...), custom_call_target="tpu_custom_call" | custom-call | bytes 3000000 | tf_op jit(solution)/shard_map/up/pallas_call | solution.py:796
  (8 shorter events, 0.1 us)
Async XLA Ops:
  0.6 1.0 copy-start.1
  1.7 6.7 %copy-start = (f32[16,16,128]{2,1,0:T(8,128)S(1)}, f32[16,16,128]{2,1,0:T(8,128)}, u32[]{:S(2)}) copy-start(f32[16,16,128]{2,1,0:T(8,128)} %b_ref.3) | copy-start | bytes 393220
  1.7 6.7 %collective-permute-start = (f32[17,16,128]{2,1,0:T(8,128)S(1)}, f32[17,16,128]{2,1,0:T(8,128)S(1)}, u32[]{:S(2)}, u32[]{:S(2)}) collective-permute-start(f32[17,16,128]{2,1,0:T(8,128)S(1)} %get-tuple-element.109), channel_id=1, source_target_pairs={{192,0},{0,64},{64,128},{128,192},{193,1},{1,65},{65,129},{129,193... | collective-permute-start | bytes 417800 | tf_op jit(solution)/shard_map/ppermute | solution.py:813
  3.3 5.1 %collective-permute-start.1 = (f32[17,16,128]{2,1,0:T(8,128)S(1)}, f32[17,16,128]{2,1,0:T(8,128)S(1)}, u32[]{:S(2)}, u32[]{:S(2)}) collective-permute-start(f32[17,16,128]{2,1,0:T(8,128)S(1)} %get-tuple-element.108), channel_id=1, source_target_pairs={{64,0},{128,64},{192,128},{0,192},{65,1},{129,65},{193,129},{1,193... | collective-permute-start | bytes 417800 | tf_op jit(solution)/shard_map/ppermute | solution.py:813
  8.5 7.1 %collective-permute-start.2 = (f32[66,8,128]{2,1,0:T(8,128)S(1)}, f32[66,8,128]{2,1,0:T(8,128)S(1)}, u32[]{:S(2)}, u32[]{:S(2)}) collective-permute-start(f32[66,8,128]{2,1,0:T(8,128)S(1)} %get-tuple-element.55), channel_id=1, source_target_pairs={{56,0},{0,8},{8,16},{16,24},{24,32},{32,40},{40,48},{48,56},{57,1}... | collective-permute-start | bytes 811016 | tf_op jit(solution)/shard_map/ppermute | solution.py:813
  8.5 7.1 %collective-permute-start.3 = (f32[66,8,128]{2,1,0:T(8,128)S(1)}, f32[66,8,128]{2,1,0:T(8,128)S(1)}, u32[]{:S(2)}, u32[]{:S(2)}) collective-permute-start(f32[66,8,128]{2,1,0:T(8,128)S(1)} %get-tuple-element.56), channel_id=1, source_target_pairs={{8,0},{16,8},{24,16},{32,24},{40,32},{48,40},{56,48},{0,56},{9,1},... | collective-permute-start | bytes 811016 | tf_op jit(solution)/shard_map/ppermute | solution.py:813
  15.9 6.6 %collective-permute-start.4 = (f32[7,32,128]{2,1,0:T(8,128)S(1)}, f32[7,32,128]{2,1,0:T(8,128)S(1)}, u32[]{:S(2)}, u32[]{:S(2)}) collective-permute-start(f32[7,32,128]{2,1,0:T(8,128)S(1)} %get-tuple-element.58), channel_id=1, source_target_pairs={{7,0},{0,1},{1,2},{2,3},{3,4},{4,5},{5,6},{6,7},{15,8},{8,9},{9,10... | collective-permute-start | bytes 344072 | tf_op jit(solution)/shard_map/ppermute | solution.py:813
  17.9 5.4 %collective-permute-start.5 = (f32[7,32,128]{2,1,0:T(8,128)S(1)}, f32[7,32,128]{2,1,0:T(8,128)S(1)}, u32[]{:S(2)}, u32[]{:S(2)}) collective-permute-start(f32[7,32,128]{2,1,0:T(8,128)S(1)} %get-tuple-element.59), channel_id=1, source_target_pairs={{1,0},{2,1},{3,2},{4,3},{5,4},{6,5},{7,6},{0,7},{9,8},{10,9},{11,1... | collective-permute-start | bytes 344072 | tf_op jit(solution)/shard_map/ppermute | solution.py:813
  18.3 7.8 %collective-permute-start.6 = (f32[7,32,128]{2,1,0:T(8,128)S(1)}, f32[7,32,128]{2,1,0:T(8,128)S(1)}, u32[]{:S(2)}, u32[]{:S(2)}) collective-permute-start(f32[7,32,128]{2,1,0:T(8,128)S(1)} %get-tuple-element.61), channel_id=1, source_target_pairs={{7,0},{0,1},{1,2},{2,3},{3,4},{4,5},{5,6},{6,7},{15,8},{8,9},{9,10... | collective-permute-start | bytes 344072 | tf_op jit(solution)/shard_map/ppermute | solution.py:813
  20.3 6.2 %collective-permute-start.7 = (f32[7,32,128]{2,1,0:T(8,128)S(1)}, f32[7,32,128]{2,1,0:T(8,128)S(1)}, u32[]{:S(2)}, u32[]{:S(2)}) collective-permute-start(f32[7,32,128]{2,1,0:T(8,128)S(1)} %get-tuple-element.62), channel_id=1, source_target_pairs={{1,0},{2,1},{3,2},{4,3},{5,4},{6,5},{7,6},{0,7},{9,8},{10,9},{11,1... | collective-permute-start | bytes 344072 | tf_op jit(solution)/shard_map/ppermute | solution.py:813
  26.6 9.1 %collective-permute-start.10 = (f32[20,16,128]{2,1,0:T(8,128)S(1)}, f32[20,16,128]{2,1,0:T(8,128)S(1)}, u32[]{:S(2)}, u32[]{:S(2)}) collective-permute-start(f32[20,16,128]{2,1,0:T(8,128)S(1)} %get-tuple-element.73.x0.c0), channel_id=1, source_target_pairs={{192,0},{0,64},{64,128},{128,192},{193,1},{1,65},{65,129},{129,193... | collective-permute-start | bytes 491528 | tf_op jit(solution)/shard_map/ppermute | solution.py:813
  28.1 7.6 %collective-permute-start.8 = (f32[20,16,128]{2,1,0:T(8,128)S(1)}, f32[20,16,128]{2,1,0:T(8,128)S(1)}, u32[]{:S(2)}, u32[]{:S(2)}) collective-permute-start(f32[20,16,128]{2,1,0:T(8,128)S(1)} %get-tuple-element.73.x0.c0), channel_id=1, source_target_pairs={{64,0},{128,64},{192,128},{0,192},{65,1},{129,65},{193,129},{1,193... | collective-permute-start | bytes 491528 | tf_op jit(solution)/shard_map/ppermute | solution.py:813
  29.8 8.1 %collective-permute-start.9 = (f32[20,16,128]{2,1,0:T(8,128)S(1)}, f32[20,16,128]{2,1,0:T(8,128)S(1)}, u32[]{:S(2)}, u32[]{:S(2)}) collective-permute-start(f32[20,16,128]{2,1,0:T(8,128)S(1)} %get-tuple-element.73.x0.c0), channel_id=1, source_target_pairs={{128,0},{192,64},{0,128},{64,192},{129,1},{193,65},{1,129},{65,193... | collective-permute-start | bytes 491528 | tf_op jit(solution)/shard_map/ppermute | solution.py:813
  38.0 17.3 %collective-permute-start.11 = (f32[114,8,128]{2,1,0:T(8,128)S(1)}, f32[114,8,128]{2,1,0:T(8,128)S(1)}, u32[]{:S(2)}, u32[]{:S(2)}) collective-permute-start(f32[114,8,128]{2,1,0:T(8,128)S(1)} %get-tuple-element.77), channel_id=1, source_target_pairs={{56,0},{0,8},{8,16},{16,24},{24,32},{32,40},{40,48},{48,56},{57,1}... | collective-permute-start | bytes 1400840 | tf_op jit(solution)/shard_map/ppermute | solution.py:813
  38.0 17.3 %collective-permute-start.12 = (f32[114,8,128]{2,1,0:T(8,128)S(1)}, f32[114,8,128]{2,1,0:T(8,128)S(1)}, u32[]{:S(2)}, u32[]{:S(2)}) collective-permute-start(f32[114,8,128]{2,1,0:T(8,128)S(1)} %get-tuple-element.78), channel_id=1, source_target_pairs={{8,0},{16,8},{24,16},{32,24},{40,32},{48,40},{56,48},{0,56},{9,1},... | collective-permute-start | bytes 1400840 | tf_op jit(solution)/shard_map/ppermute | solution.py:813
  41.0 4.1 %collective-permute-start.13 = (f32[6,16,128]{2,1,0:T(8,128)S(1)}, f32[6,16,128]{2,1,0:T(8,128)S(1)}, u32[]{:S(2)}, u32[]{:S(2)}) collective-permute-start(f32[6,16,128]{2,1,0:T(8,128)S(1)} %get-tuple-element.79.x0.f0), channel_id=1, source_target_pairs={{64,0},{128,64},{192,128},{0,192},{65,1},{129,65},{193,129},{1,193... | collective-permute-start | bytes 147464 | tf_op jit(solution)/shard_map/ppermute | solution.py:813
  42.8 5.6 %collective-permute-start.14 = (f32[6,16,128]{2,1,0:T(8,128)S(1)}, f32[6,16,128]{2,1,0:T(8,128)S(1)}, u32[]{:S(2)}, u32[]{:S(2)}) collective-permute-start(f32[6,16,128]{2,1,0:T(8,128)S(1)} %get-tuple-element.79.x0.f0), channel_id=1, source_target_pairs={{128,0},{192,64},{0,128},{64,192},{129,1},{193,65},{1,129},{65,193... | collective-permute-start | bytes 147464 | tf_op jit(solution)/shard_map/ppermute | solution.py:813
  44.2 5.3 %collective-permute-start.15 = (f32[6,16,128]{2,1,0:T(8,128)S(1)}, f32[6,16,128]{2,1,0:T(8,128)S(1)}, u32[]{:S(2)}, u32[]{:S(2)}) collective-permute-start(f32[6,16,128]{2,1,0:T(8,128)S(1)} %get-tuple-element.79.x0.f0), channel_id=1, source_target_pairs={{192,0},{0,64},{64,128},{128,192},{193,1},{1,65},{65,129},{129,193... | collective-permute-start | bytes 147464 | tf_op jit(solution)/shard_map/ppermute | solution.py:813
  49.5 5.8 %collective-permute-start.16 = (f32[36,8,128]{2,1,0:T(8,128)S(1)}, f32[36,8,128]{2,1,0:T(8,128)S(1)}, u32[]{:S(2)}, u32[]{:S(2)}) collective-permute-start(f32[36,8,128]{2,1,0:T(8,128)S(1)} %get-tuple-element.80), channel_id=1, source_target_pairs={{56,0},{0,8},{8,16},{16,24},{24,32},{32,40},{40,48},{48,56},{57,1}... | collective-permute-start | bytes 442376 | tf_op jit(solution)/shard_map/ppermute | solution.py:813
  49.5 5.8 %collective-permute-start.17 = (f32[36,8,128]{2,1,0:T(8,128)S(1)}, f32[36,8,128]{2,1,0:T(8,128)S(1)}, u32[]{:S(2)}, u32[]{:S(2)}) collective-permute-start(f32[36,8,128]{2,1,0:T(8,128)S(1)} %get-tuple-element.81), channel_id=1, source_target_pairs={{8,0},{16,8},{24,16},{32,24},{40,32},{48,40},{56,48},{0,56},{9,1},... | collective-permute-start | bytes 442376 | tf_op jit(solution)/shard_map/ppermute | solution.py:813
  59.0 4.5 %collective-permute-start.18 = (f32[5,4,8,128]{3,2,1,0:T(8,128)S(1)}, f32[5,4,8,128]{3,2,1,0:T(8,128)S(1)}, u32[]{:S(2)}, u32[]{:S(2)}) collective-permute-start(f32[5,4,8,128]{3,2,1,0:T(8,128)S(1)} %get-tuple-element.83), channel_id=1, source_target_pairs={{16,0},{24,8},{32,16},{40,24},{48,32},{56,40},{0,48},{8,56},{17,1}... | collective-permute-start | bytes 245768 | tf_op jit(solution)/shard_map/ppermute | solution.py:813
  59.7 6.0 %collective-permute-start.19 = (f32[5,4,8,128]{3,2,1,0:T(8,128)S(1)}, f32[5,4,8,128]{3,2,1,0:T(8,128)S(1)}, u32[]{:S(2)}, u32[]{:S(2)}) collective-permute-start(f32[5,4,8,128]{3,2,1,0:T(8,128)S(1)} %get-tuple-element.83), channel_id=1, source_target_pairs={{32,0},{40,8},{48,16},{56,24},{0,32},{8,40},{16,48},{24,56},{33,1}... | collective-permute-start | bytes 245768 | tf_op jit(solution)/shard_map/ppermute | solution.py:813
  60.3 7.6 %collective-permute-start.20 = (f32[5,4,8,128]{3,2,1,0:T(8,128)S(1)}, f32[5,4,8,128]{3,2,1,0:T(8,128)S(1)}, u32[]{:S(2)}, u32[]{:S(2)}) collective-permute-start(f32[5,4,8,128]{3,2,1,0:T(8,128)S(1)} %get-tuple-element.84), channel_id=1, source_target_pairs={{48,0},{56,8},{0,16},{8,24},{16,32},{24,40},{32,48},{40,56},{49,1}... | collective-permute-start | bytes 245768 | tf_op jit(solution)/shard_map/ppermute | solution.py:813
  68.7 6.9 %collective-permute-start.21 = (f32[8,32,128]{2,1,0:T(8,128)S(1)}, f32[8,32,128]{2,1,0:T(8,128)S(1)}, u32[]{:S(2)}, u32[]{:S(2)}) collective-permute-start(f32[8,32,128]{2,1,0:T(8,128)S(1)} %get-tuple-element.86), channel_id=1, source_target_pairs={{7,0},{0,1},{1,2},{2,3},{3,4},{4,5},{5,6},{6,7},{15,8},{8,9},{9,10... | collective-permute-start | bytes 393224 | tf_op jit(solution)/shard_map/ppermute | solution.py:813
  72.5 6.3 %collective-permute-start.22 = (f32[8,32,128]{2,1,0:T(8,128)S(1)}, f32[8,32,128]{2,1,0:T(8,128)S(1)}, u32[]{:S(2)}, u32[]{:S(2)}) collective-permute-start(f32[8,32,128]{2,1,0:T(8,128)S(1)} %get-tuple-element.87), channel_id=1, source_target_pairs={{1,0},{2,1},{3,2},{4,3},{5,4},{6,5},{7,6},{0,7},{9,8},{10,9},{11,1... | collective-permute-start | bytes 393224 | tf_op jit(solution)/shard_map/ppermute | solution.py:813

commit v5 on v4

--- a/solution.py
+++ b/solution.py
@@ -11,7 +11,7 @@
 F32 = jnp.float32
 CSWEEPS = 32
 MIB = 1024 * 1024
-NEAR, FULL = 12, 32
+NEAR, FULL = 16, 32
 
 
 def chebyshev_terms(sweep_count, lower_bound, upper_bound):
@@ -259,7 +259,7 @@
         outer = jnp.where((px == 3) & (i == 24), below, here)
         cxw[i] = harmonic(outer, inner)
 
-    loop(0, 33, 3, face_x)
+    loop(0, 33, 11, face_x)
 
     def coefficients(i):
         b = bw[i + 1]
@@ -287,7 +287,7 @@
         inv_ref[i] = 1.0 / d
         dw[i] = d
 
-    loop(0, 32, 4, coefficients)
+    loop(0, 32, 8, coefficients)
     for p in range(8):
         i = 8 + 2 * p
         put_lanes(scr, 0, p, 0.25 * cxw[i])
@@ -850,7 +850,8 @@
     )
 
     def along_x(xp):
-        return [xp] + [move(xp, "gx", k) for k in (1, 2, 3)]
+        got = {k: move(xp, "gx", k) for k in (1, 3, 2)}
+        return [xp, got[1], got[2], got[3]]
 
     def along_y(xs, tiles, us):
         to_hi, to_lo = call(packy1, xs, [(6 * tiles, 8, 128)] * 2, us=us)

time: 109 us -> 109 us (level)
  Pallas kernels: 25.8 us -> 24.7 us
  transfers between devices with their start and end apart: 23 -> 23, of which waited for: 14 -> 15; matrix products, arithmetic and copies ran while one was open for 0% -> 0% of each run, Pallas kernels for 7% -> 6%
where the time goes in v5:
time: 109 us
  starting transfers between devices  33 us (30%)
  waiting for transfers between devices  32.6 us (30%)
  Pallas kernels  24.7 us (23%)
  blocking collectives  16.5 us (15%)
    ppermute x23, starting transfers between devices, move(): lax.ppermute(values, axis, [((i + shift) % size, i) for i in range(size)])  33 us
    ppermute x23, waiting for transfers between devices, move(): lax.ppermute(values, axis, [((i + shift) % size, i) for i in range(size)])  32.6 us
    pallas_call x11, Pallas kernels, call(): pl.pallas_call(body, out_shape=[jax.ShapeDtypeStruct(s, F32) for s in out...  24.7 us
    all_to_all x1, blocking collectives, local(): gathered = lax.all_to_all(everyone, 'gz', 0, 0)  16.5 us
  transfers between devices with their start and end apart: 23, of which 15 were waited for; matrix products, arithmetic and copies ran while one was open for 0% of the time, Pallas kernels for 6%

profile of v5, /device:TPU:32, one launch (start us, length us, event | category | flops | bytes accessed | tf_op | source)
XLA Modules:
  0.0 108.9 jit_solution(13482044508933995209)
XLA Ops:
  0.6 0.0 copy-start.1
  0.6 1.0 fusion.2
  1.6 0.0 copy-done.1
  1.7 0.0 copy-start
  1.7 1.6 %collective-permute-start = (f32[17,16,128]{2,1,0:T(8,128)S(1)}, f32[17,16,128]{2,1,0:T(8,128)S(1)}, u32[]{:S(2)}, u32[]{:S(2)}) collective-permute-start(f32[17,16,128]{2,1,0:T(8,128)S(1)} %get-tuple-element.109), channel_id=1, source_target_pairs={{192,0},{0,64},{64,128},{128,192},{193,1},{1,65},{65,129},{129,193... | collective-permute-start | bytes 417800 | tf_op jit(solution)/shard_map/ppermute | solution.py:813
  3.3 1.7 %collective-permute-start.1 = (f32[17,16,128]{2,1,0:T(8,128)S(1)}, f32[17,16,128]{2,1,0:T(8,128)S(1)}, u32[]{:S(2)}, u32[]{:S(2)}) collective-permute-start(f32[17,16,128]{2,1,0:T(8,128)S(1)} %get-tuple-element.108), channel_id=1, source_target_pairs={{64,0},{128,64},{192,128},{0,192},{65,1},{129,65},{193,129},{1,193... | collective-permute-start | bytes 417800 | tf_op jit(solution)/shard_map/ppermute | solution.py:813
  5.0 3.4 %collective-permute-done.lo_ref.xlo_ref = f32[17,16,128]{2,1,0:T(8,128)S(1)} collective-permute-done((f32[17,16,128]{2,1,0:T(8,128)S(1)}, f32[17,16,128]{2,1,0:T(8,128)S(1)}, u32[]{:S(2)}, u32[]{:S(2)}) %collective-permute-start) | collective-permute-done | bytes 139296 | tf_op jit(solution)/shard_map/ppermute | solution.py:813
  8.4 0.0 collective-permute-done.1.hi_ref.xhi_ref
  8.4 0.0 copy-done
  8.5 0.0 collective-permute-start.2
  8.5 2.9 %collective-permute-start.3 = (f32[66,8,128]{2,1,0:T(8,128)S(1)}, f32[66,8,128]{2,1,0:T(8,128)S(1)}, u32[]{:S(2)}, u32[]{:S(2)}) collective-permute-start(f32[66,8,128]{2,1,0:T(8,128)S(1)} %get-tuple-element.56), channel_id=1, source_target_pairs={{8,0},{16,8},{24,16},{32,24},{40,32},{48,40},{56,48},{0,56},{9,1},... | collective-permute-start | bytes 811016 | tf_op jit(solution)/shard_map/ppermute | solution.py:813
  11.4 4.1 %collective-permute-done.2.ylo_ref = f32[66,8,128]{2,1,0:T(8,128)S(1)} collective-permute-done((f32[66,8,128]{2,1,0:T(8,128)S(1)}, f32[66,8,128]{2,1,0:T(8,128)S(1)}, u32[]{:S(2)}, u32[]{:S(2)}) %collective-permute-start.2) | collective-permute-done | bytes 270368 | tf_op jit(solution)/shard_map/ppermute | solution.py:813
  15.6 0.0 collective-permute-done.3.yhi_ref
  15.6 0.3 pack0b.1
  15.9 2.0 %collective-permute-start.4 = (f32[7,32,128]{2,1,0:T(8,128)S(1)}, f32[7,32,128]{2,1,0:T(8,128)S(1)}, u32[]{:S(2)}, u32[]{:S(2)}) collective-permute-start(f32[7,32,128]{2,1,0:T(8,128)S(1)} %get-tuple-element.58), channel_id=1, source_target_pairs={{7,0},{0,1},{1,2},{2,3},{3,4},{4,5},{5,6},{6,7},{15,8},{8,9},{9,10... | collective-permute-start | bytes 344072 | tf_op jit(solution)/shard_map/ppermute | solution.py:813
  17.9 0.1 collective-permute-start.5
  18.0 0.3 pack0f.1
  18.3 2.0 %collective-permute-start.6 = (f32[7,32,128]{2,1,0:T(8,128)S(1)}, f32[7,32,128]{2,1,0:T(8,128)S(1)}, u32[]{:S(2)}, u32[]{:S(2)}) collective-permute-start(f32[7,32,128]{2,1,0:T(8,128)S(1)} %get-tuple-element.61), channel_id=1, source_target_pairs={{7,0},{0,1},{1,2},{2,3},{3,4},{4,5},{5,6},{6,7},{15,8},{8,9},{9,10... | collective-permute-start | bytes 344072 | tf_op jit(solution)/shard_map/ppermute | solution.py:813
  20.3 2.2 %collective-permute-start.7 = (f32[7,32,128]{2,1,0:T(8,128)S(1)}, f32[7,32,128]{2,1,0:T(8,128)S(1)}, u32[]{:S(2)}, u32[]{:S(2)}) collective-permute-start(f32[7,32,128]{2,1,0:T(8,128)S(1)} %get-tuple-element.62), channel_id=1, source_target_pairs={{1,0},{2,1},{3,2},{4,3},{5,4},{6,5},{7,6},{0,7},{9,8},{10,9},{11,1... | collective-permute-start | bytes 344072 | tf_op jit(solution)/shard_map/ppermute | solution.py:813
  22.5 0.0 collective-permute-done.4.zlo_ref
  22.5 0.8 collective-permute-done.5.zhi_ref
  23.3 2.3 %fine_coef.1 = (f32[32,32,256]{2,1,0:T(8,128)S(1)}, f32[32,32,256]{2,1,0:T(8,128)S(1)}, f32[32,32,256]{2,1,0:T(8,128)S(1)}, f32[32,32,256]{2,1,0:T(8,128)S(1)}, ...) custom-call(f32[34,32,128]{2,1,0:T(8,128)S(1)} %get-tuple-element.57.b_ref, ...), custom_call_target="tpu_custom_call" | custom-call | bytes 60000000 | tf_op jit(solution)/shard_map/fine_coef/pallas_call | solution.py:796
  25.6 0.3 collective-permute-done.6.zlo_ref
  25.9 0.6 collective-permute-done.7.zhi_ref
  26.6 1.5 %collective-permute-start.10 = (f32[20,16,128]{2,1,0:T(8,128)S(1)}, f32[20,16,128]{2,1,0:T(8,128)S(1)}, u32[]{:S(2)}, u32[]{:S(2)}) collective-permute-start(f32[20,16,128]{2,1,0:T(8,128)S(1)} %get-tuple-element.73.x0.c0), channel_id=1, source_target_pairs={{192,0},{0,64},{64,128},{128,192},{193,1},{1,65},{65,129},{129,193... | collective-permute-start | bytes 491528 | tf_op jit(solution)/shard_map/ppermute | solution.py:813
  28.1 1.7 %collective-permute-start.8 = (f32[20,16,128]{2,1,0:T(8,128)S(1)}, f32[20,16,128]{2,1,0:T(8,128)S(1)}, u32[]{:S(2)}, u32[]{:S(2)}) collective-permute-start(f32[20,16,128]{2,1,0:T(8,128)S(1)} %get-tuple-element.73.x0.c0), channel_id=1, source_target_pairs={{64,0},{128,64},{192,128},{0,192},{65,1},{129,65},{193,129},{1,193... | collective-permute-start | bytes 491528 | tf_op jit(solution)/shard_map/ppermute | solution.py:813
  29.8 1.5 %collective-permute-start.9 = (f32[20,16,128]{2,1,0:T(8,128)S(1)}, f32[20,16,128]{2,1,0:T(8,128)S(1)}, u32[]{:S(2)}, u32[]{:S(2)}) collective-permute-start(f32[20,16,128]{2,1,0:T(8,128)S(1)} %get-tuple-element.73.x0.c0), channel_id=1, source_target_pairs={{128,0},{192,64},{0,128},{64,192},{129,1},{193,65},{1,129},{65,193... | collective-permute-start | bytes 491528 | tf_op jit(solution)/shard_map/ppermute | solution.py:813
  31.3 4.1 %fine_down.1 = (f32[32,32,256]{2,1,0:T(8,128)S(1)}, f32[32,32,256]{2,1,0:T(8,128)S(1)}, f32[32,32,256]{2,1,0:T(8,128)S(1)}, f32[32,32,256]{2,1,0:T(8,128)S(1)}, ...) custom-call(f32[32,32,128]{2,1,0:T(8,128)S(1)} %get-tuple-element.64, ...), custom_call_target="tpu_custom_call" | custom-call | bytes 60000000 | tf_op jit(solution)/shard_map/fine_down/pallas_call | solution.py:796
  35.4 0.0 collective-permute-done.10.x3.c3
  35.4 0.0 collective-permute-done.8.x1.c1
  35.4 2.5 %collective-permute-done.9.x2.c2 = f32[20,16,128]{2,1,0:T(8,128)S(1)} collective-permute-done((f32[20,16,128]{2,1,0:T(8,128)S(1)}, f32[20,16,128]{2,1,0:T(8,128)S(1)}, u32[]{:S(2)}, u32[]{:S(2)}) %collective-permute-start.9) | collective-permute-done | bytes 163872 | tf_op jit(solution)/shard_map/ppermute | solution.py:813
  38.0 0.1 packy1.2
  38.0 0.0 collective-permute-start.11
  38.0 2.9 %collective-permute-start.12 = (f32[114,8,128]{2,1,0:T(8,128)S(1)}, f32[114,8,128]{2,1,0:T(8,128)S(1)}, u32[]{:S(2)}, u32[]{:S(2)}) collective-permute-start(f32[114,8,128]{2,1,0:T(8,128)S(1)} %get-tuple-element.78), channel_id=1, source_target_pairs={{8,0},{16,8},{24,16},{32,24},{40,32},{48,40},{56,48},{0,56},{9,1},... | collective-permute-start | bytes 1400840 | tf_op jit(solution)/shard_map/ppermute | solution.py:813
  41.0 1.8 %collective-permute-start.13 = (f32[6,16,128]{2,1,0:T(8,128)S(1)}, f32[6,16,128]{2,1,0:T(8,128)S(1)}, u32[]{:S(2)}, u32[]{:S(2)}) collective-permute-start(f32[6,16,128]{2,1,0:T(8,128)S(1)} %get-tuple-element.79.x0.f0), channel_id=1, source_target_pairs={{64,0},{128,64},{192,128},{0,192},{65,1},{129,65},{193,129},{1,193... | collective-permute-start | bytes 147464 | tf_op jit(solution)/shard_map/ppermute | solution.py:813
  42.8 1.4 %collective-permute-start.14 = (f32[6,16,128]{2,1,0:T(8,128)S(1)}, f32[6,16,128]{2,1,0:T(8,128)S(1)}, u32[]{:S(2)}, u32[]{:S(2)}) collective-permute-start(f32[6,16,128]{2,1,0:T(8,128)S(1)} %get-tuple-element.79.x0.f0), channel_id=1, source_target_pairs={{128,0},{192,64},{0,128},{64,192},{129,1},{193,65},{1,129},{65,193... | collective-permute-start | bytes 147464 | tf_op jit(solution)/shard_map/ppermute | solution.py:813
  44.2 0.0 collective-permute-start.15
  44.2 0.9 collective-permute-done.13.x1.f1
  45.1 3.3 %collective-permute-done.14.x2.f2 = f32[6,16,128]{2,1,0:T(8,128)S(1)} collective-permute-done((f32[6,16,128]{2,1,0:T(8,128)S(1)}, f32[6,16,128]{2,1,0:T(8,128)S(1)}, u32[]{:S(2)}, u32[]{:S(2)}) %collective-permute-start.14) | collective-permute-done | bytes 49184 | tf_op jit(solution)/shard_map/ppermute | solution.py:813
  48.4 1.1 collective-permute-done.15.x3.f3
  49.5 0.0 collective-permute-start.16
  49.5 2.9 %collective-permute-start.17 = (f32[36,8,128]{2,1,0:T(8,128)S(1)}, f32[36,8,128]{2,1,0:T(8,128)S(1)}, u32[]{:S(2)}, u32[]{:S(2)}) collective-permute-start(f32[36,8,128]{2,1,0:T(8,128)S(1)} %get-tuple-element.81), channel_id=1, source_target_pairs={{8,0},{16,8},{24,16},{32,24},{40,32},{48,40},{56,48},{0,56},{9,1},... | collective-permute-start | bytes 442376 | tf_op jit(solution)/shard_map/ppermute | solution.py:813
  52.5 2.8 %collective-permute-done.16.flo_ref = f32[36,8,128]{2,1,0:T(8,128)S(1)} collective-permute-done((f32[36,8,128]{2,1,0:T(8,128)S(1)}, f32[36,8,128]{2,1,0:T(8,128)S(1)}, u32[]{:S(2)}, u32[]{:S(2)}) %collective-permute-start.16) | collective-permute-done | bytes 147488 | tf_op jit(solution)/shard_map/ppermute | solution.py:813
  55.3 0.0 collective-permute-done.17.fhi_ref
  55.3 0.0 collective-permute-done.11.clo_ref
  55.3 0.0 collective-permute-done.12.chi_ref
  55.3 3.7 %mid_down.1 = (f32[32,32,128]{2,1,0:T(8,128)S(1)}, f32[32,32,128]{2,1,0:T(8,128)S(1)}, f32[32,32,128]{2,1,0:T(8,128)S(1)}, f32[32,32,128]{2,1,0:T(8,128)S(1)}, f...) custom-call(f32[20,16,128]{2,1,0:T(8,128)S(1)} %get-tuple-element.73, ...), custom_call_target="tpu_custom_call" | custom-call | bytes 3000000 | tf_op jit(solution)/shard_map/mid_down/pallas_call | solution.py:796
  59.0 0.7 collective-permute-start.18
  59.7 0.6 collective-permute-start.19
  60.3 1.1 %collective-permute-start.20 = (f32[5,4,8,128]{3,2,1,0:T(8,128)S(1)}, f32[5,4,8,128]{3,2,1,0:T(8,128)S(1)}, u32[]{:S(2)}, u32[]{:S(2)}) collective-permute-start(f32[5,4,8,128]{3,2,1,0:T(8,128)S(1)} %get-tuple-element.84), channel_id=1, source_target_pairs={{48,0},{56,8},{0,16},{8,24},{16,32},{24,40},{32,48},{40,56},{49,1}... | collective-permute-start | bytes 245768 | tf_op jit(solution)/shard_map/ppermute | solution.py:813
  61.4 2.1 %collective-permute-done.18.hi_ref = f32[5,4,8,128]{3,2,1,0:T(8,128)S(1)} collective-permute-done((f32[5,4,8,128]{3,2,1,0:T(8,128)S(1)}, f32[5,4,8,128]{3,2,1,0:T(8,128)S(1)}, u32[]{:S(2)}, u32[]{:S(2)}) %collective-permute-start.18) | collective-permute-done | bytes 81952 | tf_op jit(solution)/shard_map/ppermute | solution.py:813
  63.5 2.1 %collective-permute-done.19.far_ref = f32[5,4,8,128]{3,2,1,0:T(8,128)S(1)} collective-permute-done((f32[5,4,8,128]{3,2,1,0:T(8,128)S(1)}, f32[5,4,8,128]{3,2,1,0:T(8,128)S(1)}, u32[]{:S(2)}, u32[]{:S(2)}) %collective-permute-start.19) | collective-permute-done | bytes 81952 | tf_op jit(solution)/shard_map/ppermute | solution.py:813
  65.7 2.3 %collective-permute-done.20.lo_ref = f32[5,4,8,128]{3,2,1,0:T(8,128)S(1)} collective-permute-done((f32[5,4,8,128]{3,2,1,0:T(8,128)S(1)}, f32[5,4,8,128]{3,2,1,0:T(8,128)S(1)}, u32[]{:S(2)}, u32[]{:S(2)}) %collective-permute-start.20) | collective-permute-done | bytes 81952 | tf_op jit(solution)/shard_map/ppermute | solution.py:813
  67.9 0.7 pack2.1
  68.7 4.1 %collective-permute-start.21 = (f32[8,32,128]{2,1,0:T(8,128)S(1)}, f32[8,32,128]{2,1,0:T(8,128)S(1)}, u32[]{:S(2)}, u32[]{:S(2)}) collective-permute-start(f32[8,32,128]{2,1,0:T(8,128)S(1)} %get-tuple-element.86), channel_id=1, source_target_pairs={{7,0},{0,1},{1,2},{2,3},{3,4},{4,5},{5,6},{6,7},{15,8},{8,9},{9,10... | collective-permute-start | bytes 393224 | tf_op jit(solution)/shard_map/ppermute | solution.py:813
  72.8 0.0 collective-permute-start.22
  72.8 3.0 %collective-permute-done.21.zlo_ref = f32[8,32,128]{2,1,0:T(8,128)S(1)} collective-permute-done((f32[8,32,128]{2,1,0:T(8,128)S(1)}, f32[8,32,128]{2,1,0:T(8,128)S(1)}, u32[]{:S(2)}, u32[]{:S(2)}) %collective-permute-start.21) | collective-permute-done | bytes 131104 | tf_op jit(solution)/shard_map/ppermute | solution.py:813
  75.8 3.2 %collective-permute-done.22.zhi_ref = f32[8,32,128]{2,1,0:T(8,128)S(1)} collective-permute-done((f32[8,32,128]{2,1,0:T(8,128)S(1)}, f32[8,32,128]{2,1,0:T(8,128)S(1)}, u32[]{:S(2)}, u32[]{:S(2)}) %collective-permute-start.22) | collective-permute-done | bytes 131104 | tf_op jit(solution)/shard_map/ppermute | solution.py:813
  79.0 2.6 %low_down.1 = (f32[16,32,128]{2,1,0:T(8,128)S(1)}, f32[16,32,128]{2,1,0:T(8,128)S(1)}, f32[16,32,128]{2,1,0:T(8,128)S(1)}, f32[16,32,128]{2,1,0:T(8,128)S(1)}, f...) custom-call(f32[5,4,32,128]{3,2,1,0:T(8,128)S(1)} %get-tuple-element.85.w_ref, ...), custom_call_target="tpu_custom_call" | custom-call | bytes 3000000 | tf_op jit(solution)/shard_map/low_down/pallas_call | solution.py:796
  81.6 16.5 %all_to_all.5.g_ref = f32[8,5,16,128]{3,2,1,0:T(8,128)S(1)} all-to-all(f32[8,5,16,128]{3,2,1,0:T(8,128)S(1)} %broadcast_in_dim.2), channel_id=1, replica_groups=mesh['gx'=4,'gy'=8,'gz'=8] {'gz'}, dimensions={0} | all-to-all | bytes 655360 | tf_op jit(solution)/shard_map/all_to_all | solution.py:886
  98.1 10.6 %up.1 = (f32[16,16,128]{2,1,0:T(8,128)}, f32[16,16,128]{2,1,0:T(8,128)}) custom-call(f32[8,5,16,128]{3,2,1,0:T(8,128)S(1)} %all_to_all.5.g_ref, f32[16,32,128]{2,1,0:T(8,128)S(1)} %get-tuple-element.89.refs_0_, f32[16,32,128]{2,1,0:T(8,128)S(1)} %get-tuple-element.90.refs_1_, f32[16,32,128]{2,1,0:T(8,128)S(1)} %get-tuple-element.91.refs_2_, ...), custom_call_target="tpu_custom_call" | custom-call | bytes 3000000 | tf_op jit(solution)/shard_map/up/pallas_call | solution.py:796
  (8 shorter events, 0.1 us)
Async XLA Ops:
  0.6 1.0 copy-start.1
  1.7 6.7 %copy-start = (f32[16,16,128]{2,1,0:T(8,128)S(1)}, f32[16,16,128]{2,1,0:T(8,128)}, u32[]{:S(2)}) copy-start(f32[16,16,128]{2,1,0:T(8,128)} %b_ref.3) | copy-start | bytes 393220
  1.7 6.7 %collective-permute-start = (f32[17,16,128]{2,1,0:T(8,128)S(1)}, f32[17,16,128]{2,1,0:T(8,128)S(1)}, u32[]{:S(2)}, u32[]{:S(2)}) collective-permute-start(f32[17,16,128]{2,1,0:T(8,128)S(1)} %get-tuple-element.109), channel_id=1, source_target_pairs={{192,0},{0,64},{64,128},{128,192},{193,1},{1,65},{65,129},{129,193... | collective-permute-start | bytes 417800 | tf_op jit(solution)/shard_map/ppermute | solution.py:813
  3.3 5.1 %collective-permute-start.1 = (f32[17,16,128]{2,1,0:T(8,128)S(1)}, f32[17,16,128]{2,1,0:T(8,128)S(1)}, u32[]{:S(2)}, u32[]{:S(2)}) collective-permute-start(f32[17,16,128]{2,1,0:T(8,128)S(1)} %get-tuple-element.108), channel_id=1, source_target_pairs={{64,0},{128,64},{192,128},{0,192},{65,1},{129,65},{193,129},{1,193... | collective-permute-start | bytes 417800 | tf_op jit(solution)/shard_map/ppermute | solution.py:813
  8.5 7.1 %collective-permute-start.2 = (f32[66,8,128]{2,1,0:T(8,128)S(1)}, f32[66,8,128]{2,1,0:T(8,128)S(1)}, u32[]{:S(2)}, u32[]{:S(2)}) collective-permute-start(f32[66,8,128]{2,1,0:T(8,128)S(1)} %get-tuple-element.55), channel_id=1, source_target_pairs={{56,0},{0,8},{8,16},{16,24},{24,32},{32,40},{40,48},{48,56},{57,1}... | collective-permute-start | bytes 811016 | tf_op jit(solution)/shard_map/ppermute | solution.py:813
  8.5 7.1 %collective-permute-start.3 = (f32[66,8,128]{2,1,0:T(8,128)S(1)}, f32[66,8,128]{2,1,0:T(8,128)S(1)}, u32[]{:S(2)}, u32[]{:S(2)}) collective-permute-start(f32[66,8,128]{2,1,0:T(8,128)S(1)} %get-tuple-element.56), channel_id=1, source_target_pairs={{8,0},{16,8},{24,16},{32,24},{40,32},{48,40},{56,48},{0,56},{9,1},... | collective-permute-start | bytes 811016 | tf_op jit(solution)/shard_map/ppermute | solution.py:813
  15.9 6.6 %collective-permute-start.4 = (f32[7,32,128]{2,1,0:T(8,128)S(1)}, f32[7,32,128]{2,1,0:T(8,128)S(1)}, u32[]{:S(2)}, u32[]{:S(2)}) collective-permute-start(f32[7,32,128]{2,1,0:T(8,128)S(1)} %get-tuple-element.58), channel_id=1, source_target_pairs={{7,0},{0,1},{1,2},{2,3},{3,4},{4,5},{5,6},{6,7},{15,8},{8,9},{9,10... | collective-permute-start | bytes 344072 | tf_op jit(solution)/shard_map/ppermute | solution.py:813
  17.9 5.4 %collective-permute-start.5 = (f32[7,32,128]{2,1,0:T(8,128)S(1)}, f32[7,32,128]{2,1,0:T(8,128)S(1)}, u32[]{:S(2)}, u32[]{:S(2)}) collective-permute-start(f32[7,32,128]{2,1,0:T(8,128)S(1)} %get-tuple-element.59), channel_id=1, source_target_pairs={{1,0},{2,1},{3,2},{4,3},{5,4},{6,5},{7,6},{0,7},{9,8},{10,9},{11,1... | collective-permute-start | bytes 344072 | tf_op jit(solution)/shard_map/ppermute | solution.py:813
  18.3 7.6 %collective-permute-start.6 = (f32[7,32,128]{2,1,0:T(8,128)S(1)}, f32[7,32,128]{2,1,0:T(8,128)S(1)}, u32[]{:S(2)}, u32[]{:S(2)}) collective-permute-start(f32[7,32,128]{2,1,0:T(8,128)S(1)} %get-tuple-element.61), channel_id=1, source_target_pairs={{7,0},{0,1},{1,2},{2,3},{3,4},{4,5},{5,6},{6,7},{15,8},{8,9},{9,10... | collective-permute-start | bytes 344072 | tf_op jit(solution)/shard_map/ppermute | solution.py:813
  20.3 6.2 %collective-permute-start.7 = (f32[7,32,128]{2,1,0:T(8,128)S(1)}, f32[7,32,128]{2,1,0:T(8,128)S(1)}, u32[]{:S(2)}, u32[]{:S(2)}) collective-permute-start(f32[7,32,128]{2,1,0:T(8,128)S(1)} %get-tuple-element.62), channel_id=1, source_target_pairs={{1,0},{2,1},{3,2},{4,3},{5,4},{6,5},{7,6},{0,7},{9,8},{10,9},{11,1... | collective-permute-start | bytes 344072 | tf_op jit(solution)/shard_map/ppermute | solution.py:813
  26.6 8.9 %collective-permute-start.10 = (f32[20,16,128]{2,1,0:T(8,128)S(1)}, f32[20,16,128]{2,1,0:T(8,128)S(1)}, u32[]{:S(2)}, u32[]{:S(2)}) collective-permute-start(f32[20,16,128]{2,1,0:T(8,128)S(1)} %get-tuple-element.73.x0.c0), channel_id=1, source_target_pairs={{192,0},{0,64},{64,128},{128,192},{193,1},{1,65},{65,129},{129,193... | collective-permute-start | bytes 491528 | tf_op jit(solution)/shard_map/ppermute | solution.py:813
  28.1 7.4 %collective-permute-start.8 = (f32[20,16,128]{2,1,0:T(8,128)S(1)}, f32[20,16,128]{2,1,0:T(8,128)S(1)}, u32[]{:S(2)}, u32[]{:S(2)}) collective-permute-start(f32[20,16,128]{2,1,0:T(8,128)S(1)} %get-tuple-element.73.x0.c0), channel_id=1, source_target_pairs={{64,0},{128,64},{192,128},{0,192},{65,1},{129,65},{193,129},{1,193... | collective-permute-start | bytes 491528 | tf_op jit(solution)/shard_map/ppermute | solution.py:813
  29.8 8.1 %collective-permute-start.9 = (f32[20,16,128]{2,1,0:T(8,128)S(1)}, f32[20,16,128]{2,1,0:T(8,128)S(1)}, u32[]{:S(2)}, u32[]{:S(2)}) collective-permute-start(f32[20,16,128]{2,1,0:T(8,128)S(1)} %get-tuple-element.73.x0.c0), channel_id=1, source_target_pairs={{128,0},{192,64},{0,128},{64,192},{129,1},{193,65},{1,129},{65,193... | collective-permute-start | bytes 491528 | tf_op jit(solution)/shard_map/ppermute | solution.py:813
  38.0 17.3 %collective-permute-start.11 = (f32[114,8,128]{2,1,0:T(8,128)S(1)}, f32[114,8,128]{2,1,0:T(8,128)S(1)}, u32[]{:S(2)}, u32[]{:S(2)}) collective-permute-start(f32[114,8,128]{2,1,0:T(8,128)S(1)} %get-tuple-element.77), channel_id=1, source_target_pairs={{56,0},{0,8},{8,16},{16,24},{24,32},{32,40},{40,48},{48,56},{57,1}... | collective-permute-start | bytes 1400840 | tf_op jit(solution)/shard_map/ppermute | solution.py:813
  38.0 17.3 %collective-permute-start.12 = (f32[114,8,128]{2,1,0:T(8,128)S(1)}, f32[114,8,128]{2,1,0:T(8,128)S(1)}, u32[]{:S(2)}, u32[]{:S(2)}) collective-permute-start(f32[114,8,128]{2,1,0:T(8,128)S(1)} %get-tuple-element.78), channel_id=1, source_target_pairs={{8,0},{16,8},{24,16},{32,24},{40,32},{48,40},{56,48},{0,56},{9,1},... | collective-permute-start | bytes 1400840 | tf_op jit(solution)/shard_map/ppermute | solution.py:813
  41.0 4.1 %collective-permute-start.13 = (f32[6,16,128]{2,1,0:T(8,128)S(1)}, f32[6,16,128]{2,1,0:T(8,128)S(1)}, u32[]{:S(2)}, u32[]{:S(2)}) collective-permute-start(f32[6,16,128]{2,1,0:T(8,128)S(1)} %get-tuple-element.79.x0.f0), channel_id=1, source_target_pairs={{64,0},{128,64},{192,128},{0,192},{65,1},{129,65},{193,129},{1,193... | collective-permute-start | bytes 147464 | tf_op jit(solution)/shard_map/ppermute | solution.py:813
  42.8 5.6 %collective-permute-start.14 = (f32[6,16,128]{2,1,0:T(8,128)S(1)}, f32[6,16,128]{2,1,0:T(8,128)S(1)}, u32[]{:S(2)}, u32[]{:S(2)}) collective-permute-start(f32[6,16,128]{2,1,0:T(8,128)S(1)} %get-tuple-element.79.x0.f0), channel_id=1, source_target_pairs={{128,0},{192,64},{0,128},{64,192},{129,1},{193,65},{1,129},{65,193... | collective-permute-start | bytes 147464 | tf_op jit(solution)/shard_map/ppermute | solution.py:813
  44.2 5.3 %collective-permute-start.15 = (f32[6,16,128]{2,1,0:T(8,128)S(1)}, f32[6,16,128]{2,1,0:T(8,128)S(1)}, u32[]{:S(2)}, u32[]{:S(2)}) collective-permute-start(f32[6,16,128]{2,1,0:T(8,128)S(1)} %get-tuple-element.79.x0.f0), channel_id=1, source_target_pairs={{192,0},{0,64},{64,128},{128,192},{193,1},{1,65},{65,129},{129,193... | collective-permute-start | bytes 147464 | tf_op jit(solution)/shard_map/ppermute | solution.py:813
  49.5 5.8 %collective-permute-start.16 = (f32[36,8,128]{2,1,0:T(8,128)S(1)}, f32[36,8,128]{2,1,0:T(8,128)S(1)}, u32[]{:S(2)}, u32[]{:S(2)}) collective-permute-start(f32[36,8,128]{2,1,0:T(8,128)S(1)} %get-tuple-element.80), channel_id=1, source_target_pairs={{56,0},{0,8},{8,16},{16,24},{24,32},{32,40},{40,48},{48,56},{57,1}... | collective-permute-start | bytes 442376 | tf_op jit(solution)/shard_map/ppermute | solution.py:813
  49.5 5.8 %collective-permute-start.17 = (f32[36,8,128]{2,1,0:T(8,128)S(1)}, f32[36,8,128]{2,1,0:T(8,128)S(1)}, u32[]{:S(2)}, u32[]{:S(2)}) collective-permute-start(f32[36,8,128]{2,1,0:T(8,128)S(1)} %get-tuple-element.81), channel_id=1, source_target_pairs={{8,0},{16,8},{24,16},{32,24},{40,32},{48,40},{56,48},{0,56},{9,1},... | collective-permute-start | bytes 442376 | tf_op jit(solution)/shard_map/ppermute | solution.py:813
  59.0 4.5 %collective-permute-start.18 = (f32[5,4,8,128]{3,2,1,0:T(8,128)S(1)}, f32[5,4,8,128]{3,2,1,0:T(8,128)S(1)}, u32[]{:S(2)}, u32[]{:S(2)}) collective-permute-start(f32[5,4,8,128]{3,2,1,0:T(8,128)S(1)} %get-tuple-element.83), channel_id=1, source_target_pairs={{16,0},{24,8},{32,16},{40,24},{48,32},{56,40},{0,48},{8,56},{17,1}... | collective-permute-start | bytes 245768 | tf_op jit(solution)/shard_map/ppermute | solution.py:813
  59.7 6.0 %collective-permute-start.19 = (f32[5,4,8,128]{3,2,1,0:T(8,128)S(1)}, f32[5,4,8,128]{3,2,1,0:T(8,128)S(1)}, u32[]{:S(2)}, u32[]{:S(2)}) collective-permute-start(f32[5,4,8,128]{3,2,1,0:T(8,128)S(1)} %get-tuple-element.83), channel_id=1, source_target_pairs={{32,0},{40,8},{48,16},{56,24},{0,32},{8,40},{16,48},{24,56},{33,1}... | collective-permute-start | bytes 245768 | tf_op jit(solution)/shard_map/ppermute | solution.py:813
  60.3 7.6 %collective-permute-start.20 = (f32[5,4,8,128]{3,2,1,0:T(8,128)S(1)}, f32[5,4,8,128]{3,2,1,0:T(8,128)S(1)}, u32[]{:S(2)}, u32[]{:S(2)}) collective-permute-start(f32[5,4,8,128]{3,2,1,0:T(8,128)S(1)} %get-tuple-element.84), channel_id=1, source_target_pairs={{48,0},{56,8},{0,16},{8,24},{16,32},{24,40},{32,48},{40,56},{49,1}... | collective-permute-start | bytes 245768 | tf_op jit(solution)/shard_map/ppermute | solution.py:813
  68.7 7.2 %collective-permute-start.21 = (f32[8,32,128]{2,1,0:T(8,128)S(1)}, f32[8,32,128]{2,1,0:T(8,128)S(1)}, u32[]{:S(2)}, u32[]{:S(2)}) collective-permute-start(f32[8,32,128]{2,1,0:T(8,128)S(1)} %get-tuple-element.86), channel_id=1, source_target_pairs={{7,0},{0,1},{1,2},{2,3},{3,4},{4,5},{5,6},{6,7},{15,8},{8,9},{9,10... | collective-permute-start | bytes 393224 | tf_op jit(solution)/shard_map/ppermute | solution.py:813
  72.8 6.2 %collective-permute-start.22 = (f32[8,32,128]{2,1,0:T(8,128)S(1)}, f32[8,32,128]{2,1,0:T(8,128)S(1)}, u32[]{:S(2)}, u32[]{:S(2)}) collective-permute-start(f32[8,32,128]{2,1,0:T(8,128)S(1)} %get-tuple-element.87), channel_id=1, source_target_pairs={{1,0},{2,1},{3,2},{4,3},{5,4},{6,5},{7,6},{0,7},{9,8},{10,9},{11,1... | collective-permute-start | bytes 393224 | tf_op jit(solution)/shard_map/ppermute | solution.py:813

commit v6 on v5

--- a/solution.py
+++ b/solution.py
@@ -476,7 +476,7 @@
         upd[i] = first
         va[i] = first
 
-    loop(0, 32, 8, coefficients)
+    loop(0, 32, 16, coefficients)
     for m in saves[:5]:
         m.start()
     level = Level(cx_ref, cy_ref, cz_ref, inv_ref, rhs_ref, 32)
@@ -575,7 +575,7 @@
         upd[i] = first
         va[i] = first
 
-    loop(0, 16, 8, coefficients)
+    loop(0, 16, 16, coefficients)
     for m in saves[:5]:
         m.start()
     level = Level(cx_ref, cy_ref, cz_ref, inv_ref, rhs_ref, 16)

time: 109 us -> 109 us (level)
  no operation moved by 1% of the time
where the time goes in v6:
time: 109 us
  starting transfers between devices  33 us (30%)
  waiting for transfers between devices  32.6 us (30%)
  Pallas kernels  24.6 us (23%)
  blocking collectives  16.5 us (15%)
    ppermute x23, starting transfers between devices, move(): lax.ppermute(values, axis, [((i + shift) % size, i) for i in range(size)])  33 us
    ppermute x23, waiting for transfers between devices, move(): lax.ppermute(values, axis, [((i + shift) % size, i) for i in range(size)])  32.6 us
    pallas_call x11, Pallas kernels, call(): pl.pallas_call(body, out_shape=[jax.ShapeDtypeStruct(s, F32) for s in out...  24.6 us
    all_to_all x1, blocking collectives, local(): gathered = lax.all_to_all(everyone, 'gz', 0, 0)  16.5 us
  transfers between devices with their start and end apart: 23, of which 15 were waited for; matrix products, arithmetic and copies ran while one was open for 0% of the time, Pallas kernels for 6%

profile of v6, /device:TPU:32, one launch (start us, length us, event | category | flops | bytes accessed | tf_op | source)
XLA Modules:
  0.0 108.7 jit_solution(9666701720378783614)
XLA Ops:
  0.6 0.0 copy-start.1
  0.6 1.0 fusion.2
  1.6 0.0 copy-done.1
  1.7 0.0 copy-start
  1.7 1.6 %collective-permute-start = (f32[17,16,128]{2,1,0:T(8,128)S(1)}, f32[17,16,128]{2,1,0:T(8,128)S(1)}, u32[]{:S(2)}, u32[]{:S(2)}) collective-permute-start(f32[17,16,128]{2,1,0:T(8,128)S(1)} %get-tuple-element.109), channel_id=1, source_target_pairs={{192,0},{0,64},{64,128},{128,192},{193,1},{1,65},{65,129},{129,193... | collective-permute-start | bytes 417800 | tf_op jit(solution)/shard_map/ppermute | solution.py:813
  3.3 1.7 %collective-permute-start.1 = (f32[17,16,128]{2,1,0:T(8,128)S(1)}, f32[17,16,128]{2,1,0:T(8,128)S(1)}, u32[]{:S(2)}, u32[]{:S(2)}) collective-permute-start(f32[17,16,128]{2,1,0:T(8,128)S(1)} %get-tuple-element.108), channel_id=1, source_target_pairs={{64,0},{128,64},{192,128},{0,192},{65,1},{129,65},{193,129},{1,193... | collective-permute-start | bytes 417800 | tf_op jit(solution)/shard_map/ppermute | solution.py:813
  5.0 3.4 %collective-permute-done.lo_ref.xlo_ref = f32[17,16,128]{2,1,0:T(8,128)S(1)} collective-permute-done((f32[17,16,128]{2,1,0:T(8,128)S(1)}, f32[17,16,128]{2,1,0:T(8,128)S(1)}, u32[]{:S(2)}, u32[]{:S(2)}) %collective-permute-start) | collective-permute-done | bytes 139296 | tf_op jit(solution)/shard_map/ppermute | solution.py:813
  8.4 0.0 collective-permute-done.1.hi_ref.xhi_ref
  8.4 0.0 copy-done
  8.5 0.0 collective-permute-start.2
  8.5 2.9 %collective-permute-start.3 = (f32[66,8,128]{2,1,0:T(8,128)S(1)}, f32[66,8,128]{2,1,0:T(8,128)S(1)}, u32[]{:S(2)}, u32[]{:S(2)}) collective-permute-start(f32[66,8,128]{2,1,0:T(8,128)S(1)} %get-tuple-element.56), channel_id=1, source_target_pairs={{8,0},{16,8},{24,16},{32,24},{40,32},{48,40},{56,48},{0,56},{9,1},... | collective-permute-start | bytes 811016 | tf_op jit(solution)/shard_map/ppermute | solution.py:813
  11.4 4.1 %collective-permute-done.2.ylo_ref = f32[66,8,128]{2,1,0:T(8,128)S(1)} collective-permute-done((f32[66,8,128]{2,1,0:T(8,128)S(1)}, f32[66,8,128]{2,1,0:T(8,128)S(1)}, u32[]{:S(2)}, u32[]{:S(2)}) %collective-permute-start.2) | collective-permute-done | bytes 270368 | tf_op jit(solution)/shard_map/ppermute | solution.py:813
  15.6 0.0 collective-permute-done.3.yhi_ref
  15.6 0.3 pack0b.1
  15.9 2.0 %collective-permute-start.4 = (f32[7,32,128]{2,1,0:T(8,128)S(1)}, f32[7,32,128]{2,1,0:T(8,128)S(1)}, u32[]{:S(2)}, u32[]{:S(2)}) collective-permute-start(f32[7,32,128]{2,1,0:T(8,128)S(1)} %get-tuple-element.58), channel_id=1, source_target_pairs={{7,0},{0,1},{1,2},{2,3},{3,4},{4,5},{5,6},{6,7},{15,8},{8,9},{9,10... | collective-permute-start | bytes 344072 | tf_op jit(solution)/shard_map/ppermute | solution.py:813
  17.9 0.1 collective-permute-start.5
  18.0 0.3 pack0f.1
  18.3 2.0 %collective-permute-start.6 = (f32[7,32,128]{2,1,0:T(8,128)S(1)}, f32[7,32,128]{2,1,0:T(8,128)S(1)}, u32[]{:S(2)}, u32[]{:S(2)}) collective-permute-start(f32[7,32,128]{2,1,0:T(8,128)S(1)} %get-tuple-element.61), channel_id=1, source_target_pairs={{7,0},{0,1},{1,2},{2,3},{3,4},{4,5},{5,6},{6,7},{15,8},{8,9},{9,10... | collective-permute-start | bytes 344072 | tf_op jit(solution)/shard_map/ppermute | solution.py:813
  20.3 2.2 %collective-permute-start.7 = (f32[7,32,128]{2,1,0:T(8,128)S(1)}, f32[7,32,128]{2,1,0:T(8,128)S(1)}, u32[]{:S(2)}, u32[]{:S(2)}) collective-permute-start(f32[7,32,128]{2,1,0:T(8,128)S(1)} %get-tuple-element.62), channel_id=1, source_target_pairs={{1,0},{2,1},{3,2},{4,3},{5,4},{6,5},{7,6},{0,7},{9,8},{10,9},{11,1... | collective-permute-start | bytes 344072 | tf_op jit(solution)/shard_map/ppermute | solution.py:813
  22.5 0.0 collective-permute-done.4.zlo_ref
  22.5 0.8 collective-permute-done.5.zhi_ref
  23.3 2.3 %fine_coef.1 = (f32[32,32,256]{2,1,0:T(8,128)S(1)}, f32[32,32,256]{2,1,0:T(8,128)S(1)}, f32[32,32,256]{2,1,0:T(8,128)S(1)}, f32[32,32,256]{2,1,0:T(8,128)S(1)}, ...) custom-call(f32[34,32,128]{2,1,0:T(8,128)S(1)} %get-tuple-element.57.b_ref, ...), custom_call_target="tpu_custom_call" | custom-call | bytes 60000000 | tf_op jit(solution)/shard_map/fine_coef/pallas_call | solution.py:796
  25.6 0.3 collective-permute-done.6.zlo_ref
  25.9 0.6 collective-permute-done.7.zhi_ref
  26.6 1.5 %collective-permute-start.10 = (f32[20,16,128]{2,1,0:T(8,128)S(1)}, f32[20,16,128]{2,1,0:T(8,128)S(1)}, u32[]{:S(2)}, u32[]{:S(2)}) collective-permute-start(f32[20,16,128]{2,1,0:T(8,128)S(1)} %get-tuple-element.73.x0.c0), channel_id=1, source_target_pairs={{192,0},{0,64},{64,128},{128,192},{193,1},{1,65},{65,129},{129,193... | collective-permute-start | bytes 491528 | tf_op jit(solution)/shard_map/ppermute | solution.py:813
  28.1 1.7 %collective-permute-start.8 = (f32[20,16,128]{2,1,0:T(8,128)S(1)}, f32[20,16,128]{2,1,0:T(8,128)S(1)}, u32[]{:S(2)}, u32[]{:S(2)}) collective-permute-start(f32[20,16,128]{2,1,0:T(8,128)S(1)} %get-tuple-element.73.x0.c0), channel_id=1, source_target_pairs={{64,0},{128,64},{192,128},{0,192},{65,1},{129,65},{193,129},{1,193... | collective-permute-start | bytes 491528 | tf_op jit(solution)/shard_map/ppermute | solution.py:813
  29.8 1.5 %collective-permute-start.9 = (f32[20,16,128]{2,1,0:T(8,128)S(1)}, f32[20,16,128]{2,1,0:T(8,128)S(1)}, u32[]{:S(2)}, u32[]{:S(2)}) collective-permute-start(f32[20,16,128]{2,1,0:T(8,128)S(1)} %get-tuple-element.73.x0.c0), channel_id=1, source_target_pairs={{128,0},{192,64},{0,128},{64,192},{129,1},{193,65},{1,129},{65,193... | collective-permute-start | bytes 491528 | tf_op jit(solution)/shard_map/ppermute | solution.py:813
  31.3 4.1 %fine_down.1 = (f32[32,32,256]{2,1,0:T(8,128)S(1)}, f32[32,32,256]{2,1,0:T(8,128)S(1)}, f32[32,32,256]{2,1,0:T(8,128)S(1)}, f32[32,32,256]{2,1,0:T(8,128)S(1)}, ...) custom-call(f32[32,32,128]{2,1,0:T(8,128)S(1)} %get-tuple-element.64, ...), custom_call_target="tpu_custom_call" | custom-call | bytes 60000000 | tf_op jit(solution)/shard_map/fine_down/pallas_call | solution.py:796
  35.4 0.0 collective-permute-done.10.x3.c3
  35.4 0.0 collective-permute-done.8.x1.c1
  35.4 2.5 %collective-permute-done.9.x2.c2 = f32[20,16,128]{2,1,0:T(8,128)S(1)} collective-permute-done((f32[20,16,128]{2,1,0:T(8,128)S(1)}, f32[20,16,128]{2,1,0:T(8,128)S(1)}, u32[]{:S(2)}, u32[]{:S(2)}) %collective-permute-start.9) | collective-permute-done | bytes 163872 | tf_op jit(solution)/shard_map/ppermute | solution.py:813
  38.0 0.1 packy1.2
  38.0 0.0 collective-permute-start.11
  38.0 2.9 %collective-permute-start.12 = (f32[114,8,128]{2,1,0:T(8,128)S(1)}, f32[114,8,128]{2,1,0:T(8,128)S(1)}, u32[]{:S(2)}, u32[]{:S(2)}) collective-permute-start(f32[114,8,128]{2,1,0:T(8,128)S(1)} %get-tuple-element.78), channel_id=1, source_target_pairs={{8,0},{16,8},{24,16},{32,24},{40,32},{48,40},{56,48},{0,56},{9,1},... | collective-permute-start | bytes 1400840 | tf_op jit(solution)/shard_map/ppermute | solution.py:813
  41.0 1.8 %collective-permute-start.13 = (f32[6,16,128]{2,1,0:T(8,128)S(1)}, f32[6,16,128]{2,1,0:T(8,128)S(1)}, u32[]{:S(2)}, u32[]{:S(2)}) collective-permute-start(f32[6,16,128]{2,1,0:T(8,128)S(1)} %get-tuple-element.79.x0.f0), channel_id=1, source_target_pairs={{64,0},{128,64},{192,128},{0,192},{65,1},{129,65},{193,129},{1,193... | collective-permute-start | bytes 147464 | tf_op jit(solution)/shard_map/ppermute | solution.py:813
  42.8 1.4 %collective-permute-start.14 = (f32[6,16,128]{2,1,0:T(8,128)S(1)}, f32[6,16,128]{2,1,0:T(8,128)S(1)}, u32[]{:S(2)}, u32[]{:S(2)}) collective-permute-start(f32[6,16,128]{2,1,0:T(8,128)S(1)} %get-tuple-element.79.x0.f0), channel_id=1, source_target_pairs={{128,0},{192,64},{0,128},{64,192},{129,1},{193,65},{1,129},{65,193... | collective-permute-start | bytes 147464 | tf_op jit(solution)/shard_map/ppermute | solution.py:813
  44.2 0.0 collective-permute-start.15
  44.2 0.9 collective-permute-done.13.x1.f1
  45.1 3.3 %collective-permute-done.14.x2.f2 = f32[6,16,128]{2,1,0:T(8,128)S(1)} collective-permute-done((f32[6,16,128]{2,1,0:T(8,128)S(1)}, f32[6,16,128]{2,1,0:T(8,128)S(1)}, u32[]{:S(2)}, u32[]{:S(2)}) %collective-permute-start.14) | collective-permute-done | bytes 49184 | tf_op jit(solution)/shard_map/ppermute | solution.py:813
  48.4 1.1 collective-permute-done.15.x3.f3
  49.5 0.0 collective-permute-start.16
  49.5 2.9 %collective-permute-start.17 = (f32[36,8,128]{2,1,0:T(8,128)S(1)}, f32[36,8,128]{2,1,0:T(8,128)S(1)}, u32[]{:S(2)}, u32[]{:S(2)}) collective-permute-start(f32[36,8,128]{2,1,0:T(8,128)S(1)} %get-tuple-element.81), channel_id=1, source_target_pairs={{8,0},{16,8},{24,16},{32,24},{40,32},{48,40},{56,48},{0,56},{9,1},... | collective-permute-start | bytes 442376 | tf_op jit(solution)/shard_map/ppermute | solution.py:813
  52.5 2.8 %collective-permute-done.16.flo_ref = f32[36,8,128]{2,1,0:T(8,128)S(1)} collective-permute-done((f32[36,8,128]{2,1,0:T(8,128)S(1)}, f32[36,8,128]{2,1,0:T(8,128)S(1)}, u32[]{:S(2)}, u32[]{:S(2)}) %collective-permute-start.16) | collective-permute-done | bytes 147488 | tf_op jit(solution)/shard_map/ppermute | solution.py:813
  55.3 0.0 collective-permute-done.17.fhi_ref
  55.3 0.0 collective-permute-done.11.clo_ref
  55.3 0.0 collective-permute-done.12.chi_ref
  55.3 3.6 %mid_down.1 = (f32[32,32,128]{2,1,0:T(8,128)S(1)}, f32[32,32,128]{2,1,0:T(8,128)S(1)}, f32[32,32,128]{2,1,0:T(8,128)S(1)}, f32[32,32,128]{2,1,0:T(8,128)S(1)}, f...) custom-call(f32[20,16,128]{2,1,0:T(8,128)S(1)} %get-tuple-element.73, ...), custom_call_target="tpu_custom_call" | custom-call | bytes 3000000 | tf_op jit(solution)/shard_map/mid_down/pallas_call | solution.py:796
  58.9 0.7 collective-permute-start.18
  59.6 0.6 collective-permute-start.19
  60.2 1.1 %collective-permute-start.20 = (f32[5,4,8,128]{3,2,1,0:T(8,128)S(1)}, f32[5,4,8,128]{3,2,1,0:T(8,128)S(1)}, u32[]{:S(2)}, u32[]{:S(2)}) collective-permute-start(f32[5,4,8,128]{3,2,1,0:T(8,128)S(1)} %get-tuple-element.84), channel_id=1, source_target_pairs={{48,0},{56,8},{0,16},{8,24},{16,32},{24,40},{32,48},{40,56},{49,1}... | collective-permute-start | bytes 245768 | tf_op jit(solution)/shard_map/ppermute | solution.py:813
  61.3 2.1 %collective-permute-done.18.hi_ref = f32[5,4,8,128]{3,2,1,0:T(8,128)S(1)} collective-permute-done((f32[5,4,8,128]{3,2,1,0:T(8,128)S(1)}, f32[5,4,8,128]{3,2,1,0:T(8,128)S(1)}, u32[]{:S(2)}, u32[]{:S(2)}) %collective-permute-start.18) | collective-permute-done | bytes 81952 | tf_op jit(solution)/shard_map/ppermute | solution.py:813
  63.4 2.1 %collective-permute-done.19.far_ref = f32[5,4,8,128]{3,2,1,0:T(8,128)S(1)} collective-permute-done((f32[5,4,8,128]{3,2,1,0:T(8,128)S(1)}, f32[5,4,8,128]{3,2,1,0:T(8,128)S(1)}, u32[]{:S(2)}, u32[]{:S(2)}) %collective-permute-start.19) | collective-permute-done | bytes 81952 | tf_op jit(solution)/shard_map/ppermute | solution.py:813
  65.6 2.3 %collective-permute-done.20.lo_ref = f32[5,4,8,128]{3,2,1,0:T(8,128)S(1)} collective-permute-done((f32[5,4,8,128]{3,2,1,0:T(8,128)S(1)}, f32[5,4,8,128]{3,2,1,0:T(8,128)S(1)}, u32[]{:S(2)}, u32[]{:S(2)}) %collective-permute-start.20) | collective-permute-done | bytes 81952 | tf_op jit(solution)/shard_map/ppermute | solution.py:813
  67.8 0.7 pack2.1
  68.6 4.1 %collective-permute-start.21 = (f32[8,32,128]{2,1,0:T(8,128)S(1)}, f32[8,32,128]{2,1,0:T(8,128)S(1)}, u32[]{:S(2)}, u32[]{:S(2)}) collective-permute-start(f32[8,32,128]{2,1,0:T(8,128)S(1)} %get-tuple-element.86), channel_id=1, source_target_pairs={{7,0},{0,1},{1,2},{2,3},{3,4},{4,5},{5,6},{6,7},{15,8},{8,9},{9,10... | collective-permute-start | bytes 393224 | tf_op jit(solution)/shard_map/ppermute | solution.py:813
  72.7 0.0 collective-permute-start.22
  72.7 3.0 %collective-permute-done.21.zlo_ref = f32[8,32,128]{2,1,0:T(8,128)S(1)} collective-permute-done((f32[8,32,128]{2,1,0:T(8,128)S(1)}, f32[8,32,128]{2,1,0:T(8,128)S(1)}, u32[]{:S(2)}, u32[]{:S(2)}) %collective-permute-start.21) | collective-permute-done | bytes 131104 | tf_op jit(solution)/shard_map/ppermute | solution.py:813
  75.7 3.2 %collective-permute-done.22.zhi_ref = f32[8,32,128]{2,1,0:T(8,128)S(1)} collective-permute-done((f32[8,32,128]{2,1,0:T(8,128)S(1)}, f32[8,32,128]{2,1,0:T(8,128)S(1)}, u32[]{:S(2)}, u32[]{:S(2)}) %collective-permute-start.22) | collective-permute-done | bytes 131104 | tf_op jit(solution)/shard_map/ppermute | solution.py:813
  78.9 2.5 %low_down.1 = (f32[16,32,128]{2,1,0:T(8,128)S(1)}, f32[16,32,128]{2,1,0:T(8,128)S(1)}, f32[16,32,128]{2,1,0:T(8,128)S(1)}, f32[16,32,128]{2,1,0:T(8,128)S(1)}, f...) custom-call(f32[5,4,32,128]{3,2,1,0:T(8,128)S(1)} %get-tuple-element.85.w_ref, ...), custom_call_target="tpu_custom_call" | custom-call | bytes 3000000 | tf_op jit(solution)/shard_map/low_down/pallas_call | solution.py:796
  81.5 16.5 %all_to_all.5.g_ref = f32[8,5,16,128]{3,2,1,0:T(8,128)S(1)} all-to-all(f32[8,5,16,128]{3,2,1,0:T(8,128)S(1)} %broadcast_in_dim.2), channel_id=1, replica_groups=mesh['gx'=4,'gy'=8,'gz'=8] {'gz'}, dimensions={0} | all-to-all | bytes 655360 | tf_op jit(solution)/shard_map/all_to_all | solution.py:886
  97.9 10.6 %up.1 = (f32[16,16,128]{2,1,0:T(8,128)}, f32[16,16,128]{2,1,0:T(8,128)}) custom-call(f32[8,5,16,128]{3,2,1,0:T(8,128)S(1)} %all_to_all.5.g_ref, f32[16,32,128]{2,1,0:T(8,128)S(1)} %get-tuple-element.89.refs_0_, f32[16,32,128]{2,1,0:T(8,128)S(1)} %get-tuple-element.90.refs_1_, f32[16,32,128]{2,1,0:T(8,128)S(1)} %get-tuple-element.91.refs_2_, ...), custom_call_target="tpu_custom_call" | custom-call | bytes 3000000 | tf_op jit(solution)/shard_map/up/pallas_call | solution.py:796
  (8 shorter events, 0.1 us)
Async XLA Ops:
  0.6 1.0 copy-start.1
  1.7 6.7 %copy-start = (f32[16,16,128]{2,1,0:T(8,128)S(1)}, f32[16,16,128]{2,1,0:T(8,128)}, u32[]{:S(2)}) copy-start(f32[16,16,128]{2,1,0:T(8,128)} %b_ref.3) | copy-start | bytes 393220
  1.7 6.7 %collective-permute-start = (f32[17,16,128]{2,1,0:T(8,128)S(1)}, f32[17,16,128]{2,1,0:T(8,128)S(1)}, u32[]{:S(2)}, u32[]{:S(2)}) collective-permute-start(f32[17,16,128]{2,1,0:T(8,128)S(1)} %get-tuple-element.109), channel_id=1, source_target_pairs={{192,0},{0,64},{64,128},{128,192},{193,1},{1,65},{65,129},{129,193... | collective-permute-start | bytes 417800 | tf_op jit(solution)/shard_map/ppermute | solution.py:813
  3.3 5.1 %collective-permute-start.1 = (f32[17,16,128]{2,1,0:T(8,128)S(1)}, f32[17,16,128]{2,1,0:T(8,128)S(1)}, u32[]{:S(2)}, u32[]{:S(2)}) collective-permute-start(f32[17,16,128]{2,1,0:T(8,128)S(1)} %get-tuple-element.108), channel_id=1, source_target_pairs={{64,0},{128,64},{192,128},{0,192},{65,1},{129,65},{193,129},{1,193... | collective-permute-start | bytes 417800 | tf_op jit(solution)/shard_map/ppermute | solution.py:813
  8.5 7.1 %collective-permute-start.2 = (f32[66,8,128]{2,1,0:T(8,128)S(1)}, f32[66,8,128]{2,1,0:T(8,128)S(1)}, u32[]{:S(2)}, u32[]{:S(2)}) collective-permute-start(f32[66,8,128]{2,1,0:T(8,128)S(1)} %get-tuple-element.55), channel_id=1, source_target_pairs={{56,0},{0,8},{8,16},{16,24},{24,32},{32,40},{40,48},{48,56},{57,1}... | collective-permute-start | bytes 811016 | tf_op jit(solution)/shard_map/ppermute | solution.py:813
  8.5 7.1 %collective-permute-start.3 = (f32[66,8,128]{2,1,0:T(8,128)S(1)}, f32[66,8,128]{2,1,0:T(8,128)S(1)}, u32[]{:S(2)}, u32[]{:S(2)}) collective-permute-start(f32[66,8,128]{2,1,0:T(8,128)S(1)} %get-tuple-element.56), channel_id=1, source_target_pairs={{8,0},{16,8},{24,16},{32,24},{40,32},{48,40},{56,48},{0,56},{9,1},... | collective-permute-start | bytes 811016 | tf_op jit(solution)/shard_map/ppermute | solution.py:813
  15.9 6.6 %collective-permute-start.4 = (f32[7,32,128]{2,1,0:T(8,128)S(1)}, f32[7,32,128]{2,1,0:T(8,128)S(1)}, u32[]{:S(2)}, u32[]{:S(2)}) collective-permute-start(f32[7,32,128]{2,1,0:T(8,128)S(1)} %get-tuple-element.58), channel_id=1, source_target_pairs={{7,0},{0,1},{1,2},{2,3},{3,4},{4,5},{5,6},{6,7},{15,8},{8,9},{9,10... | collective-permute-start | bytes 344072 | tf_op jit(solution)/shard_map/ppermute | solution.py:813
  17.9 5.4 %collective-permute-start.5 = (f32[7,32,128]{2,1,0:T(8,128)S(1)}, f32[7,32,128]{2,1,0:T(8,128)S(1)}, u32[]{:S(2)}, u32[]{:S(2)}) collective-permute-start(f32[7,32,128]{2,1,0:T(8,128)S(1)} %get-tuple-element.59), channel_id=1, source_target_pairs={{1,0},{2,1},{3,2},{4,3},{5,4},{6,5},{7,6},{0,7},{9,8},{10,9},{11,1... | collective-permute-start | bytes 344072 | tf_op jit(solution)/shard_map/ppermute | solution.py:813
  18.3 7.6 %collective-permute-start.6 = (f32[7,32,128]{2,1,0:T(8,128)S(1)}, f32[7,32,128]{2,1,0:T(8,128)S(1)}, u32[]{:S(2)}, u32[]{:S(2)}) collective-permute-start(f32[7,32,128]{2,1,0:T(8,128)S(1)} %get-tuple-element.61), channel_id=1, source_target_pairs={{7,0},{0,1},{1,2},{2,3},{3,4},{4,5},{5,6},{6,7},{15,8},{8,9},{9,10... | collective-permute-start | bytes 344072 | tf_op jit(solution)/shard_map/ppermute | solution.py:813
  20.3 6.2 %collective-permute-start.7 = (f32[7,32,128]{2,1,0:T(8,128)S(1)}, f32[7,32,128]{2,1,0:T(8,128)S(1)}, u32[]{:S(2)}, u32[]{:S(2)}) collective-permute-start(f32[7,32,128]{2,1,0:T(8,128)S(1)} %get-tuple-element.62), channel_id=1, source_target_pairs={{1,0},{2,1},{3,2},{4,3},{5,4},{6,5},{7,6},{0,7},{9,8},{10,9},{11,1... | collective-permute-start | bytes 344072 | tf_op jit(solution)/shard_map/ppermute | solution.py:813
  26.6 8.9 %collective-permute-start.10 = (f32[20,16,128]{2,1,0:T(8,128)S(1)}, f32[20,16,128]{2,1,0:T(8,128)S(1)}, u32[]{:S(2)}, u32[]{:S(2)}) collective-permute-start(f32[20,16,128]{2,1,0:T(8,128)S(1)} %get-tuple-element.73.x0.c0), channel_id=1, source_target_pairs={{192,0},{0,64},{64,128},{128,192},{193,1},{1,65},{65,129},{129,193... | collective-permute-start | bytes 491528 | tf_op jit(solution)/shard_map/ppermute | solution.py:813
  28.1 7.4 %collective-permute-start.8 = (f32[20,16,128]{2,1,0:T(8,128)S(1)}, f32[20,16,128]{2,1,0:T(8,128)S(1)}, u32[]{:S(2)}, u32[]{:S(2)}) collective-permute-start(f32[20,16,128]{2,1,0:T(8,128)S(1)} %get-tuple-element.73.x0.c0), channel_id=1, source_target_pairs={{64,0},{128,64},{192,128},{0,192},{65,1},{129,65},{193,129},{1,193... | collective-permute-start | bytes 491528 | tf_op jit(solution)/shard_map/ppermute | solution.py:813
  29.8 8.1 %collective-permute-start.9 = (f32[20,16,128]{2,1,0:T(8,128)S(1)}, f32[20,16,128]{2,1,0:T(8,128)S(1)}, u32[]{:S(2)}, u32[]{:S(2)}) collective-permute-start(f32[20,16,128]{2,1,0:T(8,128)S(1)} %get-tuple-element.73.x0.c0), channel_id=1, source_target_pairs={{128,0},{192,64},{0,128},{64,192},{129,1},{193,65},{1,129},{65,193... | collective-permute-start | bytes 491528 | tf_op jit(solution)/shard_map/ppermute | solution.py:813
  38.0 17.3 %collective-permute-start.11 = (f32[114,8,128]{2,1,0:T(8,128)S(1)}, f32[114,8,128]{2,1,0:T(8,128)S(1)}, u32[]{:S(2)}, u32[]{:S(2)}) collective-permute-start(f32[114,8,128]{2,1,0:T(8,128)S(1)} %get-tuple-element.77), channel_id=1, source_target_pairs={{56,0},{0,8},{8,16},{16,24},{24,32},{32,40},{40,48},{48,56},{57,1}... | collective-permute-start | bytes 1400840 | tf_op jit(solution)/shard_map/ppermute | solution.py:813
  38.0 17.3 %collective-permute-start.12 = (f32[114,8,128]{2,1,0:T(8,128)S(1)}, f32[114,8,128]{2,1,0:T(8,128)S(1)}, u32[]{:S(2)}, u32[]{:S(2)}) collective-permute-start(f32[114,8,128]{2,1,0:T(8,128)S(1)} %get-tuple-element.78), channel_id=1, source_target_pairs={{8,0},{16,8},{24,16},{32,24},{40,32},{48,40},{56,48},{0,56},{9,1},... | collective-permute-start | bytes 1400840 | tf_op jit(solution)/shard_map/ppermute | solution.py:813
  41.0 4.1 %collective-permute-start.13 = (f32[6,16,128]{2,1,0:T(8,128)S(1)}, f32[6,16,128]{2,1,0:T(8,128)S(1)}, u32[]{:S(2)}, u32[]{:S(2)}) collective-permute-start(f32[6,16,128]{2,1,0:T(8,128)S(1)} %get-tuple-element.79.x0.f0), channel_id=1, source_target_pairs={{64,0},{128,64},{192,128},{0,192},{65,1},{129,65},{193,129},{1,193... | collective-permute-start | bytes 147464 | tf_op jit(solution)/shard_map/ppermute | solution.py:813
  42.8 5.6 %collective-permute-start.14 = (f32[6,16,128]{2,1,0:T(8,128)S(1)}, f32[6,16,128]{2,1,0:T(8,128)S(1)}, u32[]{:S(2)}, u32[]{:S(2)}) collective-permute-start(f32[6,16,128]{2,1,0:T(8,128)S(1)} %get-tuple-element.79.x0.f0), channel_id=1, source_target_pairs={{128,0},{192,64},{0,128},{64,192},{129,1},{193,65},{1,129},{65,193... | collective-permute-start | bytes 147464 | tf_op jit(solution)/shard_map/ppermute | solution.py:813
  44.2 5.3 %collective-permute-start.15 = (f32[6,16,128]{2,1,0:T(8,128)S(1)}, f32[6,16,128]{2,1,0:T(8,128)S(1)}, u32[]{:S(2)}, u32[]{:S(2)}) collective-permute-start(f32[6,16,128]{2,1,0:T(8,128)S(1)} %get-tuple-element.79.x0.f0), channel_id=1, source_target_pairs={{192,0},{0,64},{64,128},{128,192},{193,1},{1,65},{65,129},{129,193... | collective-permute-start | bytes 147464 | tf_op jit(solution)/shard_map/ppermute | solution.py:813
  49.5 5.8 %collective-permute-start.16 = (f32[36,8,128]{2,1,0:T(8,128)S(1)}, f32[36,8,128]{2,1,0:T(8,128)S(1)}, u32[]{:S(2)}, u32[]{:S(2)}) collective-permute-start(f32[36,8,128]{2,1,0:T(8,128)S(1)} %get-tuple-element.80), channel_id=1, source_target_pairs={{56,0},{0,8},{8,16},{16,24},{24,32},{32,40},{40,48},{48,56},{57,1}... | collective-permute-start | bytes 442376 | tf_op jit(solution)/shard_map/ppermute | solution.py:813
  49.5 5.8 %collective-permute-start.17 = (f32[36,8,128]{2,1,0:T(8,128)S(1)}, f32[36,8,128]{2,1,0:T(8,128)S(1)}, u32[]{:S(2)}, u32[]{:S(2)}) collective-permute-start(f32[36,8,128]{2,1,0:T(8,128)S(1)} %get-tuple-element.81), channel_id=1, source_target_pairs={{8,0},{16,8},{24,16},{32,24},{40,32},{48,40},{56,48},{0,56},{9,1},... | collective-permute-start | bytes 442376 | tf_op jit(solution)/shard_map/ppermute | solution.py:813
  58.9 4.5 %collective-permute-start.18 = (f32[5,4,8,128]{3,2,1,0:T(8,128)S(1)}, f32[5,4,8,128]{3,2,1,0:T(8,128)S(1)}, u32[]{:S(2)}, u32[]{:S(2)}) collective-permute-start(f32[5,4,8,128]{3,2,1,0:T(8,128)S(1)} %get-tuple-element.83), channel_id=1, source_target_pairs={{16,0},{24,8},{32,16},{40,24},{48,32},{56,40},{0,48},{8,56},{17,1}... | collective-permute-start | bytes 245768 | tf_op jit(solution)/shard_map/ppermute | solution.py:813
  59.6 6.0 %collective-permute-start.19 = (f32[5,4,8,128]{3,2,1,0:T(8,128)S(1)}, f32[5,4,8,128]{3,2,1,0:T(8,128)S(1)}, u32[]{:S(2)}, u32[]{:S(2)}) collective-permute-start(f32[5,4,8,128]{3,2,1,0:T(8,128)S(1)} %get-tuple-element.83), channel_id=1, source_target_pairs={{32,0},{40,8},{48,16},{56,24},{0,32},{8,40},{16,48},{24,56},{33,1}... | collective-permute-start | bytes 245768 | tf_op jit(solution)/shard_map/ppermute | solution.py:813
  60.2 7.6 %collective-permute-start.20 = (f32[5,4,8,128]{3,2,1,0:T(8,128)S(1)}, f32[5,4,8,128]{3,2,1,0:T(8,128)S(1)}, u32[]{:S(2)}, u32[]{:S(2)}) collective-permute-start(f32[5,4,8,128]{3,2,1,0:T(8,128)S(1)} %get-tuple-element.84), channel_id=1, source_target_pairs={{48,0},{56,8},{0,16},{8,24},{16,32},{24,40},{32,48},{40,56},{49,1}... | collective-permute-start | bytes 245768 | tf_op jit(solution)/shard_map/ppermute | solution.py:813
  68.6 7.2 %collective-permute-start.21 = (f32[8,32,128]{2,1,0:T(8,128)S(1)}, f32[8,32,128]{2,1,0:T(8,128)S(1)}, u32[]{:S(2)}, u32[]{:S(2)}) collective-permute-start(f32[8,32,128]{2,1,0:T(8,128)S(1)} %get-tuple-element.86), channel_id=1, source_target_pairs={{7,0},{0,1},{1,2},{2,3},{3,4},{4,5},{5,6},{6,7},{15,8},{8,9},{9,10... | collective-permute-start | bytes 393224 | tf_op jit(solution)/shard_map/ppermute | solution.py:813
  72.7 6.2 %collective-permute-start.22 = (f32[8,32,128]{2,1,0:T(8,128)S(1)}, f32[8,32,128]{2,1,0:T(8,128)S(1)}, u32[]{:S(2)}, u32[]{:S(2)}) collective-permute-start(f32[8,32,128]{2,1,0:T(8,128)S(1)} %get-tuple-element.87), channel_id=1, source_target_pairs={{1,0},{2,1},{3,2},{4,3},{5,4},{6,5},{7,6},{0,7},{9,8},{10,9},{11,1... | collective-permute-start | bytes 393224 | tf_op jit(solution)/shard_map/ppermute | solution.py:813
